TPU v7x, 512 devices: a whole 4x4x16 slice. The times are simulated.
512 devices in a mesh: row: 64 (over z, x), col: 8 (over y, core).
Axes of the slice: x: 4, y: 4, z: 16, core: 2. Of those that a mesh axis runs over, the one named last changes fastest.
Arguments:
- pattern: int32 [256, 16], replicated, may hold values from -1 to 255, as said below
- matrix: bfloat16 [256, 16, 128, 128], P('row', 'col'), as said below
- atom_set: int32 [4096], P('row'), may hold values from 0 to 4095, as said below
- atom_slab: int32 [4096], P('row'), may hold values from 0 to 63, as said below
- atom_offset: float32 [3, 4096], P(None, 'row'), as said below
Outputs:
- purified: float32 [256, 16, 128, 128], P('row', 'col')
- density: float32 [256, 640, 640], P('row', 'col')
Inputs may be any that keep to these rules, and one draw needn't show every extreme that they name: `pattern`: entry [I, s] is -1 or a block column. The slots c * 2 to c * 2 + 1 belong to col index c and hold distinct block columns J with J mod (the number of col indices) = c. Every block row I holds its own column I. The block rows of one row index name, among the block rows of any other row index, at most one block row. `matrix`: blocks at empty slots are zero. The diagonal entries of a block at block column I of block row I lie in [0.02, 0.99]. `atom_set`: the atoms of one row index name, each once, the atom sets of that row index's block rows; atom set I * 16 + g holds orbitals g * 8 to g * 8 + 7 of block row I. `atom_slab`: an atom of row index r sits in slab r - 1, r or r + 1, taken cyclically. `atom_offset`: the first coordinate lies in [0, 4), the second in [0, 640), the third in [0, 640).
All inputs are finite; a program needn't handle non-finite values.
Results may differ from a plain program's by a relative error of at most 0.0003.
Values may be sent and summed in bfloat16 or wider, within the bound.
No kernel may reach another device: no remote copies, remote signals or barrier semaphores. Data moves between devices by JAX's collectives and lax.ppermute only.
A program may use at most 64 MiB of HBM per device.

v0:
```python
import jax
import jax.numpy as jnp
from jax import lax
from jax.sharding import PartitionSpec as P

ORB = 8
PLANES = 4
YC = 80
GZ = 640


sharpness = 64.0
half_fill = 0.5


def from_behind(value, axis, steps):
    count = lax.axis_size(axis)
    pairs = [(source, (source + steps) % count) for source in range(count)]
    return lax.ppermute(value, axis, pairs)


def window(delta, length):
    folded = jnp.mod(delta + 0.5 * length, length) - 0.5 * length
    inside = jnp.maximum(1.0 - folded / PLANES * (folded / PLANES), 0.0)
    return inside * inside


def collocate(near, x_cells, y_cells, z_cells, length_x, length_y, length_z):
    along_x = window(x_cells[None, :] - near[1][:, None], length_x)
    along_y = window(y_cells[None, :] - near[2][:, None], length_y)
    along_z = window(z_cells[None, :] - near[3][:, None], length_z)
    plane = near[0][:, None, None] * along_x[:, :, None] * along_y[:, None, :]
    plane = plane.reshape(near.shape[1], x_cells.shape[0] * y_cells.shape[0])
    dense = jnp.dot(plane.T, along_z, precision=lax.Precision.HIGHEST)
    return dense.reshape(x_cells.shape[0], y_cells.shape[0], z_cells.shape[0])


def shards(pattern, matrix, atom_set, atom_slab, atom_offset):
    rows = matrix.shape[0]
    per_group = matrix.shape[1]
    block_width = matrix.shape[2]
    slots = pattern.shape[1]
    row_count = lax.axis_size("row")
    col_count = lax.axis_size("col")
    row_index = lax.axis_index("row")
    col_index = lax.axis_index("col")
    block_count = rows * row_count
    own_ids = row_index * rows + jnp.arange(rows, dtype=jnp.int32)
    own_pattern = lax.dynamic_slice_in_dim(pattern, row_index * rows, rows, 0)
    out_columns = lax.dynamic_slice_in_dim(own_pattern, col_index * per_group, per_group, 1)
    current = jnp.where((out_columns >= 0)[:, :, None, None], matrix, jnp.zeros((), matrix.dtype))
    on_diag = out_columns == own_ids[:, None]
    diag_entries = jnp.diagonal(current, axis1=2, axis2=3).astype(jnp.float32)
    own_diag = jnp.sum(jnp.where(on_diag[:, :, None], diag_entries, 0.0), axis=1)
    set_part = jnp.sum(own_diag.reshape(rows * (block_width // ORB), ORB), axis=1)
    set_charge = lax.psum(set_part, "col")
    trace = lax.psum(jnp.sum(set_part), ("row", "col"))
    weight = jax.nn.sigmoid(sharpness * (half_fill - trace / (block_count * block_width)))
    per_row = pattern.reshape(row_count, rows * slots)
    hits = jnp.any(per_row[:, :, None] == own_ids[None, None, :], axis=1)
    hits = hits & (jnp.arange(row_count, dtype=jnp.int32) != row_index)[:, None]
    outgoing = jnp.einsum(
        "qu,ukab->qkab", hits.astype(matrix.dtype), current, preferred_element_type=jnp.float32
    ).astype(matrix.dtype)
    incoming = lax.all_to_all(outgoing, "row", split_axis=0, concat_axis=0, tiled=True)
    my_refs = own_pattern.reshape(rows * slots)
    owners = jnp.floor_divide(my_refs, rows)
    from_owner = (owners[:, None] == jnp.arange(row_count, dtype=jnp.int32)[None, :]) & (
        owners != row_index
    )[:, None]
    incoming_ids = jnp.max(jnp.where(from_owner, my_refs[:, None], -1), axis=0)
    candidate_ids = jnp.concatenate([own_ids, incoming_ids])
    candidate_rows = pattern[jnp.maximum(candidate_ids, 0)]
    candidate_columns = jnp.where(
        candidate_ids[:, None] >= 0,
        lax.dynamic_slice_in_dim(candidate_rows, col_index * per_group, per_group, 1),
        -1,
    )
    candidates = jnp.concatenate([current, incoming], axis=0)
    start_total = jnp.zeros(matrix.shape, jnp.float32)
    piece = lax.all_gather(current, "col", axis=1, tiled=True)

    def one_group(number, running):
        offset = number * per_group
        blocks = lax.dynamic_slice_in_dim(piece, offset, per_group, 1)
        targets = lax.dynamic_slice_in_dim(own_pattern, offset, per_group, 1)
        holder = jnp.floor_divide(targets, rows)
        places = jnp.where(holder == row_index, targets - row_index * rows, rows + holder)
        places = jnp.where(targets >= 0, places, 0)
        chosen = candidates[places]
        chosen_columns = candidate_columns[places]
        matches = (
            (chosen_columns[..., None] == out_columns[:, None, None, :])
            & (targets >= 0)[:, :, None, None]
            & (out_columns >= 0)[:, None, None, :]
        )
        terms = jnp.einsum("itab,itkbc->itkac", blocks, chosen, preferred_element_type=jnp.float32)
        return running + jnp.einsum(
            "itkj,itkac->ijac", matches.astype(jnp.float32), terms, precision=lax.Precision.HIGHEST
        )

    product = lax.fori_loop(0, piece.shape[1] // per_group, one_group, start_total)
    purified = product + 2.0 * weight * (current.astype(jnp.float32) - product)
    atoms_here = atom_set.shape[0]
    lookup = (
        atom_set[:, None] - row_index * atoms_here
        == jnp.arange(atoms_here, dtype=jnp.int32)[None, :]
    ).astype(jnp.float32)
    charge = jnp.dot(lookup, set_charge, precision=lax.Precision.HIGHEST)
    start_x = atom_slab.astype(jnp.float32) * PLANES + atom_offset[0]
    packed = jnp.stack([charge, start_x, atom_offset[1], atom_offset[2]])
    pieces = [packed]
    for distance in (1, -1, 2, -2):
        pieces.append(from_behind(packed, "row", distance))
    near = jnp.concatenate(pieces, axis=1)
    x_cells = (row_index * PLANES + jnp.arange(PLANES, dtype=jnp.int32)).astype(jnp.float32)
    y_cells = (col_index * YC + jnp.arange(YC, dtype=jnp.int32)).astype(jnp.float32)
    z_cells = jnp.arange(GZ, dtype=jnp.int32).astype(jnp.float32)
    density = collocate(near, x_cells, y_cells, z_cells, PLANES * row_count, YC * col_count, GZ)
    return (purified, density)


def solution(mesh):
    placed = (P(), P("row", "col", None, None), P("row"), P("row"), P(None, "row"))
    return jax.shard_map(
        shards,
        mesh=mesh,
        in_specs=placed,
        out_specs=(P("row", "col", None, None), P("row", "col", None)),
        check_vma=False,
    )
```

profile of v0, /device:TPU:6, one launch (start us, length us, event | category | flops | bytes accessed | tf_op | source)
XLA Modules:
  0.0 375.9 jit_solution(17938466572439853437)
XLA Ops:
  7.2 0.8 copy.83
  8.5 1.0 broadcast_select_fusion
  9.6 1.3 convolution_convert_fusion
  10.9 4.7 %copy.88 = bf16[64,2,128,128]{3,2,1,0:T(8,128)(2,1)} copy(bf16[64,2,128,128]{3,0,2,1:T(8,128)(2,1)S(1)} %convolution_convert_fusion) | data formatting | bytes 8388608 | tf_op jit(solution)/shard_map/convert_element_type | solution.py:64
  15.5 18.8 %all-to-all-start = ((bf16[64,2,128,128]{3,2,1,0:T(8,128)(2,1)}), bf16[64,2,128,128]{3,2,1,0:T(8,128)(2,1)}, u32[]{:S(2)}, u32[]{:S(2)}) async-start(bf16[64,2,128,128]{3,2,1,0:T(8,128)(2,1)} %copy.88), calls=%async_computation | async-start | bytes 8388608 | tf_op jit(solution)/shard_map/all_to_all | solution.py:65
  35.2 9.4 %copy.92 = bf16[4,2,128,128]{0,1,3,2:T(2,128)(2,1)} copy(bf16[4,2,128,128]{3,2,1,0:T(8,128)(2,1)S(1)} %broadcast_select_fusion) | data formatting | bytes 524288 | tf_op jit(solution)/shard_map/jit(_where)/select_n | solution.py:51
  44.7 4.3 %gather_fusion.3 = bf16[128,4,2]{1,2,0:T(2,128)(2,1)S(1)} fusion(bf16[4,2,128,128]{0,1,3,2:T(2,128)(2,1)} %copy.92, s32[128]{0:T(128)S(1)} %or_bitcast_fusion), kind=kCustom, calls=%fused_computation.3 | custom fusion | bytes 5120 | tf_op jit(solution)/shard_map/jit(diagonal)/gather | solution.py:53
  49.0 0.8 fusion.38
  50.1 15.1 %psum.15 = f32[64]{0:T(128)S(1)} all-reduce(f32[64]{0:T(128)S(1)} %reduce_sum.29), channel_id=1, replica_groups=mesh['row'=64,'col'=8] {'col'}, use_global_device_ids=true, to_apply=%region_8.9 | all-reduce | flops 64 | bytes 512 | tf_op jit(solution)/shard_map/psum | solution.py:56
  65.4 3.0 collective-permute-start
  68.4 2.9 collective-permute-start.1
  71.3 4.3 %collective-permute-start.2 = (f32[4,64]{1,0:T(4,128)S(1)}, f32[4,64]{1,0:T(4,128)S(1)}, u32[]{:S(2)}, u32[]{:S(2)}) collective-permute-start(f32[4,64]{1,0:T(4,128)S(1)} %pad_maximum_fusion.1), channel_id=1, source_target_pairs={{0,16},{8,24},{16,32},{24,40},{32,48},{40,56},{48,64},{56,72},{64,... | collective-permute-start | bytes 3080 | tf_op jit(solution)/shard_map/ppermute | solution.py:19
  75.6 3.0 collective-permute-start.3
  79.7 208.1 %psum.14 = f32[]{:T(128)} all-reduce(f32[]{:T(128)} %get-tuple-element.292), channel_id=1, replica_groups=mesh['row'=64,'col'=8] {'row','col'}, use_global_device_ids=true, to_apply=%region_5.6 | all-reduce | flops 1 | bytes 8 | tf_op jit(solution)/shard_map/psum | solution.py:57
  288.9 3.1 fusion.18
  292.0 4.6 %pad_maximum_fusion = bf16[68,2,128,128]{3,2,1,0:T(8,128)(2,1)} fusion(bf16[64,2,128,128]{3,2,1,0:T(8,128)(2,1)} %all-to-all-done, bf16[4,2,128,128]{3,2,1,0:T(8,128)(2,1)S(1)} %broadcast_select_fusion), kind=kLoop, calls=%fused_computation.28 | loop fusion | flops 2228224 | bytes 8912896 | tf_op jit(solution)/shard_map/concatenate | solution.py:79
  296.7 71.4 %while.16 = (s32[]{:T(128)}, f32[4,2,128,128]{3,1,2,0:T(2,128)S(1)}, s32[4,16]{1,0:T(4,128)S(1)}, s32[]{:T(128)}, s32[]{:T(128)}, /*index=5*/s32[68,2]{1,0:T(8,1...) while((s32[]{:T(128)}, ...), condition=%wide.region_3.4_spmd.clone, body=%wide.region_2.3_spmd.clone.sunk | while | flops 73663792 | bytes 7082829 | solution.py:102
  296.8 2.9 gather_fusion
  299.8 1.3 convolution_bitcast_fusion.3
  301.1 0.7 copy.113
  302.5 3.1 fusion.84
  305.8 2.9 gather_fusion
  308.7 1.3 convolution_bitcast_fusion.3
  310.0 0.7 copy.113
  311.4 3.1 fusion.84
  314.7 2.9 gather_fusion
  317.6 1.3 convolution_bitcast_fusion.3
  318.9 0.7 copy.113
  320.4 3.1 fusion.84
  323.6 2.9 gather_fusion
  326.5 1.3 convolution_bitcast_fusion.3
  327.8 0.7 copy.113
  329.3 3.1 fusion.84
  332.5 2.9 gather_fusion
  335.5 1.3 convolution_bitcast_fusion.3
  336.8 0.7 copy.113
  338.2 3.1 fusion.84
  341.5 2.9 gather_fusion
  344.4 1.3 convolution_bitcast_fusion.3
  345.7 0.7 copy.113
  347.1 3.1 fusion.84
  350.4 2.9 gather_fusion
  353.3 1.3 convolution_bitcast_fusion.3
  356.1 3.1 fusion.84
  359.3 2.9 gather_fusion
  362.2 1.3 convolution_bitcast_fusion.3
  365.0 3.1 fusion.84
  368.1 1.0 multiply_add_fusion
  (100 shorter events, 11.6 us)
Async XLA Ops:
  15.5 276.5 %all-to-all-start = ((bf16[64,2,128,128]{3,2,1,0:T(8,128)(2,1)}), bf16[64,2,128,128]{3,2,1,0:T(8,128)(2,1)}, u32[]{:S(2)}, u32[]{:S(2)}) async-start(bf16[64,2,128,128]{3,2,1,0:T(8,128)(2,1)} %copy.88), calls=%async_computation | async-start | bytes 8388608 | tf_op jit(solution)/shard_map/all_to_all | solution.py:65
  34.3 262.3 %all-gather.2.cloned.1.call-start = ((), (), s32[]{:S(2)}) async-start(), calls=%async_computation.1 | async-start | bytes 2359296 | tf_op jit(solution)/shard_map/all_gather | solution.py:81
  35.1 9.6 %copy-start.1 = (f32[3,64]{1,0:T(4,128)S(1)}, f32[3,64]{1,0:T(4,128)}, u32[]{:S(2)}) copy-start(f32[3,64]{1,0:T(4,128)} %param.11) | copy-start | bytes 2308
  35.1 30.1 %copy-start.2 = (s32[64]{0:T(128)S(1)}, s32[64]{0:T(128)}, u32[]{:S(2)}) copy-start(s32[64]{0:T(128)} %param.9) | copy-start | bytes 772
  35.1 30.2 %copy-start.3 = (s32[64]{0:T(128)S(1)}, s32[64]{0:T(128)}, u32[]{:S(2)}) copy-start(s32[64]{0:T(128)} %param.10) | copy-start | bytes 772
  65.4 223.0 %collective-permute-start = (f32[4,64]{1,0:T(4,128)S(1)}, f32[4,64]{1,0:T(4,128)S(1)}, u32[]{:S(2)}, u32[]{:S(2)}) collective-permute-start(f32[4,64]{1,0:T(4,128)S(1)} %pad_maximum_fusion.1), channel_id=1, source_target_pairs={{0,8},{8,16},{16,24},{24,32},{32,40},{40,48},{48,56},{56,64},{64,7... | collective-permute-start | bytes 3080 | tf_op jit(solution)/shard_map/ppermute | solution.py:19
  68.4 220.1 %collective-permute-start.1 = (f32[4,64]{1,0:T(4,128)S(1)}, f32[4,64]{1,0:T(4,128)S(1)}, u32[]{:S(2)}, u32[]{:S(2)}) collective-permute-start(f32[4,64]{1,0:T(4,128)S(1)} %pad_maximum_fusion.1), channel_id=1, source_target_pairs={{0,504},{8,0},{16,8},{24,16},{32,24},{40,32},{48,40},{56,48},{64,5... | collective-permute-start | bytes 3080 | tf_op jit(solution)/shard_map/ppermute | solution.py:19
  71.3 217.2 %collective-permute-start.2 = (f32[4,64]{1,0:T(4,128)S(1)}, f32[4,64]{1,0:T(4,128)S(1)}, u32[]{:S(2)}, u32[]{:S(2)}) collective-permute-start(f32[4,64]{1,0:T(4,128)S(1)} %pad_maximum_fusion.1), channel_id=1, source_target_pairs={{0,16},{8,24},{16,32},{24,40},{32,48},{40,56},{48,64},{56,72},{64,... | collective-permute-start | bytes 3080 | tf_op jit(solution)/shard_map/ppermute | solution.py:19
  75.6 212.9 %collective-permute-start.3 = (f32[4,64]{1,0:T(4,128)S(1)}, f32[4,64]{1,0:T(4,128)S(1)}, u32[]{:S(2)}, u32[]{:S(2)}) collective-permute-start(f32[4,64]{1,0:T(4,128)S(1)} %pad_maximum_fusion.1), channel_id=1, source_target_pairs={{0,496},{8,504},{16,0},{24,8},{32,16},{40,24},{48,32},{56,40},{64,... | collective-permute-start | bytes 3080 | tf_op jit(solution)/shard_map/ppermute | solution.py:19
  296.7 71.4 %copy-start = (bf16[4,2,128,128]{3,2,1,0:T(8,128)(2,1)S(1)}, bf16[4,2,128,128]{3,2,1,0:T(8,128)(2,1)}, u32[]{:S(2)}) copy-start(bf16[4,2,128,128]{3,2,1,0:T(8,128)(2,1)} %param.8) | copy-start | bytes 786436
Sparse Core Ops, SparseCore 0:
  37.9 33.8 all-gather.1
where the time goes:
time: 378 us; the launch traced here: 376 us
  blocking collectives  223 us (59%)
  local copies, waits for them, and re-layouts  56.4 us (15%)
  matrix products  39.5 us (10%)
  starting transfers between devices  32 us (8%)
  between operations  15 us (4%)
  other arithmetic  9.32 us (2%)
    psum x1, blocking collectives, shards(): trace = lax.psum(jnp.sum(set_part), ('row', 'col'))  208 us
    dot_general x8, matrix products, one_group(): jnp.einsum('itkj,itkac->ijac', matches.astype(jnp.float32), terms, precis...  24.5 us
    gather x8, local copies, waits for them, and re-layouts, one_group(): chosen = candidates[places]  23.3 us
    all_to_all x1, starting transfers between devices, shards(): lax.all_to_all(outgoing, 'row', split_axis=0, concat_axis=0, tiled=True)  18.8 us
    psum x1, blocking collectives, shards(): set_charge = lax.psum(set_part, 'col')  15.1 us
    ppermute x4, starting transfers between devices, from_behind(): return lax.ppermute(value, axis, pairs)  13.2 us
    dot_general x8, matrix products, one_group(): jnp.einsum('itab,itkbc->itkac', blocks, chosen, preferred_element_type=jn...  10.4 us
    select_n x2, local copies, waits for them, and re-layouts, shards(): jnp.where((out_columns >= 0)[:, :, None, None], matrix, jnp.zeros((), mat...  10.2 us
  transfers between devices with their start and end apart: 6, of which 0 were waited for; matrix products, arithmetic and copies ran while one was open for 7% of the time, Pallas kernels for 0%

commit v1 on v0

v1 whole, which is shorter than its diff:
```python
import functools

import jax
import jax.numpy as jnp
from jax import lax
from jax.experimental import pallas as pl
from jax.experimental.pallas import tpu as pltpu
from jax.sharding import Mesh, PartitionSpec as P

ORB = 8
PLANES = 4
YC = 80
GZ = 640
NZ, NX, NY, NCORE = 16, 4, 4, 2
BR, KC, SLOTS, BS, NB = 4, 2, 16, 128, 256
CAP = 16
FULL = NZ * KC
ITEMS = BR * SLOTS * KC
ROW = ("z", "x")
COL = ("y", "core")

sharpness = 64.0
half_fill = 0.5


def shift(value, axis, steps):
    count = lax.axis_size(axis)
    return lax.ppermute(value, axis, [(s, (s + steps) % count) for s in range(count)])


def window(delta, length):
    folded = jnp.mod(delta + 0.5 * length, length) - 0.5 * length
    inside = jnp.maximum(1.0 - folded / PLANES * (folded / PLANES), 0.0)
    return inside * inside


def collocate(near, x_cells, y_cells, z_cells, length_x, length_y, length_z):
    along_x = window(x_cells[None, :] - near[1][:, None], length_x)
    along_y = window(y_cells[None, :] - near[2][:, None], length_y)
    along_z = window(z_cells[None, :] - near[3][:, None], length_z)
    plane = near[0][:, None, None] * along_x[:, :, None] * along_y[:, None, :]
    plane = plane.reshape(near.shape[1], x_cells.shape[0] * y_cells.shape[0])
    dense = jnp.dot(plane.T, along_z, precision=lax.Precision.HIGHEST)
    return dense.reshape(x_cells.shape[0], y_cells.shape[0], z_cells.shape[0])


def select_kernel(base, codes, counts, held, *rest):
    outs, sems = rest[: NX - 1], rest[NX - 1]

    def copy(d, j):
        return pltpu.make_async_copy(
            held.at[codes[d * FULL + base + j]], outs[d].at[j], sems.at[d, j]
        )

    fills = [jnp.clip(counts[d] - base, 0, CAP) for d in range(NX - 1)]
    for d in range(NX - 1):
        lax.fori_loop(0, fills[d], lambda j, _, d=d: copy(d, j).start(), None)
    for d in range(NX - 1):
        lax.fori_loop(0, fills[d], lambda j, _, d=d: copy(d, j).wait(), None)


def select(codes, counts, held, base):
    block = jax.ShapeDtypeStruct((CAP, BS, BS), jnp.bfloat16)
    return pl.pallas_call(
        functools.partial(select_kernel, base),
        out_shape=[block] * (NX - 1),
        in_specs=[
            pl.BlockSpec(memory_space=pltpu.SMEM),
            pl.BlockSpec(memory_space=pltpu.SMEM),
            pl.BlockSpec(memory_space=pl.ANY),
        ],
        out_specs=[pl.BlockSpec(memory_space=pl.ANY)] * (NX - 1),
        scratch_shapes=[pltpu.SemaphoreType.DMA((NX - 1, CAP))],
        name="select",
    )(codes, counts, held)


def product_kernel(items, count, scale, lefts, *rest):
    rights, mine, out = rest[:NX], rest[NX], rest[NX + 1]
    left_buf, right_buf, left_sem, right_sem = rest[NX + 2 :]
    total = count[0]

    def begin(n, _):
        code = items[n]
        pltpu.make_async_copy(
            lefts.at[lax.rem(code, 128)], left_buf.at[n], left_sem.at[n]
        ).start()
        source = lax.div(code, 1024)
        group = lax.div(source, 128)
        place = lax.rem(source, 128)
        for g in range(NX):

            @pl.when(group == g)
            def _():
                pltpu.make_async_copy(
                    rights[g].at[place], right_buf.at[n], right_sem.at[n]
                ).start()

    lax.fori_loop(0, total, begin, None)
    out[...] = jnp.zeros_like(out)

    def multiply(n, _):
        pltpu.make_async_copy(lefts.at[0], left_buf.at[n], left_sem.at[n]).wait()
        pltpu.make_async_copy(rights[0].at[0], right_buf.at[n], right_sem.at[n]).wait()
        target = lax.rem(lax.div(items[n], 128), 8)
        out[target] += jnp.dot(
            left_buf[n], right_buf[n], preferred_element_type=jnp.float32
        )

    lax.fori_loop(0, total, multiply, None)
    twice = scale[0]
    for o in range(BR * KC):
        value = out[o]
        out[o] = value + twice * (mine[o].astype(jnp.float32) - value)


def multiply_items(items, count, scale, lefts, rights, mine):
    smem = pl.BlockSpec(memory_space=pltpu.SMEM)
    anywhere = pl.BlockSpec(memory_space=pl.ANY)
    vmem = pl.BlockSpec(memory_space=pltpu.VMEM)
    return pl.pallas_call(
        product_kernel,
        out_shape=jax.ShapeDtypeStruct((BR * KC, BS, BS), jnp.float32),
        in_specs=[smem, smem, smem] + [anywhere] * (1 + NX) + [vmem],
        out_specs=vmem,
        scratch_shapes=[
            pltpu.VMEM((ITEMS, BS, BS), jnp.bfloat16),
            pltpu.VMEM((ITEMS, BS, BS), jnp.bfloat16),
            pltpu.SemaphoreType.DMA((ITEMS,)),
            pltpu.SemaphoreType.DMA((ITEMS,)),
        ],
        compiler_params=pltpu.CompilerParams(vmem_limit_bytes=24 * 1024 * 1024),
        name="product",
    )(items, count, scale, lefts, *rights, mine)


def compact(wanted, places, codes, slots):
    hit = wanted[..., None, :] & (places[..., None, :] == jnp.arange(slots)[:, None])
    return jnp.sum(jnp.where(hit, codes[..., None, :], 0), axis=-1)


def places_of(wanted):
    size = wanted.shape[-1]
    before = jnp.arange(size)[None, :] < jnp.arange(size)[:, None]
    return jnp.sum((wanted[..., None, :] & before).astype(jnp.int32), axis=-1)


def lookup(index, table):
    chosen = index[:, None] == jnp.arange(table.shape[0], dtype=jnp.int32)[None, :]
    found = jnp.dot(
        chosen.astype(jnp.bfloat16),
        table.astype(jnp.bfloat16),
        preferred_element_type=jnp.float32,
    )
    return found.astype(jnp.int32)


def plan(pattern, z, x, y, core):
    col = y * NCORE + core
    plane = lax.dynamic_slice_in_dim(pattern, z * NX * BR, NX * BR, 0)
    group = lax.dynamic_slice_in_dim(pattern, col * KC, KC, 1)
    targets = lax.dynamic_slice_in_dim(plane, col * KC, KC, 1)
    named = lookup(plane.reshape(-1), group).reshape(NX * BR, SLOTS, KC)
    match = (
        (named[..., None] == targets[:, None, None, :])
        & (plane >= 0)[:, :, None, None]
        & (targets >= 0)[:, None, None, :]
    )
    need = jnp.any(match, axis=-1).reshape(NX, BR * SLOTS, KC)
    refs = plane.reshape(NX, BR * SLOTS)
    owner = jnp.where(refs >= 0, refs // BR, -1)
    hit = owner[:, :, None] == jnp.arange(NZ * NX, dtype=jnp.int32)
    table = jnp.stack(
        [jnp.any(hit & need[:, :, u : u + 1], axis=1) for u in range(KC)], axis=-1
    )
    within = jnp.max(jnp.where(hit, (refs % BR)[:, :, None], 0), axis=1)
    table = table.reshape(NX, NZ, NX, KC).transpose(0, 2, 1, 3).reshape(NX, NX, FULL)
    within = within.reshape(NX, NZ, NX).transpose(0, 2, 1)
    place = places_of(table)
    counts = jnp.sum(table.astype(jnp.int32), axis=-1)
    apart = jnp.arange(NX)[:, None] != jnp.arange(NX)[None, :]
    over = jnp.sum((apart & (counts > CAP)).astype(jnp.int32))

    zs = jnp.arange(NZ, dtype=jnp.int32)[None, :, None]
    us = jnp.arange(KC, dtype=jnp.int32)[None, None, :]
    own_table = lax.dynamic_index_in_dim(table, x, 1, False)
    own_place = lax.dynamic_index_in_dim(place, x, 1, False)
    own_within = lax.dynamic_index_in_dim(within, x, 1, False)
    own_counts = lax.dynamic_index_in_dim(counts, x, 1, False)
    codes = (zs * BR + own_within[:, :, None]) * KC + us
    sends = compact(own_table, own_place, codes.reshape(NX, FULL), FULL)
    to = (x + jnp.arange(1, NX)) % NX
    pick = (to[:, None] == jnp.arange(NX)[None, :]).astype(jnp.int32)
    sends = jnp.sum(pick[:, :, None] * sends[None], axis=1)
    send_counts = jnp.sum(pick * own_counts[None], axis=1)

    my_refs = lax.dynamic_index_in_dim(refs, x, 0, False)
    my_match = lax.dynamic_slice_in_dim(match, x * BR, BR, 0)
    my_place = lax.dynamic_index_in_dim(place, x, 0, False)
    my_place = my_place.reshape(NX, NZ, KC).transpose(1, 0, 2).reshape(NZ * NX, KC)
    my_owner = jnp.maximum(my_refs, 0) // BR
    there = lookup(my_owner, my_place)
    from_x = my_owner % NX
    us = jnp.arange(KC, dtype=jnp.int32)[None, :]
    at_home = ((my_owner // NX * BR + my_refs % BR) * KC)[:, None] + us
    away = (x - from_x) % NX
    source = jnp.where((away == 0)[:, None], at_home, away[:, None] * 128 + there)
    slot = jnp.arange(SLOTS, dtype=jnp.int32)
    left_y = (y - slot // (KC * NCORE)) % NY
    left_core = slot // KC % NCORE
    rows = jnp.arange(BR, dtype=jnp.int32)[:, None]
    left = ((left_core * NY + left_y)[None, :] * BR + rows) * KC + (slot % KC)[None, :]
    wanted = jnp.any(my_match, axis=-1)
    aim = rows[:, :, None] * KC + my_match[..., 1].astype(jnp.int32)
    code = left[:, :, None] + 128 * aim + 1024 * source.reshape(BR, SLOTS, KC)
    wanted = wanted.reshape(ITEMS)
    items = compact(wanted, places_of(wanted), code.reshape(ITEMS), ITEMS)
    return (
        sends.reshape(-1),
        send_counts,
        items,
        jnp.sum(wanted.astype(jnp.int32)).reshape(1),
        over,
        targets,
    )


def shards(pattern, matrix, atom_set, atom_slab, atom_offset):
    z, x = lax.axis_index("z"), lax.axis_index("x")
    y, core = lax.axis_index("y"), lax.axis_index("core")
    row = z * NX + x
    col = y * NCORE + core
    held = lax.all_gather(matrix, "z", axis=0, tiled=True)
    held = held.reshape(NZ * BR * KC, BS, BS)

    lefts = jnp.stack([matrix] + [shift(matrix, "y", d) for d in range(1, NY)])
    lefts = lax.all_gather(lefts, "core", axis=0, tiled=False)
    lefts = lefts.reshape(NCORE * NY * BR * KC, BS, BS)

    sends, send_counts, items, count, over, plane_targets = plan(pattern, z, x, y, core)
    targets = lax.dynamic_slice_in_dim(plane_targets, x * BR, BR, 0)

    own_ids = row * BR + jnp.arange(BR, dtype=jnp.int32)
    on_diag = targets == own_ids[:, None]
    keep = on_diag[:, :, None, None] & jnp.eye(BS, dtype=bool)
    own_diag = jnp.sum(jnp.where(keep, matrix.astype(jnp.float32), 0.0), axis=(1, 2))
    sets = BS // ORB
    gather_sets = (
        jnp.arange(BS)[:, None] // ORB == jnp.arange(sets)[None, :]
    ).astype(jnp.float32)
    set_part = jnp.dot(own_diag, gather_sets, precision=lax.Precision.HIGHEST)
    packed = jnp.concatenate([set_part.reshape(-1), over.astype(jnp.float32)[None]])
    packed = lax.psum(packed, COL)
    set_charge = packed[: BR * sets]
    sums = jnp.stack([jnp.sum(set_charge), packed[BR * sets]])
    sums = lax.psum(lax.psum(sums, "x"), "z")
    weight = jax.nn.sigmoid(sharpness * (half_fill - sums[0] / (NB * BS)))
    scale = (2.0 * weight).reshape(1)

    atoms_here = atom_set.shape[0]
    find = (
        atom_set[:, None] - row * atoms_here
        == jnp.arange(atoms_here, dtype=jnp.int32)[None, :]
    ).astype(jnp.float32)
    charge = jnp.dot(find, set_charge, precision=lax.Precision.HIGHEST)
    start_x = atom_slab.astype(jnp.float32) * PLANES + atom_offset[0]
    packed = jnp.stack([charge, start_x, atom_offset[1], atom_offset[2]])
    pieces = [packed] + [shift(packed, ROW, d) for d in (1, -1, 2, -2)]
    near = jnp.concatenate(pieces, axis=1)
    x_cells = (row * PLANES + jnp.arange(PLANES, dtype=jnp.int32)).astype(jnp.float32)
    y_cells = (col * YC + jnp.arange(YC, dtype=jnp.int32)).astype(jnp.float32)
    z_cells = jnp.arange(GZ, dtype=jnp.int32).astype(jnp.float32)
    density = collocate(
        near, x_cells, y_cells, z_cells, PLANES * NZ * NX, YC * NY * NCORE, GZ
    )

    mine = matrix.reshape(BR * KC, BS, BS)
    outgoing = select(sends, send_counts, held, 0)
    first = [shift(outgoing[d - 1], "x", d) for d in range(1, NX)]

    def one_round(*first):
        return multiply_items(items, count, scale, lefts, [held, *first], mine)

    def two_rounds(*first):
        more = select(sends, send_counts, held, CAP)
        both = [
            jnp.concatenate([first[d - 1], shift(more[d - 1], "x", d)])
            for d in range(1, NX)
        ]
        return multiply_items(items, count, scale, lefts, [held, *both], mine)

    purified = lax.cond(sums[1] > 0, two_rounds, one_round, *first)
    return purified.reshape(matrix.shape), density


def solution(mesh):
    fine = Mesh(mesh.devices.reshape(NZ, NX, NY, NCORE), (*ROW, *COL))
    placed = (P(), P(ROW, COL, None, None), P(ROW), P(ROW), P(None, ROW))
    return jax.shard_map(
        shards,
        mesh=fine,
        in_specs=placed,
        out_specs=(P(ROW, COL, None, None), P(ROW, COL, None)),
        check_vma=False,
    )
```

time: 378 us -> 173 us (0.46)
  blocking collectives: 223 us -> 56.5 us
  local copies, waits for them, and re-layouts: 56.4 us -> 6.55 us
  matrix products: 39.5 us -> 4.64 us
  Pallas kernels: 0 us -> 20 us
  waiting for transfers between devices: 0.03 us -> 11.8 us
  starting transfers between devices: 32 us -> 43 us
    psum x2 -> x3, blocking collectives: 223 us -> 56.5 us  [the longest x2 42.9 us: shards(): sums = lax.psum(lax.psum(sums, 'x'), 'z')]
    dot_general x18 -> x4, matrix products: 36.4 us -> 1.52 us  [the longest x2 1.14 us: lookup(): jnp.dot(chosen.astype(jnp.bfloat16), table.astype(jnp.bfloat16), preferre...]
    gather x26 -> x0, local copies, waits for them, and re-layouts: 33.5 us -> none  [the longest x8 23.3 us: one_group(): chosen = candidates[places]]
    ppermute x4 -> x10, starting transfers between devices: 13.2 us -> 42.9 us  [shift(): lax.ppermute(value, axis, [(s, (s + steps) % count) for s in range(count)])]
    pallas_call x0 -> x2, Pallas kernels: none -> 20 us  [the longest x1 11 us: select(): pl.pallas_call(functools.partial(select_kernel, base), out_shape=[block]...]
    all_to_all x1 -> x0, starting transfers between devices: 18.8 us -> none  [shards(): lax.all_to_all(outgoing, 'row', split_axis=0, concat_axis=0, tiled=True)]
    ppermute x4 -> x10, waiting for transfers between devices: 0.01 us -> 11.1 us  [shift(): lax.ppermute(value, axis, [(s, (s + steps) % count) for s in range(count)])]
    select_n x2 -> x0, local copies, waits for them, and re-layouts: 10.2 us -> none  [shards(): jnp.where((out_columns >= 0)[:, :, None, None], matrix, jnp.zeros((), mat...]
  transfers between devices with their start and end apart: 6 -> 12, of which waited for: 0 -> 2; matrix products, arithmetic and copies ran while one was open for 7% -> 13% of each run, Pallas kernels for 0% -> 6%
where the time goes in v1:
time: 173 us; the launch traced here: 172 us
  blocking collectives  56.5 us (33%)
  starting transfers between devices  43 us (25%)
  Pallas kernels  20 us (12%)
  between operations  16.5 us (10%)
  other arithmetic  12.8 us (7%)
  waiting for transfers between devices  11.8 us (7%)
  local copies, waits for them, and re-layouts  6.55 us (4%)
  matrix products  4.64 us (3%)
    ppermute x10, starting transfers between devices, shift(): lax.ppermute(value, axis, [(s, (s + steps) % count) for s in range(count)])  42.9 us
    psum x2, blocking collectives, shards(): sums = lax.psum(lax.psum(sums, 'x'), 'z')  42.9 us
    psum x1, blocking collectives, shards(): packed = lax.psum(packed, COL)  13.6 us
    ppermute x10, waiting for transfers between devices, shift(): lax.ppermute(value, axis, [(s, (s + steps) % count) for s in range(count)])  11.1 us
    pallas_call x1, Pallas kernels, select(): pl.pallas_call(functools.partial(select_kernel, base), out_shape=[block]...  11 us
    pallas_call x1, Pallas kernels, multiply_items(): pl.pallas_call(product_kernel, out_shape=jax.ShapeDtypeStruct((BR * KC, B...  8.95 us
  transfers between devices with their start and end apart: 12, of which 2 were waited for; matrix products, arithmetic and copies ran while one was open for 13% of the time, Pallas kernels for 6%

profile of v1, /device:TPU:6, one launch (start us, length us, event | category | flops | bytes accessed | tf_op | source)
XLA Modules:
  0.0 171.7 jit_solution(14126285904012644390)
XLA Ops:
  7.2 0.7 all-gather.4.cloned.1.call-update
  7.9 4.9 %collective-permute-start.5 = (bf16[4,2,128,128]{3,2,1,0:T(8,128)(2,1)}, bf16[4,2,128,128]{3,2,1,0:T(8,128)(2,1)S(1)}, u32[]{:S(2)}, u32[]{:S(2)}) collective-permute-start(bf16[4,2,128,128]{3,2,1,0:T(8,128)(2,1)} %param.8), channel_id=1, source_target_pairs={{0,6},{2,0},{4,2},{6,4},{1,7},{3,1},{5,3},{7,5},{8,14},{10,8},{12,... | collective-permute-start | bytes 786440 | tf_op jit(solution)/shard_map/ppermute | solution.py:28
  12.9 2.5 %collective-permute-start.4 = (bf16[4,2,128,128]{3,2,1,0:T(8,128)(2,1)}, bf16[4,2,128,128]{3,2,1,0:T(8,128)(2,1)S(1)}, u32[]{:S(2)}, u32[]{:S(2)}) collective-permute-start(bf16[4,2,128,128]{3,2,1,0:T(8,128)(2,1)} %param.8), channel_id=1, source_target_pairs={{0,4},{2,6},{4,0},{6,2},{1,5},{3,7},{5,1},{7,3},{8,12},{10,14},{12... | collective-permute-start | bytes 786440 | tf_op jit(solution)/shard_map/ppermute | solution.py:28
  15.4 2.9 %collective-permute-start.3 = (bf16[4,2,128,128]{3,2,1,0:T(8,128)(2,1)}, bf16[4,2,128,128]{3,2,1,0:T(8,128)(2,1)S(1)}, u32[]{:S(2)}, u32[]{:S(2)}) collective-permute-start(bf16[4,2,128,128]{3,2,1,0:T(8,128)(2,1)} %param.8), channel_id=1, source_target_pairs={{0,2},{2,4},{4,6},{6,0},{1,3},{3,5},{5,7},{7,1},{8,10},{10,12},{12... | collective-permute-start | bytes 786440 | tf_op jit(solution)/shard_map/ppermute | solution.py:28
  18.3 0.8 broadcast_compare_fusion
  19.4 0.9 convolution_convert_fusion
  20.4 0.2 copy.94
  20.5 0.8 broadcast_compare_fusion.2
  21.3 0.2 fusion.91
  21.9 0.2 fusion.31
  22.5 0.2 convert_reduce_fusion.3
  22.7 0.6 convert_reduce_fusion.4
  24.0 0.8 dynamic-slice_compare_fusion
  24.9 1.1 select_reduce_fusion
  26.0 0.2 fusion.45
  26.4 13.6 %psum.21 = f32[65]{0:T(128)S(1)} all-reduce(f32[65]{0:T(128)S(1)} %pad_maximum_fusion.5), channel_id=1, replica_groups=mesh['z'=16,'x'=4,'y'=4,'core'=2] {'y','core'}, use_global_device_ids=true, to_apply=%region_6.7 | all-reduce | flops 65 | bytes 520 | tf_op jit(solution)/shard_map/psum | solution.py:253
  40.1 0.6 slice.44
  40.6 0.7 slice.49
  41.3 0.6 slice_reduce_fusion.4
  41.9 1.4 pad_maximum_fusion.6
  43.3 0.7 broadcast_subtract_fusion
  43.9 0.2 fusion.47
  44.1 0.7 fusion.80
  44.9 3.3 %collective-permute-start.9 = (f32[4,64]{1,0:T(4,128)S(1)}, f32[4,64]{1,0:T(4,128)S(1)}, u32[]{:S(2)}, u32[]{:S(2)}) collective-permute-start(f32[4,64]{1,0:T(4,128)S(1)} %pad_maximum_fusion.4), channel_id=1, source_target_pairs={{0,8},{8,16},{16,24},{24,32},{32,40},{40,48},{48,56},{56,64},{64,7... | collective-permute-start | bytes 3080 | tf_op jit(solution)/shard_map/ppermute | solution.py:28
  48.2 7.6 %psum.22 = f32[2]{0:T(128)S(1)} all-reduce(f32[2]{0:T(128)S(1)} %pad_maximum_fusion.6), channel_id=1, replica_groups=mesh['z'=16,'x'=4,'y'=4,'core'=2] {'x'}, use_global_device_ids=true, to_apply=%region_8.9 | all-reduce | flops 2 | bytes 16 | tf_op jit(solution)/shard_map/psum | solution.py:256
  55.8 3.5 %collective-permute-start.10 = (f32[4,64]{1,0:T(4,128)S(1)}, f32[4,64]{1,0:T(4,128)S(1)}, u32[]{:S(2)}, u32[]{:S(2)}) collective-permute-start(f32[4,64]{1,0:T(4,128)S(1)} %pad_maximum_fusion.4), channel_id=1, source_target_pairs={{0,504},{8,0},{16,8},{24,16},{32,24},{40,32},{48,40},{56,48},{64,5... | collective-permute-start | bytes 3080 | tf_op jit(solution)/shard_map/ppermute | solution.py:28
  59.3 35.3 %psum.23 = f32[2]{0:T(128)S(1)} all-reduce(f32[2]{0:T(128)S(1)} %psum.22), channel_id=1, replica_groups=mesh['z'=16,'x'=4,'y'=4,'core'=2] {'z'}, use_global_device_ids=true, to_apply=%region_9.10 | all-reduce | flops 2 | bytes 16 | tf_op jit(solution)/shard_map/psum | solution.py:256
  94.9 0.4 convert_reduce_fusion
  95.8 0.6 fusion.93
  96.6 0.2 fusion.2
  96.9 0.2 copy.95
  97.3 5.1 %collective-permute-start.11 = (f32[4,64]{1,0:T(4,128)S(1)}, f32[4,64]{1,0:T(4,128)S(1)}, u32[]{:S(2)}, u32[]{:S(2)}) collective-permute-start(f32[4,64]{1,0:T(4,128)S(1)} %pad_maximum_fusion.4), channel_id=1, source_target_pairs={{0,16},{8,24},{16,32},{24,40},{32,48},{40,56},{48,64},{56,72},{64,... | collective-permute-start | bytes 3080 | tf_op jit(solution)/shard_map/ppermute | solution.py:28
  102.4 2.2 %collective-permute-start.12 = (f32[4,64]{1,0:T(4,128)S(1)}, f32[4,64]{1,0:T(4,128)S(1)}, u32[]{:S(2)}, u32[]{:S(2)}) collective-permute-start(f32[4,64]{1,0:T(4,128)S(1)} %pad_maximum_fusion.4), channel_id=1, source_target_pairs={{0,496},{8,504},{16,0},{24,8},{32,16},{40,24},{48,32},{56,40},{64,... | collective-permute-start | bytes 3080 | tf_op jit(solution)/shard_map/ppermute | solution.py:28
  104.6 2.1 %pad_maximum_fusion.3 = bf16[4,4,2,128,128]{4,3,2,1,0:T(8,128)(2,1)} fusion(bf16[1,4,2,128,128]{4,3,2,1,0:T(8,128)(2,1)S(1)} %bitcast.75, bf16[1,4,2,128,128]{4,3,2,1,0:T(8,128)(2,1)S(1)} %bitcast.76, bf16[1,4,2,128,128]{4,3,2,1,0:T(8,128)(2,1)S(1)} %bitcast.77, bf16[1,4,2,128,128]{4,3,2,1,0:T(8,128)(2,1)} %bitcast.68), kind=kLoop, calls=%fused_computation.9 | loop fusion | flops 1572864 | bytes 2097152 | tf_op jit(solution)/shard_map/stack | solution.py:236
  106.8 0.2 fusion.62
  108.1 0.7 convert_reduce_fusion.2
  108.9 0.2 select_reduce_fusion.4.counts
  111.2 11.0 %select.152 = (bf16[16,128,128]{2,1,0:T(8,128)(2,1)}, bf16[16,128,128]{2,1,0:T(8,128)(2,1)}, bf16[16,128,128]{2,1,0:T(8,128)(2,1)}) custom-call(s32[96]{0:T(128)S(1)} %reshape.610.codes, s32[3]{0:T(128)S(1)} %select_reduce_fusion.4.counts, bf16[128,128,128]{2,1,0:T(8,128)(2,1)} %bitcast.63), custom_call_target="tpu_custom_call" | custom-call | tf_op jit(solution)/shard_map/select/pallas_call | solution.py:64
  122.2 13.7 %collective-permute-start.6 = (bf16[16,128,128]{2,1,0:T(8,128)(2,1)}, bf16[16,128,128]{2,1,0:T(8,128)(2,1)S(1)}, u32[]{:S(2)}, u32[]{:S(2)}) collective-permute-start(bf16[16,128,128]{2,1,0:T(8,128)(2,1)} %get-tuple-element.72), channel_id=1, source_target_pairs={{0,8},{8,16},{16,24},{24,0},{1,9},{9,17},{17,25},{25,1},{2,10},{10... | collective-permute-start | bytes 1572872 | tf_op jit(solution)/shard_map/ppermute | solution.py:28
  135.9 1.9 %collective-permute-start.7 = (bf16[16,128,128]{2,1,0:T(8,128)(2,1)}, bf16[16,128,128]{2,1,0:T(8,128)(2,1)S(1)}, u32[]{:S(2)}, u32[]{:S(2)}) collective-permute-start(bf16[16,128,128]{2,1,0:T(8,128)(2,1)} %get-tuple-element.73), channel_id=1, source_target_pairs={{0,16},{8,24},{16,0},{24,8},{1,17},{9,25},{17,1},{25,9},{2,18},{10... | collective-permute-start | bytes 1572872 | tf_op jit(solution)/shard_map/ppermute | solution.py:28
  137.9 2.8 %collective-permute-start.8 = (bf16[16,128,128]{2,1,0:T(8,128)(2,1)}, bf16[16,128,128]{2,1,0:T(8,128)(2,1)S(1)}, u32[]{:S(2)}, u32[]{:S(2)}) collective-permute-start(bf16[16,128,128]{2,1,0:T(8,128)(2,1)} %get-tuple-element.74), channel_id=1, source_target_pairs={{0,24},{8,0},{16,8},{24,16},{1,25},{9,1},{17,9},{25,17},{2,26},{10... | collective-permute-start | bytes 1572872 | tf_op jit(solution)/shard_map/ppermute | solution.py:28
  140.7 0.2 fusion.38
  140.9 3.1 %fusion.10 = f32[4,80,640]{2,1,0:T(8,128)} fusion(f32[320]{0:T(512)S(1)} %get-tuple-element.76, f32[640]{0:T(1024)S(1)} %iota_convert_fusion, f32[320,80]{0,1:T(8,128)S(1)} %fusion.38, f32[320,4]{0,1:T(4,128)S(1)} %fusion.56), kind=kOutput, calls=%fused_computation.17 | convolution fusion | flops 789401600 | bytes 930560 | tf_op jit(solution)/shard_map/dot_general | solution.py:43
  144.0 6.1 %collective-permute-done.6 = bf16[16,128,128]{2,1,0:T(8,128)(2,1)S(1)} collective-permute-done((bf16[16,128,128]{2,1,0:T(8,128)(2,1)}, bf16[16,128,128]{2,1,0:T(8,128)(2,1)S(1)}, u32[]{:S(2)}, u32[]{:S(2)}) %collective-permute-start.6) | collective-permute-done | bytes 524320 | tf_op jit(solution)/shard_map/ppermute | solution.py:28
  150.1 5.0 %collective-permute-done.8 = bf16[16,128,128]{2,1,0:T(8,128)(2,1)S(1)} collective-permute-done((bf16[16,128,128]{2,1,0:T(8,128)(2,1)}, bf16[16,128,128]{2,1,0:T(8,128)(2,1)S(1)}, u32[]{:S(2)}, u32[]{:S(2)}) %collective-permute-start.8) | collective-permute-done | bytes 524320 | tf_op jit(solution)/shard_map/ppermute | solution.py:28
  155.1 9.0 %conditional.1 = (f32[4,2,128,128]{3,2,1,0:T(8,128)S(1)}) conditional(s32[]{:T(128)} %bitcast.9, (s32[128]{0:T(128)S(1)}, s32[1]{0:T(128)}, f32[1]{0:T(128)}, bf16[64,128,128]{2,1,0:T(8,128)(2,1)}, bf16[128,128,128]{2,1,0:T(8,128)(2,1)}, /*index=5*/bf16[16,128,128]{2,1,0:T(8,128)(2,1)S(1)}, bf16[16,128,128]{2,1,0:T(8,128)(2,1)S(1)}, ...), branch_computations={%region_19.20_spmd, %region_20.21_spmd} | conditional | flops 1572864 | bytes 37748920 | solution.py:292
  155.1 8.9 %product.2 = f32[8,128,128]{2,1,0:T(8,128)S(1)} custom-call(s32[128]{0:T(128)S(1)} %get-tuple-element.44.items, s32[1]{0:T(128)} %get-tuple-element.45.count, f32[1]{0:T(128)} %get-tuple-element.46.scale, bf16[64,128,128]{2,1,0:T(8,128)(2,1)} %get-tuple-element.47.lefts, bf16[128,128,128]{2,1,0:T(8,128)(2,1)} %get-tuple-element.48.rest_0_, ...), custom_call_target="tpu_custom_call" | custom-call | tf_op jit(solution)/shard_map/cond/branch_0_fun/product/pallas_call | solution.py:121
  164.1 0.8 copy-done.3
  (84 shorter events, 4.8 us)
Async XLA Ops:
  7.2 104.0 %all-gather.4.cloned.1.call-start = ((), (), s32[]{:S(2)}) async-start(), calls=%async_computation | async-start | bytes 4456448 | tf_op jit(solution)/shard_map/all_gather | solution.py:233
  7.9 136.1 %all-gather.6.cloned.1.call-start = ((), (), s32[]{:S(2)}) async-start(), calls=%async_computation.1 | async-start | bytes 3145728 | tf_op jit(solution)/shard_map/all_gather | solution.py:237
  7.9 89.3 %collective-permute-start.5 = (bf16[4,2,128,128]{3,2,1,0:T(8,128)(2,1)}, bf16[4,2,128,128]{3,2,1,0:T(8,128)(2,1)S(1)}, u32[]{:S(2)}, u32[]{:S(2)}) collective-permute-start(bf16[4,2,128,128]{3,2,1,0:T(8,128)(2,1)} %param.8), channel_id=1, source_target_pairs={{0,6},{2,0},{4,2},{6,4},{1,7},{3,1},{5,3},{7,5},{8,14},{10,8},{12,... | collective-permute-start | bytes 786440 | tf_op jit(solution)/shard_map/ppermute | solution.py:28
  12.9 89.5 %collective-permute-start.4 = (bf16[4,2,128,128]{3,2,1,0:T(8,128)(2,1)}, bf16[4,2,128,128]{3,2,1,0:T(8,128)(2,1)S(1)}, u32[]{:S(2)}, u32[]{:S(2)}) collective-permute-start(bf16[4,2,128,128]{3,2,1,0:T(8,128)(2,1)} %param.8), channel_id=1, source_target_pairs={{0,4},{2,6},{4,0},{6,2},{1,5},{3,7},{5,1},{7,3},{8,12},{10,14},{12... | collective-permute-start | bytes 786440 | tf_op jit(solution)/shard_map/ppermute | solution.py:28
  15.4 89.2 %collective-permute-start.3 = (bf16[4,2,128,128]{3,2,1,0:T(8,128)(2,1)}, bf16[4,2,128,128]{3,2,1,0:T(8,128)(2,1)S(1)}, u32[]{:S(2)}, u32[]{:S(2)}) collective-permute-start(bf16[4,2,128,128]{3,2,1,0:T(8,128)(2,1)} %param.8), channel_id=1, source_target_pairs={{0,2},{2,4},{4,6},{6,0},{1,3},{3,5},{5,7},{7,1},{8,10},{10,12},{12... | collective-permute-start | bytes 786440 | tf_op jit(solution)/shard_map/ppermute | solution.py:28
  44.9 66.2 %collective-permute-start.9 = (f32[4,64]{1,0:T(4,128)S(1)}, f32[4,64]{1,0:T(4,128)S(1)}, u32[]{:S(2)}, u32[]{:S(2)}) collective-permute-start(f32[4,64]{1,0:T(4,128)S(1)} %pad_maximum_fusion.4), channel_id=1, source_target_pairs={{0,8},{8,16},{16,24},{24,32},{32,40},{40,48},{48,56},{56,64},{64,7... | collective-permute-start | bytes 3080 | tf_op jit(solution)/shard_map/ppermute | solution.py:28
  55.8 55.2 %collective-permute-start.10 = (f32[4,64]{1,0:T(4,128)S(1)}, f32[4,64]{1,0:T(4,128)S(1)}, u32[]{:S(2)}, u32[]{:S(2)}) collective-permute-start(f32[4,64]{1,0:T(4,128)S(1)} %pad_maximum_fusion.4), channel_id=1, source_target_pairs={{0,504},{8,0},{16,8},{24,16},{32,24},{40,32},{48,40},{56,48},{64,5... | collective-permute-start | bytes 3080 | tf_op jit(solution)/shard_map/ppermute | solution.py:28
  97.3 13.8 %collective-permute-start.11 = (f32[4,64]{1,0:T(4,128)S(1)}, f32[4,64]{1,0:T(4,128)S(1)}, u32[]{:S(2)}, u32[]{:S(2)}) collective-permute-start(f32[4,64]{1,0:T(4,128)S(1)} %pad_maximum_fusion.4), channel_id=1, source_target_pairs={{0,16},{8,24},{16,32},{24,40},{32,48},{40,56},{48,64},{56,72},{64,... | collective-permute-start | bytes 3080 | tf_op jit(solution)/shard_map/ppermute | solution.py:28
  102.4 8.7 %collective-permute-start.12 = (f32[4,64]{1,0:T(4,128)S(1)}, f32[4,64]{1,0:T(4,128)S(1)}, u32[]{:S(2)}, u32[]{:S(2)}) collective-permute-start(f32[4,64]{1,0:T(4,128)S(1)} %pad_maximum_fusion.4), channel_id=1, source_target_pairs={{0,496},{8,504},{16,0},{24,8},{32,16},{40,24},{48,32},{56,40},{64,... | collective-permute-start | bytes 3080 | tf_op jit(solution)/shard_map/ppermute | solution.py:28
  106.7 48.4 %copy-start.2 = (bf16[4,2,128,128]{3,2,1,0:T(8,128)(2,1)S(1)}, bf16[4,2,128,128]{3,2,1,0:T(8,128)(2,1)}, u32[]{:S(2)}) copy-start(bf16[4,2,128,128]{3,2,1,0:T(8,128)(2,1)} %param.8) | copy-start | bytes 786436
  122.2 27.9 %collective-permute-start.6 = (bf16[16,128,128]{2,1,0:T(8,128)(2,1)}, bf16[16,128,128]{2,1,0:T(8,128)(2,1)S(1)}, u32[]{:S(2)}, u32[]{:S(2)}) collective-permute-start(bf16[16,128,128]{2,1,0:T(8,128)(2,1)} %get-tuple-element.72), channel_id=1, source_target_pairs={{0,8},{8,16},{16,24},{24,0},{1,9},{9,17},{17,25},{25,1},{2,10},{10... | collective-permute-start | bytes 1572872 | tf_op jit(solution)/shard_map/ppermute | solution.py:28
  135.9 14.2 %collective-permute-start.7 = (bf16[16,128,128]{2,1,0:T(8,128)(2,1)}, bf16[16,128,128]{2,1,0:T(8,128)(2,1)S(1)}, u32[]{:S(2)}, u32[]{:S(2)}) collective-permute-start(bf16[16,128,128]{2,1,0:T(8,128)(2,1)} %get-tuple-element.73), channel_id=1, source_target_pairs={{0,16},{8,24},{16,0},{24,8},{1,17},{9,25},{17,1},{25,9},{2,18},{10... | collective-permute-start | bytes 1572872 | tf_op jit(solution)/shard_map/ppermute | solution.py:28
  137.9 17.3 %collective-permute-start.8 = (bf16[16,128,128]{2,1,0:T(8,128)(2,1)}, bf16[16,128,128]{2,1,0:T(8,128)(2,1)S(1)}, u32[]{:S(2)}, u32[]{:S(2)}) collective-permute-start(bf16[16,128,128]{2,1,0:T(8,128)(2,1)} %get-tuple-element.74), channel_id=1, source_target_pairs={{0,24},{8,0},{16,8},{24,16},{1,25},{9,1},{17,9},{25,17},{2,26},{10... | collective-permute-start | bytes 1572872 | tf_op jit(solution)/shard_map/ppermute | solution.py:28
  164.1 0.8 copy-start.3
Sparse Core Ops, SparseCore 0:
  10.1 83.1 all-gather.3
  106.9 19.0 all-gather.5

commit v2 on v1

--- a/solution.py
+++ b/solution.py
@@ -13,7 +13,7 @@
 GZ = 640
 NZ, NX, NY, NCORE = 16, 4, 4, 2
 BR, KC, SLOTS, BS, NB = 4, 2, 16, 128, 256
-CAP = 16
+CAP = 12
 FULL = NZ * KC
 ITEMS = BR * SLOTS * KC
 ROW = ("z", "x")
@@ -69,26 +69,28 @@
             pl.BlockSpec(memory_space=pltpu.SMEM),
             pl.BlockSpec(memory_space=pl.ANY),
         ],
-        out_specs=[pl.BlockSpec(memory_space=pl.ANY)] * (NX - 1),
+        out_specs=[pl.BlockSpec(memory_space=pltpu.VMEM)] * (NX - 1),
         scratch_shapes=[pltpu.SemaphoreType.DMA((NX - 1, CAP))],
         name="select",
     )(codes, counts, held)
 
 
-def product_kernel(items, count, scale, lefts, *rest):
-    rights, mine, out = rest[:NX], rest[NX], rest[NX + 1]
-    left_buf, right_buf, left_sem, right_sem = rest[NX + 2 :]
-    total = count[0]
-
+def run_items(items, total, lefts, rights, out, left_buf, right_buf, left_sem, right_sem):
     def begin(n, _):
         code = items[n]
-        pltpu.make_async_copy(
-            lefts.at[lax.rem(code, 128)], left_buf.at[n], left_sem.at[n]
-        ).start()
+        left = lax.rem(code, 128)
         source = lax.div(code, 1024)
         group = lax.div(source, 128)
         place = lax.rem(source, 128)
-        for g in range(NX):
+        for g in range(NCORE):
+
+            @pl.when(lax.div(left, 32) == g)
+            def _():
+                pltpu.make_async_copy(
+                    lefts[g].at[lax.rem(left, 32)], left_buf.at[n], left_sem.at[n]
+                ).start()
+
+        for g in range(len(rights)):
 
             @pl.when(group == g)
             def _():
@@ -96,33 +98,49 @@
                     rights[g].at[place], right_buf.at[n], right_sem.at[n]
                 ).start()
 
-    lax.fori_loop(0, total, begin, None)
-    out[...] = jnp.zeros_like(out)
-
     def multiply(n, _):
-        pltpu.make_async_copy(lefts.at[0], left_buf.at[n], left_sem.at[n]).wait()
+        pltpu.make_async_copy(lefts[0].at[0], left_buf.at[n], left_sem.at[n]).wait()
         pltpu.make_async_copy(rights[0].at[0], right_buf.at[n], right_sem.at[n]).wait()
         target = lax.rem(lax.div(items[n], 128), 8)
         out[target] += jnp.dot(
             left_buf[n], right_buf[n], preferred_element_type=jnp.float32
         )
 
+    lax.fori_loop(0, total, begin, None)
+    yield
     lax.fori_loop(0, total, multiply, None)
+
+
+def home_kernel(items, count, left0, left1, held, out, *scratch):
+    steps = run_items(items, count[0], (left0, left1), (held,), out, *scratch)
+    next(steps)
+    out[...] = jnp.zeros_like(out)
+    next(steps, None)
+
+
+def away_kernel(items, count, scale, left0, left1, *rest):
+    rights, begun, mine, out = rest[: NX - 1], rest[NX - 1], rest[NX], rest[NX + 1]
+    steps = run_items(items, count[0], (left0, left1), rights, out, *rest[NX + 2 :])
+    next(steps)
+    out[...] = begun[...]
+    next(steps, None)
     twice = scale[0]
     for o in range(BR * KC):
         value = out[o]
         out[o] = value + twice * (mine[o].astype(jnp.float32) - value)
 
 
-def multiply_items(items, count, scale, lefts, rights, mine):
-    smem = pl.BlockSpec(memory_space=pltpu.SMEM)
-    anywhere = pl.BlockSpec(memory_space=pl.ANY)
-    vmem = pl.BlockSpec(memory_space=pltpu.VMEM)
+SMEM = pl.BlockSpec(memory_space=pltpu.SMEM)
+ANYWHERE = pl.BlockSpec(memory_space=pl.ANY)
+VMEM = pl.BlockSpec(memory_space=pltpu.VMEM)
+
+
+def items_call(kernel, name, in_specs):
     return pl.pallas_call(
-        product_kernel,
+        kernel,
         out_shape=jax.ShapeDtypeStruct((BR * KC, BS, BS), jnp.float32),
-        in_specs=[smem, smem, smem] + [anywhere] * (1 + NX) + [vmem],
-        out_specs=vmem,
+        in_specs=in_specs,
+        out_specs=VMEM,
         scratch_shapes=[
             pltpu.VMEM((ITEMS, BS, BS), jnp.bfloat16),
             pltpu.VMEM((ITEMS, BS, BS), jnp.bfloat16),
@@ -130,8 +148,22 @@
             pltpu.SemaphoreType.DMA((ITEMS,)),
         ],
         compiler_params=pltpu.CompilerParams(vmem_limit_bytes=24 * 1024 * 1024),
-        name="product",
-    )(items, count, scale, lefts, *rights, mine)
+        cost_estimate=pl.CostEstimate(
+            flops=2 * 16 * BS**3, bytes_accessed=16 * 4 * BS * BS, transcendentals=0
+        ),
+        name=name,
+    )
+
+
+def home_products(items, count, lefts, held):
+    call = items_call(home_kernel, "home", [SMEM] * 2 + [ANYWHERE] * 3)
+    return call(items, count, *lefts, held)
+
+
+def away_products(items, count, scale, lefts, rights, begun, mine):
+    specs = [SMEM] * 3 + [ANYWHERE] * (NX + 1) + [VMEM] * 2
+    call = items_call(away_kernel, "away", specs)
+    return call(items, count, scale, *lefts, *rights, begun, mine)
 
 
 def compact(wanted, places, codes, slots):
@@ -204,25 +236,20 @@
     us = jnp.arange(KC, dtype=jnp.int32)[None, :]
     at_home = ((my_owner // NX * BR + my_refs % BR) * KC)[:, None] + us
     away = (x - from_x) % NX
-    source = jnp.where((away == 0)[:, None], at_home, away[:, None] * 128 + there)
+    source = jnp.where((away == 0)[:, None], at_home, (away[:, None] - 1) * 128 + there)
     slot = jnp.arange(SLOTS, dtype=jnp.int32)
     left_y = (y - slot // (KC * NCORE)) % NY
-    left_core = slot // KC % NCORE
+    left_core = (slot // KC + core) % NCORE
     rows = jnp.arange(BR, dtype=jnp.int32)[:, None]
     left = ((left_core * NY + left_y)[None, :] * BR + rows) * KC + (slot % KC)[None, :]
     wanted = jnp.any(my_match, axis=-1)
     aim = rows[:, :, None] * KC + my_match[..., 1].astype(jnp.int32)
     code = left[:, :, None] + 128 * aim + 1024 * source.reshape(BR, SLOTS, KC)
-    wanted = wanted.reshape(ITEMS)
-    items = compact(wanted, places_of(wanted), code.reshape(ITEMS), ITEMS)
-    return (
-        sends.reshape(-1),
-        send_counts,
-        items,
-        jnp.sum(wanted.astype(jnp.int32)).reshape(1),
-        over,
-        targets,
-    )
+    wanted = wanted & jnp.stack([away == 0, away > 0]).reshape(2, BR, SLOTS, 1)
+    wanted = wanted.reshape(2, ITEMS)
+    items = compact(wanted, places_of(wanted), code.reshape(1, ITEMS), ITEMS)
+    totals = jnp.sum(wanted.astype(jnp.int32), axis=-1)
+    return sends.reshape(-1), send_counts, items, totals, over, targets
 
 
 def shards(pattern, matrix, atom_set, atom_slab, atom_offset):
@@ -233,11 +260,7 @@
     held = lax.all_gather(matrix, "z", axis=0, tiled=True)
     held = held.reshape(NZ * BR * KC, BS, BS)
 
-    lefts = jnp.stack([matrix] + [shift(matrix, "y", d) for d in range(1, NY)])
-    lefts = lax.all_gather(lefts, "core", axis=0, tiled=False)
-    lefts = lefts.reshape(NCORE * NY * BR * KC, BS, BS)
-
-    sends, send_counts, items, count, over, plane_targets = plan(pattern, z, x, y, core)
+    sends, send_counts, items, totals, over, plane_targets = plan(pattern, z, x, y, core)
     targets = lax.dynamic_slice_in_dim(plane_targets, x * BR, BR, 0)
 
     own_ids = row * BR + jnp.arange(BR, dtype=jnp.int32)
@@ -251,11 +274,11 @@
     set_part = jnp.dot(own_diag, gather_sets, precision=lax.Precision.HIGHEST)
     packed = jnp.concatenate([set_part.reshape(-1), over.astype(jnp.float32)[None]])
     packed = lax.psum(packed, COL)
+    blocks, packed = lax.optimization_barrier((matrix, packed))
+    lefts = jnp.concatenate([blocks] + [shift(blocks, "y", d) for d in range(1, NY)])
+    lefts = lefts.reshape(NY * BR * KC, BS, BS)
+    lefts = (lefts, shift(lefts, "core", 1))
     set_charge = packed[: BR * sets]
-    sums = jnp.stack([jnp.sum(set_charge), packed[BR * sets]])
-    sums = lax.psum(lax.psum(sums, "x"), "z")
-    weight = jax.nn.sigmoid(sharpness * (half_fill - sums[0] / (NB * BS)))
-    scale = (2.0 * weight).reshape(1)
 
     atoms_here = atom_set.shape[0]
     find = (
@@ -264,9 +287,25 @@
     ).astype(jnp.float32)
     charge = jnp.dot(find, set_charge, precision=lax.Precision.HIGHEST)
     start_x = atom_slab.astype(jnp.float32) * PLANES + atom_offset[0]
-    packed = jnp.stack([charge, start_x, atom_offset[1], atom_offset[2]])
-    pieces = [packed] + [shift(packed, ROW, d) for d in (1, -1, 2, -2)]
-    near = jnp.concatenate(pieces, axis=1)
+    flag = jnp.broadcast_to(packed[BR * sets], charge.shape)
+    packed = jnp.stack([charge, start_x, atom_offset[1], atom_offset[2], flag])
+    packed = lax.all_gather(packed, "x", axis=0, tiled=False)
+    packed = lax.all_gather(packed, "z", axis=0, tiled=False)
+    packed = packed.reshape(NZ * NX, 5, atoms_here)
+    over = jnp.sum(packed[:, 4, 0])
+    trace = jnp.sum(packed[:, 0])
+    weight = jax.nn.sigmoid(sharpness * (half_fill - trace / (NB * BS)))
+    scale = (2.0 * weight).reshape(1)
+    packed = jnp.concatenate([packed[-2:], packed, packed[:2]])
+    near = lax.dynamic_slice_in_dim(packed, row, 5, 0)[:, :4]
+    near = near.transpose(1, 0, 2).reshape(4, 5 * atoms_here)
+
+    mine = matrix.reshape(BR * KC, BS, BS)
+    outgoing = select(sends, send_counts, held, 0)
+    items, near, outgoing = lax.optimization_barrier((items, near, outgoing))
+    first = [shift(outgoing[d - 1], "x", d) for d in range(1, NX)]
+    begun = home_products(items[0], totals[:1], lefts, held)
+
     x_cells = (row * PLANES + jnp.arange(PLANES, dtype=jnp.int32)).astype(jnp.float32)
     y_cells = (col * YC + jnp.arange(YC, dtype=jnp.int32)).astype(jnp.float32)
     z_cells = jnp.arange(GZ, dtype=jnp.int32).astype(jnp.float32)
@@ -274,22 +313,22 @@
         near, x_cells, y_cells, z_cells, PLANES * NZ * NX, YC * NY * NCORE, GZ
     )
 
-    mine = matrix.reshape(BR * KC, BS, BS)
-    outgoing = select(sends, send_counts, held, 0)
-    first = [shift(outgoing[d - 1], "x", d) for d in range(1, NX)]
+    def finish(rights):
+        return away_products(items[1], totals[1:], scale, lefts, rights, begun, mine)
 
     def one_round(*first):
-        return multiply_items(items, count, scale, lefts, [held, *first], mine)
+        return finish(first)
 
     def two_rounds(*first):
-        more = select(sends, send_counts, held, CAP)
-        both = [
-            jnp.concatenate([first[d - 1], shift(more[d - 1], "x", d)])
-            for d in range(1, NX)
-        ]
-        return multiply_items(items, count, scale, lefts, [held, *both], mine)
-
-    purified = lax.cond(sums[1] > 0, two_rounds, one_round, *first)
+        both = list(first)
+        for base in range(CAP, FULL, CAP):
+            more = select(sends, send_counts, held, base)
+            for d in range(1, NX):
+                coming = shift(more[d - 1], "x", d)
+                both[d - 1] = jnp.concatenate([both[d - 1], coming])
+        return finish(both)
+
+    purified = lax.cond(over > 0, two_rounds, one_round, *first)
     return purified.reshape(matrix.shape), density
 
 

time: 173 us -> 145 us (0.84)
  starting transfers between devices: 43 us -> 18.5 us
  blocking collectives: 56.5 us -> 64.6 us
  other arithmetic: 12.8 us -> 7.59 us
  Pallas kernels: 20 us -> 15.1 us
  waiting for transfers between devices: 11.8 us -> 9.86 us
    all_gather x0 -> x2, blocking collectives: none -> 49.7 us  [the longest x1 37.6 us: shards(): packed = lax.all_gather(packed, 'z', axis=0, tiled=False)]
    psum x2 -> x0, blocking collectives: 42.9 us -> none  [shards(): sums = lax.psum(lax.psum(sums, 'x'), 'z')]
    ppermute x10 -> x7, starting transfers between devices: 42.9 us -> 18.4 us  [shift(): lax.ppermute(value, axis, [(s, (s + steps) % count) for s in range(count)])]
    pallas_call x1, Pallas kernels: 11 us -> 2.76 us  [select(): pl.pallas_call(functools.partial(select_kernel, base), out_shape=[block]...]
    another operation x4 -> x1, other arithmetic: 4.19 us -> 0.02 us  [shards(): packed = jnp.stack([charge, start_x, atom_offset[1], atom_offset[2], flag])]
    pallas_call x1 -> x2, Pallas kernels: 8.95 us -> 12.4 us  [the longest x1 7.27 us: away_products(): return call(items, count, scale, *lefts, *rights, begun, mine)]
    ppermute x10 -> x7, waiting for transfers between devices: 11.1 us -> 9.15 us  [shift(): lax.ppermute(value, axis, [(s, (s + steps) % count) for s in range(count)])]
  transfers between devices with their start and end apart: 12 -> 8, of which waited for: 2 -> 2; matrix products, arithmetic and copies ran while one was open for 13% -> 12% of each run, Pallas kernels for 6% -> 5%
where the time goes in v2:
time: 145 us; the launch traced here: 143 us
  blocking collectives  64.6 us (45%)
  starting transfers between devices  18.5 us (13%)
  between operations  16.6 us (11%)
  Pallas kernels  15.1 us (10%)
  waiting for transfers between devices  9.86 us (7%)
  other arithmetic  7.59 us (5%)
  local copies, waits for them, and re-layouts  6.24 us (4%)
  matrix products  4.65 us (3%)
    all_gather x1, blocking collectives, shards(): packed = lax.all_gather(packed, 'z', axis=0, tiled=False)  37.6 us
    ppermute x7, starting transfers between devices, shift(): lax.ppermute(value, axis, [(s, (s + steps) % count) for s in range(count)])  18.4 us
    psum x1, blocking collectives, shards(): packed = lax.psum(packed, COL)  14.8 us
    all_gather x1, blocking collectives, shards(): packed = lax.all_gather(packed, 'x', axis=0, tiled=False)  12.2 us
    ppermute x7, waiting for transfers between devices, shift(): lax.ppermute(value, axis, [(s, (s + steps) % count) for s in range(count)])  9.15 us
    pallas_call x1, Pallas kernels, away_products(): return call(items, count, scale, *lefts, *rights, begun, mine)  7.27 us
    pallas_call x1, Pallas kernels, home_products(): return call(items, count, *lefts, held)  5.09 us
    dot_general x1, matrix products, collocate(): dense = jnp.dot(plane.T, along_z, precision=lax.Precision.HIGHEST)  3.13 us
  transfers between devices with their start and end apart: 8, of which 2 were waited for; matrix products, arithmetic and copies ran while one was open for 12% of the time, Pallas kernels for 5%

profile of v2, /device:TPU:6, one launch (start us, length us, event | category | flops | bytes accessed | tf_op | source)
XLA Modules:
  0.0 143.1 jit_solution(2309210407283540706)
XLA Ops:
  7.2 0.7 all-gather.5.cloned.1.call-update
  8.0 0.8 broadcast_compare_fusion
  9.0 0.9 convolution_convert_fusion
  9.9 0.2 copy.99
  10.1 0.8 broadcast_compare_fusion.2
  10.9 0.2 fusion.94
  11.5 0.2 fusion.31
  12.1 0.2 convert_reduce_fusion.3
  12.3 0.6 convert_reduce_fusion.4
  13.6 0.8 dynamic-slice_compare_fusion
  14.5 0.2 select_reduce_fusion
  14.7 0.2 fusion.44
  15.1 14.8 %psum.7 = f32[65]{0:T(128)S(1)} all-reduce(f32[65]{0:T(128)S(1)} %pad_maximum_fusion.4), channel_id=1, replica_groups=mesh['z'=16,'x'=4,'y'=4,'core'=2] {'y','core'}, use_global_device_ids=true, to_apply=%region_6.7 | all-reduce | flops 65 | bytes 520 | tf_op jit(solution)/shard_map/psum | solution.py:276
  29.9 1.9 %collective-permute-start.8 = (bf16[4,2,128,128]{3,2,1,0:T(8,128)(2,1)S(1)}, bf16[4,2,128,128]{3,2,1,0:T(8,128)(2,1)S(1)}, u32[]{:S(2)}, u32[]{:S(2)}) collective-permute-start(bf16[4,2,128,128]{3,2,1,0:T(8,128)(2,1)S(1)} %copy-done), channel_id=1, source_target_pairs={{0,6},{2,0},{4,2},{6,4},{1,7},{3,1},{5,3},{7,5},{8,14},{10,8},{12,... | collective-permute-start | bytes 786440 | tf_op jit(solution)/shard_map/ppermute | solution.py:28
  31.8 2.5 %collective-permute-start.7 = (bf16[4,2,128,128]{3,2,1,0:T(8,128)(2,1)S(1)}, bf16[4,2,128,128]{3,2,1,0:T(8,128)(2,1)S(1)}, u32[]{:S(2)}, u32[]{:S(2)}) collective-permute-start(bf16[4,2,128,128]{3,2,1,0:T(8,128)(2,1)S(1)} %copy-done), channel_id=1, source_target_pairs={{0,4},{2,6},{4,0},{6,2},{1,5},{3,7},{5,1},{7,3},{8,12},{10,14},{12... | collective-permute-start | bytes 786440 | tf_op jit(solution)/shard_map/ppermute | solution.py:28
  34.4 3.3 %collective-permute-start.6 = (bf16[4,2,128,128]{3,2,1,0:T(8,128)(2,1)S(1)}, bf16[4,2,128,128]{3,2,1,0:T(8,128)(2,1)S(1)}, u32[]{:S(2)}, u32[]{:S(2)}) collective-permute-start(bf16[4,2,128,128]{3,2,1,0:T(8,128)(2,1)S(1)} %copy-done), channel_id=1, source_target_pairs={{0,2},{2,4},{4,6},{6,0},{1,3},{3,5},{5,7},{7,1},{8,10},{10,12},{12... | collective-permute-start | bytes 786440 | tf_op jit(solution)/shard_map/ppermute | solution.py:28
  37.7 0.6 slice.73
  38.3 0.1 copy.90
  38.6 0.2 fusion.65
  39.1 0.1 and.386
  39.3 0.1 and.379
  39.4 0.2 select_reduce_fusion.1
  39.7 0.2 copy.100
  40.4 0.7 pad.21.clone
  41.2 0.2 fusion.46
  41.5 12.2 %all-gather.2 = f32[4,5,64]{2,1,0:T(8,128)S(1)} all-gather(f32[1,5,64]{2,1,0:T(8,128)S(1)} %maximum_bitcast_fusion), channel_id=2, replica_groups=mesh['z'=16,'x'=4,'y'=4,'core'=2] {'x'}, dimensions={0}, use_global_device_ids=true | all-gather | bytes 6400 | tf_op jit(solution)/shard_map/all_gather | solution.py:292
  53.6 37.6 %all-gather.1 = f32[64,5,64]{2,1,0:T(8,128)S(1)} all-gather(f32[4,5,64]{2,1,0:T(8,128)S(1)} %all-gather.2), channel_id=3, replica_groups=mesh['z'=16,'x'=4,'y'=4,'core'=2] {'z'}, dimensions={0}, use_global_device_ids=true | all-gather | bytes 87040 | tf_op jit(solution)/shard_map/all_gather | solution.py:293
  91.3 0.4 convert_reduce_fusion
  91.8 0.2 select_reduce_fusion.4.counts
  92.0 0.2 select_reduce_fusion.3
  92.4 0.7 slice_reduce_fusion
  93.1 0.7 slice_reduce_fusion.1
  94.0 0.2 fusion.2
  94.4 1.9 %collective-permute-start.9 = (bf16[32,128,128]{2,1,0:T(8,128)(2,1)S(1)}, bf16[32,128,128]{2,1,0:T(8,128)(2,1)S(1)}, u32[]{:S(2)}, u32[]{:S(2)}) collective-permute-start(bf16[32,128,128]{2,1,0:T(8,128)(2,1)S(1)} %bitcast.77), channel_id=1, source_target_pairs={{0,1},{1,0},{2,3},{3,2},{4,5},{5,4},{6,7},{7,6},{8,9},{9,8},{10,11... | collective-permute-start | bytes 3145736 | tf_op jit(solution)/shard_map/ppermute | solution.py:28
  97.3 0.1 add.445
  98.7 0.2 convert_reduce_fusion.2
  99.1 2.8 %select.166 = (bf16[12,128,128]{2,1,0:T(8,128)(2,1)}, bf16[12,128,128]{2,1,0:T(8,128)(2,1)}, bf16[12,128,128]{2,1,0:T(8,128)(2,1)}) custom-call(s32[96]{0:T(128)S(1)} %reshape.640.codes, s32[3]{0:T(128)S(1)} %select_reduce_fusion.4.counts, bf16[128,128,128]{2,1,0:T(8,128)(2,1)} %bitcast.74), custom_call_target="tpu_custom_call" | custom-call | tf_op jit(solution)/shard_map/select/pallas_call | solution.py:64
  101.8 3.0 %collective-permute-start.10 = (bf16[12,128,128]{2,1,0:T(8,128)(2,1)}, bf16[12,128,128]{2,1,0:T(8,128)(2,1)S(1)}, u32[]{:S(2)}, u32[]{:S(2)}) collective-permute-start(bf16[12,128,128]{2,1,0:T(8,128)(2,1)} %get-tuple-element.97), channel_id=1, source_target_pairs={{0,8},{8,16},{16,24},{24,0},{1,9},{9,17},{17,25},{25,1},{2,10},{10... | collective-permute-start | bytes 1179656 | tf_op jit(solution)/shard_map/ppermute | solution.py:28
  104.9 2.6 %collective-permute-start.11 = (bf16[12,128,128]{2,1,0:T(8,128)(2,1)}, bf16[12,128,128]{2,1,0:T(8,128)(2,1)}, u32[]{:S(2)}, u32[]{:S(2)}) collective-permute-start(bf16[12,128,128]{2,1,0:T(8,128)(2,1)} %get-tuple-element.98), channel_id=1, source_target_pairs={{0,16},{8,24},{16,0},{24,8},{1,17},{9,25},{17,1},{25,9},{2,18},{10... | collective-permute-start | bytes 1179656 | tf_op jit(solution)/shard_map/ppermute | solution.py:28
  107.5 3.1 %collective-permute-start.12 = (bf16[12,128,128]{2,1,0:T(8,128)(2,1)}, bf16[12,128,128]{2,1,0:T(8,128)(2,1)}, u32[]{:S(2)}, u32[]{:S(2)}) collective-permute-start(bf16[12,128,128]{2,1,0:T(8,128)(2,1)} %get-tuple-element.99), channel_id=1, source_target_pairs={{0,24},{8,0},{16,8},{24,16},{1,25},{9,1},{17,9},{25,17},{2,26},{10... | collective-permute-start | bytes 1179656 | tf_op jit(solution)/shard_map/ppermute | solution.py:28
  110.7 0.2 fusion.39
  110.9 5.1 %home.1 = f32[8,128,128]{2,1,0:T(8,128)S(1)} custom-call(s32[128]{0:T(128)S(1)} %slice_bitcast_fusion.2.items, s32[1]{0:T(128)S(1)} %bitcast.93, bf16[32,128,128]{2,1,0:T(8,128)(2,1)S(1)} %bitcast.78, bf16[32,128,128]{2,1,0:T(8,128)(2,1)S(1)} %collective-permute-done.9.left1, bf16[128,128,128]{2,1,0:T(8,128)(2,1)} %bitcast.75), custom_call_target="tpu_custom_call" | custom-call | flops 67108864 | bytes 1048576 | tf_op jit(solution)/shard_map/home/pallas_call | solution.py:160
  116.1 3.1 %fusion.10 = f32[4,80,640]{2,1,0:T(8,128)} fusion(f32[320]{0:T(512)S(1)} %get-tuple-element.102, f32[640]{0:T(1024)S(1)} %iota_convert_fusion, f32[320,80]{0,1:T(8,128)S(1)} %fusion.39, f32[320,4]{0,1:T(4,128)S(1)} %fusion.58), kind=kOutput, calls=%fused_computation.19 | convolution fusion | flops 789401600 | bytes 930560 | tf_op jit(solution)/shard_map/dot_general | solution.py:43
  119.2 1.4 collective-permute-done.11
  120.6 7.7 %collective-permute-done.12 = bf16[12,128,128]{2,1,0:T(8,128)(2,1)} collective-permute-done((bf16[12,128,128]{2,1,0:T(8,128)(2,1)}, bf16[12,128,128]{2,1,0:T(8,128)(2,1)}, u32[]{:S(2)}, u32[]{:S(2)}) %collective-permute-start.12) | collective-permute-done | bytes 393248 | tf_op jit(solution)/shard_map/ppermute | solution.py:28
  128.3 7.9 %conditional.1 = (f32[4,2,128,128]{3,2,1,0:T(8,128)}) conditional(s32[]{:T(128)} %convert_element_type.105, (s32[2,128]{1,0:T(2,128)S(1)}, s32[2]{0:T(128)S(1)}, f32[1]{0:T(128)}, bf16[32,128,128]{2,1,0:T(8,128)(2,1)S(1)}, bf16[32,128,128]{2,1,0:T(8,128)(2,1)S(1)}, /*index=5*/bf16[12,128,128]{2,1,0:T(8,128)(2,1)S(1)}, ...), branch_computations={%region_18.19_spmd, %region_19.20_spmd} | conditional | flops 70647808 | bytes 17564928 | solution.py:331
  128.3 0.6 slice.47.count
  128.9 7.3 %away.2 = f32[8,128,128]{2,1,0:T(8,128)} custom-call(s32[128]{0:T(128)S(1)} %slice_bitcast_fusion.items, s32[1]{0:T(128)} %slice.47.count, f32[1]{0:T(128)} %get-tuple-element.52.scale, bf16[32,128,128]{2,1,0:T(8,128)(2,1)S(1)} %get-tuple-element.53.left0, bf16[32,128,128]{2,1,0:T(8,128)(2,1)S(1)} %get-tuple-element.54.left1, ...), custom_call_target="tpu_custom_call" | custom-call | flops 67108864 | bytes 1048576 | tf_op jit(solution)/shard_map/cond/branch_0_fun/away/pallas_call | solution.py:166
  (93 shorter events, 4.6 us)
Async XLA Ops:
  7.2 7.4 %copy-start = (bf16[4,2,128,128]{3,2,1,0:T(8,128)(2,1)S(1)}, bf16[4,2,128,128]{3,2,1,0:T(8,128)(2,1)}, u32[]{:S(2)}) copy-start(bf16[4,2,128,128]{3,2,1,0:T(8,128)(2,1)} %param.8) | copy-start | bytes 786436
  7.2 30.5 %copy-start.1 = (f32[3,64]{1,0:T(4,128)S(1)}, f32[3,64]{1,0:T(4,128)}, u32[]{:S(2)}) copy-start(f32[3,64]{1,0:T(4,128)} %param.11) | copy-start | bytes 2308
  7.2 34.0 %copy-start.2 = (s32[64]{0:T(128)S(1)}, s32[64]{0:T(128)}, u32[]{:S(2)}) copy-start(s32[64]{0:T(128)} %param.9) | copy-start | bytes 772
  7.2 34.2 %copy-start.3 = (s32[64]{0:T(128)S(1)}, s32[64]{0:T(128)}, u32[]{:S(2)}) copy-start(s32[64]{0:T(128)} %param.10) | copy-start | bytes 772
  7.2 91.9 %all-gather.5.cloned.1.call-start = ((), (), s32[]{:S(2)}) async-start(), calls=%async_computation | async-start | bytes 4456448 | tf_op jit(solution)/shard_map/all_gather | solution.py:260
  29.9 64.3 %collective-permute-start.8 = (bf16[4,2,128,128]{3,2,1,0:T(8,128)(2,1)S(1)}, bf16[4,2,128,128]{3,2,1,0:T(8,128)(2,1)S(1)}, u32[]{:S(2)}, u32[]{:S(2)}) collective-permute-start(bf16[4,2,128,128]{3,2,1,0:T(8,128)(2,1)S(1)} %copy-done), channel_id=1, source_target_pairs={{0,6},{2,0},{4,2},{6,4},{1,7},{3,1},{5,3},{7,5},{8,14},{10,8},{12,... | collective-permute-start | bytes 786440 | tf_op jit(solution)/shard_map/ppermute | solution.py:28
  31.8 62.4 %collective-permute-start.7 = (bf16[4,2,128,128]{3,2,1,0:T(8,128)(2,1)S(1)}, bf16[4,2,128,128]{3,2,1,0:T(8,128)(2,1)S(1)}, u32[]{:S(2)}, u32[]{:S(2)}) collective-permute-start(bf16[4,2,128,128]{3,2,1,0:T(8,128)(2,1)S(1)} %copy-done), channel_id=1, source_target_pairs={{0,4},{2,6},{4,0},{6,2},{1,5},{3,7},{5,1},{7,3},{8,12},{10,14},{12... | collective-permute-start | bytes 786440 | tf_op jit(solution)/shard_map/ppermute | solution.py:28
  34.4 59.9 %collective-permute-start.6 = (bf16[4,2,128,128]{3,2,1,0:T(8,128)(2,1)S(1)}, bf16[4,2,128,128]{3,2,1,0:T(8,128)(2,1)S(1)}, u32[]{:S(2)}, u32[]{:S(2)}) collective-permute-start(bf16[4,2,128,128]{3,2,1,0:T(8,128)(2,1)S(1)} %copy-done), channel_id=1, source_target_pairs={{0,2},{2,4},{4,6},{6,0},{1,3},{3,5},{5,7},{7,1},{8,10},{10,12},{12... | collective-permute-start | bytes 786440 | tf_op jit(solution)/shard_map/ppermute | solution.py:28
  94.4 16.5 %collective-permute-start.9 = (bf16[32,128,128]{2,1,0:T(8,128)(2,1)S(1)}, bf16[32,128,128]{2,1,0:T(8,128)(2,1)S(1)}, u32[]{:S(2)}, u32[]{:S(2)}) collective-permute-start(bf16[32,128,128]{2,1,0:T(8,128)(2,1)S(1)} %bitcast.77), channel_id=1, source_target_pairs={{0,1},{1,0},{2,3},{3,2},{4,5},{5,4},{6,7},{7,6},{8,9},{9,8},{10,11... | collective-permute-start | bytes 3145736 | tf_op jit(solution)/shard_map/ppermute | solution.py:28
  101.8 17.3 %collective-permute-start.10 = (bf16[12,128,128]{2,1,0:T(8,128)(2,1)}, bf16[12,128,128]{2,1,0:T(8,128)(2,1)S(1)}, u32[]{:S(2)}, u32[]{:S(2)}) collective-permute-start(bf16[12,128,128]{2,1,0:T(8,128)(2,1)} %get-tuple-element.97), channel_id=1, source_target_pairs={{0,8},{8,16},{16,24},{24,0},{1,9},{9,17},{17,25},{25,1},{2,10},{10... | collective-permute-start | bytes 1179656 | tf_op jit(solution)/shard_map/ppermute | solution.py:28
  104.9 15.7 %collective-permute-start.11 = (bf16[12,128,128]{2,1,0:T(8,128)(2,1)}, bf16[12,128,128]{2,1,0:T(8,128)(2,1)}, u32[]{:S(2)}, u32[]{:S(2)}) collective-permute-start(bf16[12,128,128]{2,1,0:T(8,128)(2,1)} %get-tuple-element.98), channel_id=1, source_target_pairs={{0,16},{8,24},{16,0},{24,8},{1,17},{9,25},{17,1},{25,9},{2,18},{10... | collective-permute-start | bytes 1179656 | tf_op jit(solution)/shard_map/ppermute | solution.py:28
  107.5 20.8 %collective-permute-start.12 = (bf16[12,128,128]{2,1,0:T(8,128)(2,1)}, bf16[12,128,128]{2,1,0:T(8,128)(2,1)}, u32[]{:S(2)}, u32[]{:S(2)}) collective-permute-start(bf16[12,128,128]{2,1,0:T(8,128)(2,1)} %get-tuple-element.99), channel_id=1, source_target_pairs={{0,24},{8,0},{16,8},{24,16},{1,25},{9,1},{17,9},{25,17},{2,26},{10... | collective-permute-start | bytes 1179656 | tf_op jit(solution)/shard_map/ppermute | solution.py:28
Sparse Core Ops, SparseCore 0:
  10.1 83.9 all-gather.4

commit v3 on v2

--- a/solution.py
+++ b/solution.py
@@ -16,6 +16,8 @@
 CAP = 12
 FULL = NZ * KC
 ITEMS = BR * SLOTS * KC
+GROUP = 4
+SUMS = BR * KC + 1
 ROW = ("z", "x")
 COL = ("y", "core")
 
@@ -26,6 +28,12 @@
 def shift(value, axis, steps):
     count = lax.axis_size(axis)
     return lax.ppermute(value, axis, [(s, (s + steps) % count) for s in range(count)])
+
+
+def everyone(value, axis):
+    count = lax.axis_size(axis)
+    spread = jnp.broadcast_to(value[None], (count, *value.shape))
+    return lax.all_to_all(spread, axis, split_axis=0, concat_axis=0, tiled=True)
 
 
 def window(delta, length):
@@ -75,7 +83,7 @@
     )(codes, counts, held)
 
 
-def run_items(items, total, lefts, rights, out, left_buf, right_buf, left_sem, right_sem):
+def run_items(items, total, lefts, rights, sums, left_buf, right_buf, left_sem, right_sem):
     def begin(n, _):
         code = items[n]
         left = lax.rem(code, 128)
@@ -98,35 +106,49 @@
                     rights[g].at[place], right_buf.at[n], right_sem.at[n]
                 ).start()
 
-    def multiply(n, _):
-        pltpu.make_async_copy(lefts[0].at[0], left_buf.at[n], left_sem.at[n]).wait()
-        pltpu.make_async_copy(rights[0].at[0], right_buf.at[n], right_sem.at[n]).wait()
-        target = lax.rem(lax.div(items[n], 128), 8)
-        out[target] += jnp.dot(
-            left_buf[n], right_buf[n], preferred_element_type=jnp.float32
-        )
+    def multiply(q, _):
+        places = [q * GROUP + k for k in range(GROUP)]
+        for n in places:
+
+            @pl.when(n < total)
+            def _():
+                pltpu.make_async_copy(
+                    lefts[0].at[0], left_buf.at[n], left_sem.at[n]
+                ).wait()
+                pltpu.make_async_copy(
+                    rights[0].at[0], right_buf.at[n], right_sem.at[n]
+                ).wait()
+
+        terms = [
+            jnp.dot(left_buf[n], right_buf[n], preferred_element_type=jnp.float32)
+            for n in places
+        ]
+        for n, term in zip(places, terms):
+            target = lax.rem(lax.div(items[n], 128), 8)
+            sums[jnp.where(n < total, target, BR * KC)] += term
 
     lax.fori_loop(0, total, begin, None)
     yield
-    lax.fori_loop(0, total, multiply, None)
-
-
-def home_kernel(items, count, left0, left1, held, out, *scratch):
-    steps = run_items(items, count[0], (left0, left1), (held,), out, *scratch)
+    lax.fori_loop(0, lax.div(total + GROUP - 1, GROUP), multiply, None)
+
+
+def home_kernel(items, count, left0, left1, held, sums, *scratch):
+    steps = run_items(items, count[0], (left0, left1), (held,), sums, *scratch)
     next(steps)
-    out[...] = jnp.zeros_like(out)
+    sums[...] = jnp.zeros_like(sums)
     next(steps, None)
 
 
 def away_kernel(items, count, scale, left0, left1, *rest):
     rights, begun, mine, out = rest[: NX - 1], rest[NX - 1], rest[NX], rest[NX + 1]
-    steps = run_items(items, count[0], (left0, left1), rights, out, *rest[NX + 2 :])
+    *scratch, sums = rest[NX + 2 :]
+    steps = run_items(items, count[0], (left0, left1), rights, sums, *scratch)
     next(steps)
-    out[...] = begun[...]
+    sums[...] = begun[...]
     next(steps, None)
     twice = scale[0]
     for o in range(BR * KC):
-        value = out[o]
+        value = sums[o]
         out[o] = value + twice * (mine[o].astype(jnp.float32) - value)
 
 
@@ -135,10 +157,10 @@
 VMEM = pl.BlockSpec(memory_space=pltpu.VMEM)
 
 
-def items_call(kernel, name, in_specs):
+def items_call(kernel, name, in_specs, size, more):
     return pl.pallas_call(
         kernel,
-        out_shape=jax.ShapeDtypeStruct((BR * KC, BS, BS), jnp.float32),
+        out_shape=jax.ShapeDtypeStruct((size, BS, BS), jnp.float32),
         in_specs=in_specs,
         out_specs=VMEM,
         scratch_shapes=[
@@ -146,6 +168,7 @@
             pltpu.VMEM((ITEMS, BS, BS), jnp.bfloat16),
             pltpu.SemaphoreType.DMA((ITEMS,)),
             pltpu.SemaphoreType.DMA((ITEMS,)),
+            *more,
         ],
         compiler_params=pltpu.CompilerParams(vmem_limit_bytes=24 * 1024 * 1024),
         cost_estimate=pl.CostEstimate(
@@ -156,13 +179,14 @@
 
 
 def home_products(items, count, lefts, held):
-    call = items_call(home_kernel, "home", [SMEM] * 2 + [ANYWHERE] * 3)
+    call = items_call(home_kernel, "home", [SMEM] * 2 + [ANYWHERE] * 3, SUMS, [])
     return call(items, count, *lefts, held)
 
 
 def away_products(items, count, scale, lefts, rights, begun, mine):
     specs = [SMEM] * 3 + [ANYWHERE] * (NX + 1) + [VMEM] * 2
-    call = items_call(away_kernel, "away", specs)
+    sums = pltpu.VMEM((SUMS, BS, BS), jnp.float32)
+    call = items_call(away_kernel, "away", specs, BR * KC, [sums])
     return call(items, count, scale, *lefts, *rights, begun, mine)
 
 
@@ -273,7 +297,7 @@
     ).astype(jnp.float32)
     set_part = jnp.dot(own_diag, gather_sets, precision=lax.Precision.HIGHEST)
     packed = jnp.concatenate([set_part.reshape(-1), over.astype(jnp.float32)[None]])
-    packed = lax.psum(packed, COL)
+    packed = jnp.sum(everyone(packed[None], COL), axis=0)[0]
     blocks, packed = lax.optimization_barrier((matrix, packed))
     lefts = jnp.concatenate([blocks] + [shift(blocks, "y", d) for d in range(1, NY)])
     lefts = lefts.reshape(NY * BR * KC, BS, BS)
@@ -289,9 +313,7 @@
     start_x = atom_slab.astype(jnp.float32) * PLANES + atom_offset[0]
     flag = jnp.broadcast_to(packed[BR * sets], charge.shape)
     packed = jnp.stack([charge, start_x, atom_offset[1], atom_offset[2], flag])
-    packed = lax.all_gather(packed, "x", axis=0, tiled=False)
-    packed = lax.all_gather(packed, "z", axis=0, tiled=False)
-    packed = packed.reshape(NZ * NX, 5, atoms_here)
+    packed = everyone(packed, ROW)
     over = jnp.sum(packed[:, 4, 0])
     trace = jnp.sum(packed[:, 0])
     weight = jax.nn.sigmoid(sharpness * (half_fill - trace / (NB * BS)))
@@ -302,8 +324,10 @@
 
     mine = matrix.reshape(BR * KC, BS, BS)
     outgoing = select(sends, send_counts, held, 0)
-    items, near, outgoing = lax.optimization_barrier((items, near, outgoing))
-    first = [shift(outgoing[d - 1], "x", d) for d in range(1, NX)]
+    first = [None] * (NX - 1)
+    for d in (2, 3, 1):
+        items, outgoing = lax.optimization_barrier((items, outgoing))
+        first[d - 1] = shift(outgoing[d - 1], "x", d)
     begun = home_products(items[0], totals[:1], lefts, held)
 
     x_cells = (row * PLANES + jnp.arange(PLANES, dtype=jnp.int32)).astype(jnp.float32)

time: 145 us -> 134 us (0.924)
  blocking collectives: 64.6 us -> 0 us
  waiting for transfers between devices: 9.86 us -> 35.8 us
  starting transfers between devices: 18.5 us -> 44.2 us
  local copies, waits for them, and re-layouts: 6.24 us -> 8.48 us
    all_gather x2 -> x0, blocking collectives: 49.7 us -> none  [the longest x1 37.6 us: shards(): packed = lax.all_gather(packed, 'z', axis=0, tiled=False)]
    all_to_all x0 -> x2, starting transfers between devices: none -> 23 us  [everyone(): return lax.all_to_all(spread, axis, split_axis=0, concat_axis=0, tiled=True)]
    all_gather x1, waiting for transfers between devices: 0.02 us -> 20.1 us  [shards(): held = lax.all_gather(matrix, 'z', axis=0, tiled=True)]
    psum x1 -> x0, blocking collectives: 14.8 us -> none  [shards(): packed = lax.psum(packed, COL)]
    all_to_all x0 -> x2, waiting for transfers between devices: none -> 13.2 us  [everyone(): return lax.all_to_all(spread, axis, split_axis=0, concat_axis=0, tiled=True)]
    ppermute x7, waiting for transfers between devices: 9.15 us -> 1.92 us  [shift(): lax.ppermute(value, axis, [(s, (s + steps) % count) for s in range(count)])]
    ppermute x7, starting transfers between devices: 18.4 us -> 21.1 us  [shift(): lax.ppermute(value, axis, [(s, (s + steps) % count) for s in range(count)])]
  transfers between devices with their start and end apart: 8 -> 10, of which waited for: 2 -> 4; matrix products, arithmetic and copies ran while one was open for 12% -> 16% of each run, Pallas kernels for 5% -> 5%
where the time goes in v3:
time: 134 us; the launch traced here: 132 us
  starting transfers between devices  44.2 us (33%)
  waiting for transfers between devices  35.8 us (27%)
  between operations  16.6 us (12%)
  Pallas kernels  13.9 us (10%)
  local copies, waits for them, and re-layouts  8.48 us (6%)
  other arithmetic  8.46 us (6%)
  matrix products  4.64 us (3%)
    all_to_all x2, starting transfers between devices, everyone(): return lax.all_to_all(spread, axis, split_axis=0, concat_axis=0, tiled=True)  23 us
    ppermute x7, starting transfers between devices, shift(): lax.ppermute(value, axis, [(s, (s + steps) % count) for s in range(count)])  21.1 us
    all_gather x1, waiting for transfers between devices, shards(): held = lax.all_gather(matrix, 'z', axis=0, tiled=True)  20.1 us
    all_to_all x2, waiting for transfers between devices, everyone(): return lax.all_to_all(spread, axis, split_axis=0, concat_axis=0, tiled=True)  13.2 us
    pallas_call x1, Pallas kernels, away_products(): return call(items, count, scale, *lefts, *rights, begun, mine)  6.84 us
    pallas_call x1, Pallas kernels, home_products(): return call(items, count, *lefts, held)  4.39 us
    dot_general x1, matrix products, collocate(): dense = jnp.dot(plane.T, along_z, precision=lax.Precision.HIGHEST)  3.13 us
    pallas_call x1, Pallas kernels, select(): pl.pallas_call(functools.partial(select_kernel, base), out_shape=[block]...  2.69 us
  transfers between devices with their start and end apart: 10, of which 4 were waited for; matrix products, arithmetic and copies ran while one was open for 16% of the time, Pallas kernels for 5%

profile of v3, /device:TPU:6, one launch (start us, length us, event | category | flops | bytes accessed | tf_op | source)
XLA Modules:
  0.0 132.1 jit_solution(358292419754701406)
XLA Ops:
  7.2 0.7 all-gather.2.cloned.1.call-update
  8.0 0.8 broadcast_compare_fusion
  9.1 0.9 convolution_convert_fusion
  10.0 0.2 copy.135
  10.2 0.8 broadcast_compare_fusion.2
  11.0 0.2 fusion.94
  11.5 0.2 fusion.31
  12.1 0.2 convert_reduce_fusion.3
  12.3 0.6 convert_reduce_fusion.4
  13.6 0.8 dynamic-slice_compare_fusion
  14.6 0.2 select_reduce_fusion
  14.7 0.2 fusion.44
  15.1 0.6 broadcast_in_dim.55
  15.7 4.4 %all-to-all-start = ((f32[8,1,65]{2,1,0:T(1,128)}), f32[8,1,65]{2,1,0:T(1,128)S(1)}, u32[]{:S(2)}, u32[]{:S(2)}) async-start(f32[8,1,65]{2,1,0:T(1,128)} %broadcast_in_dim.55), calls=%async_computation | async-start | bytes 8192 | tf_op jit(solution)/shard_map/all_to_all | solution.py:36
  20.4 0.2 fusion.65
  20.6 0.4 convert_reduce_fusion
  21.3 0.2 fusion.2
  21.6 0.2 mul.245
  23.4 0.2 copy.136
  24.1 0.2 select_reduce_fusion.4.counts
  24.7 0.2 convert_reduce_fusion.2
  25.1 0.2 all-to-all-done
  25.4 4.9 %collective-permute-start.8 = (bf16[4,2,128,128]{3,2,1,0:T(8,128)(2,1)S(1)}, bf16[4,2,128,128]{3,2,1,0:T(8,128)(2,1)S(1)}, u32[]{:S(2)}, u32[]{:S(2)}) collective-permute-start(bf16[4,2,128,128]{3,2,1,0:T(8,128)(2,1)S(1)} %copy-done), channel_id=1, source_target_pairs={{0,6},{2,0},{4,2},{6,4},{1,7},{3,1},{5,3},{7,5},{8,14},{10,8},{12,... | collective-permute-start | bytes 786440 | tf_op jit(solution)/shard_map/ppermute | solution.py:30
  30.3 2.8 %collective-permute-start.7 = (bf16[4,2,128,128]{3,2,1,0:T(8,128)(2,1)S(1)}, bf16[4,2,128,128]{3,2,1,0:T(8,128)(2,1)S(1)}, u32[]{:S(2)}, u32[]{:S(2)}) collective-permute-start(bf16[4,2,128,128]{3,2,1,0:T(8,128)(2,1)S(1)} %copy-done), channel_id=1, source_target_pairs={{0,4},{2,6},{4,0},{6,2},{1,5},{3,7},{5,1},{7,3},{8,12},{10,14},{12... | collective-permute-start | bytes 786440 | tf_op jit(solution)/shard_map/ppermute | solution.py:30
  33.1 2.8 %collective-permute-start.6 = (bf16[4,2,128,128]{3,2,1,0:T(8,128)(2,1)S(1)}, bf16[4,2,128,128]{3,2,1,0:T(8,128)(2,1)S(1)}, u32[]{:S(2)}, u32[]{:S(2)}) collective-permute-start(bf16[4,2,128,128]{3,2,1,0:T(8,128)(2,1)S(1)} %copy-done), channel_id=1, source_target_pairs={{0,2},{2,4},{4,6},{6,0},{1,3},{3,5},{5,7},{7,1},{8,10},{10,12},{12... | collective-permute-start | bytes 786440 | tf_op jit(solution)/shard_map/ppermute | solution.py:30
  35.8 0.6 slice.77
  36.4 0.7 pad.21.clone
  37.1 0.2 fusion.46
  37.5 0.8 reshape.674
  38.2 18.6 %all-to-all-start.1 = ((f32[64,1,320]{2,1,0:T(1,128)}), f32[64,1,320]{2,1,0:T(1,128)S(1)}, u32[]{:S(2)}, u32[]{:S(2)}) async-start(f32[64,1,320]{2,1,0:T(1,128)} %reshape.674), calls=%async_computation.1 | async-start | bytes 196608 | tf_op jit(solution)/shard_map/all_to_all | solution.py:36
  57.1 1.9 %collective-permute-start.9 = (bf16[32,128,128]{2,1,0:T(8,128)(2,1)S(1)}, bf16[32,128,128]{2,1,0:T(8,128)(2,1)S(1)}, u32[]{:S(2)}, u32[]{:S(2)}) collective-permute-start(bf16[32,128,128]{2,1,0:T(8,128)(2,1)S(1)} %bitcast.77), channel_id=1, source_target_pairs={{0,1},{1,0},{2,3},{3,2},{4,5},{5,4},{6,7},{7,6},{8,9},{9,8},{10,11... | collective-permute-start | bytes 3145736 | tf_op jit(solution)/shard_map/ppermute | solution.py:30
  59.0 13.0 %all-to-all-done.1 = f32[64,1,320]{2,1,0:T(1,128)S(1)} async-done(((f32[64,1,320]{2,1,0:T(1,128)}), f32[64,1,320]{2,1,0:T(1,128)S(1)}, u32[]{:S(2)}, u32[]{:S(2)}) %all-to-all-start.1) | async-done | bytes 81952 | tf_op jit(solution)/shard_map/all_to_all | solution.py:36
  72.0 0.5 broadcast.963
  72.5 0.9 reduce.23
  73.5 0.7 slice_reduce_fusion
  74.9 0.6 reduce_sum.129
  76.7 0.2 fusion.39
  76.8 20.1 %all-gather.2.cloned.1.call-done = bf16[64,2,128,128]{3,2,1,0:T(8,128)(2,1)} async-done(((bf16[4,2,128,128]{3,2,1,0:T(8,128)(2,1)}), bf16[64,2,128,128]{3,2,1,0:T(8,128)(2,1)}) %all-gather.2.cloned.1.call-update) | async-done | bytes 4194320 | tf_op jit(solution)/shard_map/all_gather | solution.py:284
  96.9 2.7 %select.166 = (bf16[12,128,128]{2,1,0:T(8,128)(2,1)}, bf16[12,128,128]{2,1,0:T(8,128)(2,1)}, bf16[12,128,128]{2,1,0:T(8,128)(2,1)}) custom-call(s32[96]{0:T(128)S(1)} %reshape.647.codes, s32[3]{0:T(128)S(1)} %select_reduce_fusion.4.counts, bf16[128,128,128]{2,1,0:T(8,128)(2,1)} %bitcast.74), custom_call_target="tpu_custom_call" | custom-call | tf_op jit(solution)/shard_map/select/pallas_call | solution.py:72
  99.6 2.5 %collective-permute-start.10 = (bf16[12,128,128]{2,1,0:T(8,128)(2,1)}, bf16[12,128,128]{2,1,0:T(8,128)(2,1)S(1)}, u32[]{:S(2)}, u32[]{:S(2)}) collective-permute-start(bf16[12,128,128]{2,1,0:T(8,128)(2,1)} %get-tuple-element.111), channel_id=1, source_target_pairs={{0,8},{8,16},{16,24},{24,0},{1,9},{9,17},{17,25},{25,1},{2,10},{10... | collective-permute-start | bytes 1179656 | tf_op jit(solution)/shard_map/ppermute | solution.py:30
  102.1 4.3 %collective-permute-start.11 = (bf16[12,128,128]{2,1,0:T(8,128)(2,1)}, bf16[12,128,128]{2,1,0:T(8,128)(2,1)}, u32[]{:S(2)}, u32[]{:S(2)}) collective-permute-start(bf16[12,128,128]{2,1,0:T(8,128)(2,1)} %get-tuple-element.112), channel_id=1, source_target_pairs={{0,16},{8,24},{16,0},{24,8},{1,17},{9,25},{17,1},{25,9},{2,18},{10... | collective-permute-start | bytes 1179656 | tf_op jit(solution)/shard_map/ppermute | solution.py:30
  106.5 1.9 %collective-permute-start.12 = (bf16[12,128,128]{2,1,0:T(8,128)(2,1)}, bf16[12,128,128]{2,1,0:T(8,128)(2,1)}, u32[]{:S(2)}, u32[]{:S(2)}) collective-permute-start(bf16[12,128,128]{2,1,0:T(8,128)(2,1)} %get-tuple-element.113), channel_id=1, source_target_pairs={{0,24},{8,0},{16,8},{24,16},{1,25},{9,1},{17,9},{25,17},{2,26},{10... | collective-permute-start | bytes 1179656 | tf_op jit(solution)/shard_map/ppermute | solution.py:30
  108.4 3.1 %fusion.10 = f32[4,80,640]{2,1,0:T(8,128)} fusion(f32[320]{0:T(512)S(1)} %sub.195, f32[640]{0:T(1024)S(1)} %iota_convert_fusion, f32[320,80]{0,1:T(8,128)S(1)} %fusion.39, f32[320,4]{0,1:T(4,128)S(1)} %fusion.58), kind=kOutput, calls=%fused_computation.19 | convolution fusion | flops 789401600 | bytes 930560 | tf_op jit(solution)/shard_map/dot_general | solution.py:51
  111.5 4.4 %home.1 = f32[9,128,128]{2,1,0:T(8,128)S(1)} custom-call(s32[128]{0:T(128)S(1)} %slice_bitcast_fusion.2.items, s32[1]{0:T(128)S(1)} %bitcast.95, bf16[32,128,128]{2,1,0:T(8,128)(2,1)S(1)} %bitcast.78, bf16[32,128,128]{2,1,0:T(8,128)(2,1)S(1)} %collective-permute-done.9.left1, bf16[128,128,128]{2,1,0:T(8,128)(2,1)} %bitcast.75), custom_call_target="tpu_custom_call" | custom-call | flops 67108864 | bytes 1048576 | tf_op jit(solution)/shard_map/home/pallas_call | solution.py:183
  115.9 1.9 %collective-permute-done.12 = bf16[12,128,128]{2,1,0:T(8,128)(2,1)} collective-permute-done((bf16[12,128,128]{2,1,0:T(8,128)(2,1)}, bf16[12,128,128]{2,1,0:T(8,128)(2,1)}, u32[]{:S(2)}, u32[]{:S(2)}) %collective-permute-start.12) | collective-permute-done | bytes 393248 | tf_op jit(solution)/shard_map/ppermute | solution.py:30
  117.8 7.4 %conditional.1 = (f32[4,2,128,128]{3,2,1,0:T(8,128)}) conditional(s32[]{:T(128)} %convert_element_type.105, (s32[2,128]{1,0:T(2,128)S(1)}, s32[2]{0:T(128)S(1)}, f32[1]{0:T(128)}, bf16[32,128,128]{2,1,0:T(8,128)(2,1)S(1)}, bf16[32,128,128]{2,1,0:T(8,128)(2,1)S(1)}, /*index=5*/bf16[12,128,128]{2,1,0:T(8,128)(2,1)S(1)}, ...), branch_computations={%region_18.19_spmd, %region_19.20_spmd} | conditional | flops 70647808 | bytes 17564928 | solution.py:355
  117.8 0.6 slice.51.count
  118.4 6.8 %away.2 = f32[8,128,128]{2,1,0:T(8,128)} custom-call(s32[128]{0:T(128)S(1)} %slice_bitcast_fusion.items, s32[1]{0:T(128)} %slice.51.count, f32[1]{0:T(128)} %get-tuple-element.57.scale, bf16[32,128,128]{2,1,0:T(8,128)(2,1)S(1)} %get-tuple-element.58.left0, bf16[32,128,128]{2,1,0:T(8,128)(2,1)S(1)} %get-tuple-element.59.left1, ...), custom_call_target="tpu_custom_call" | custom-call | flops 67108864 | bytes 1048576 | tf_op jit(solution)/shard_map/cond/branch_0_fun/away/pallas_call | solution.py:190
  (104 shorter events, 5.7 us)
Async XLA Ops:
  7.2 7.4 %copy-start = (bf16[4,2,128,128]{3,2,1,0:T(8,128)(2,1)S(1)}, bf16[4,2,128,128]{3,2,1,0:T(8,128)(2,1)}, u32[]{:S(2)}) copy-start(bf16[4,2,128,128]{3,2,1,0:T(8,128)(2,1)} %param.8) | copy-start | bytes 786436
  7.2 17.8 %copy-start.2 = (s32[64]{0:T(128)S(1)}, s32[64]{0:T(128)}, u32[]{:S(2)}) copy-start(s32[64]{0:T(128)} %param.9) | copy-start | bytes 772
  7.2 17.8 %copy-start.1 = (f32[3,64]{1,0:T(4,128)S(1)}, f32[3,64]{1,0:T(4,128)}, u32[]{:S(2)}) copy-start(f32[3,64]{1,0:T(4,128)} %param.11) | copy-start | bytes 2308
  7.2 17.8 %copy-start.3 = (s32[64]{0:T(128)S(1)}, s32[64]{0:T(128)}, u32[]{:S(2)}) copy-start(s32[64]{0:T(128)} %param.10) | copy-start | bytes 772
  7.2 89.7 %all-gather.2.cloned.1.call-start = ((), (), s32[]{:S(2)}) async-start(), calls=%async_computation.2 | async-start | bytes 4456448 | tf_op jit(solution)/shard_map/all_gather | solution.py:284
  15.7 9.6 %all-to-all-start = ((f32[8,1,65]{2,1,0:T(1,128)}), f32[8,1,65]{2,1,0:T(1,128)S(1)}, u32[]{:S(2)}, u32[]{:S(2)}) async-start(f32[8,1,65]{2,1,0:T(1,128)} %broadcast_in_dim.55), calls=%async_computation | async-start | bytes 8192 | tf_op jit(solution)/shard_map/all_to_all | solution.py:36
  25.4 31.6 %collective-permute-start.8 = (bf16[4,2,128,128]{3,2,1,0:T(8,128)(2,1)S(1)}, bf16[4,2,128,128]{3,2,1,0:T(8,128)(2,1)S(1)}, u32[]{:S(2)}, u32[]{:S(2)}) collective-permute-start(bf16[4,2,128,128]{3,2,1,0:T(8,128)(2,1)S(1)} %copy-done), channel_id=1, source_target_pairs={{0,6},{2,0},{4,2},{6,4},{1,7},{3,1},{5,3},{7,5},{8,14},{10,8},{12,... | collective-permute-start | bytes 786440 | tf_op jit(solution)/shard_map/ppermute | solution.py:30
  30.3 26.7 %collective-permute-start.7 = (bf16[4,2,128,128]{3,2,1,0:T(8,128)(2,1)S(1)}, bf16[4,2,128,128]{3,2,1,0:T(8,128)(2,1)S(1)}, u32[]{:S(2)}, u32[]{:S(2)}) collective-permute-start(bf16[4,2,128,128]{3,2,1,0:T(8,128)(2,1)S(1)} %copy-done), channel_id=1, source_target_pairs={{0,4},{2,6},{4,0},{6,2},{1,5},{3,7},{5,1},{7,3},{8,12},{10,14},{12... | collective-permute-start | bytes 786440 | tf_op jit(solution)/shard_map/ppermute | solution.py:30
  33.1 23.9 %collective-permute-start.6 = (bf16[4,2,128,128]{3,2,1,0:T(8,128)(2,1)S(1)}, bf16[4,2,128,128]{3,2,1,0:T(8,128)(2,1)S(1)}, u32[]{:S(2)}, u32[]{:S(2)}) collective-permute-start(bf16[4,2,128,128]{3,2,1,0:T(8,128)(2,1)S(1)} %copy-done), channel_id=1, source_target_pairs={{0,2},{2,4},{4,6},{6,0},{1,3},{3,5},{5,7},{7,1},{8,10},{10,12},{12... | collective-permute-start | bytes 786440 | tf_op jit(solution)/shard_map/ppermute | solution.py:30
  38.2 33.8 %all-to-all-start.1 = ((f32[64,1,320]{2,1,0:T(1,128)}), f32[64,1,320]{2,1,0:T(1,128)S(1)}, u32[]{:S(2)}, u32[]{:S(2)}) async-start(f32[64,1,320]{2,1,0:T(1,128)} %reshape.674), calls=%async_computation.1 | async-start | bytes 196608 | tf_op jit(solution)/shard_map/all_to_all | solution.py:36
  57.1 54.4 %collective-permute-start.9 = (bf16[32,128,128]{2,1,0:T(8,128)(2,1)S(1)}, bf16[32,128,128]{2,1,0:T(8,128)(2,1)S(1)}, u32[]{:S(2)}, u32[]{:S(2)}) collective-permute-start(bf16[32,128,128]{2,1,0:T(8,128)(2,1)S(1)} %bitcast.77), channel_id=1, source_target_pairs={{0,1},{1,0},{2,3},{3,2},{4,5},{5,4},{6,7},{7,6},{8,9},{9,8},{10,11... | collective-permute-start | bytes 3145736 | tf_op jit(solution)/shard_map/ppermute | solution.py:30
  99.6 16.3 %collective-permute-start.10 = (bf16[12,128,128]{2,1,0:T(8,128)(2,1)}, bf16[12,128,128]{2,1,0:T(8,128)(2,1)S(1)}, u32[]{:S(2)}, u32[]{:S(2)}) collective-permute-start(bf16[12,128,128]{2,1,0:T(8,128)(2,1)} %get-tuple-element.111), channel_id=1, source_target_pairs={{0,8},{8,16},{16,24},{24,0},{1,9},{9,17},{17,25},{25,1},{2,10},{10... | collective-permute-start | bytes 1179656 | tf_op jit(solution)/shard_map/ppermute | solution.py:30
  102.1 13.8 %collective-permute-start.11 = (bf16[12,128,128]{2,1,0:T(8,128)(2,1)}, bf16[12,128,128]{2,1,0:T(8,128)(2,1)}, u32[]{:S(2)}, u32[]{:S(2)}) collective-permute-start(bf16[12,128,128]{2,1,0:T(8,128)(2,1)} %get-tuple-element.112), channel_id=1, source_target_pairs={{0,16},{8,24},{16,0},{24,8},{1,17},{9,25},{17,1},{25,9},{2,18},{10... | collective-permute-start | bytes 1179656 | tf_op jit(solution)/shard_map/ppermute | solution.py:30
  106.5 11.4 %collective-permute-start.12 = (bf16[12,128,128]{2,1,0:T(8,128)(2,1)}, bf16[12,128,128]{2,1,0:T(8,128)(2,1)}, u32[]{:S(2)}, u32[]{:S(2)}) collective-permute-start(bf16[12,128,128]{2,1,0:T(8,128)(2,1)} %get-tuple-element.113), channel_id=1, source_target_pairs={{0,24},{8,0},{16,8},{24,16},{1,25},{9,1},{17,9},{25,17},{2,26},{10... | collective-permute-start | bytes 1179656 | tf_op jit(solution)/shard_map/ppermute | solution.py:30
Sparse Core Ops, SparseCore 0:
  10.1 86.7 all-gather.1

commit v4 on v3

--- a/solution.py
+++ b/solution.py
@@ -30,10 +30,14 @@
     return lax.ppermute(value, axis, [(s, (s + steps) % count) for s in range(count)])
 
 
+def exchange(value, axis):
+    return lax.all_to_all(value, axis, split_axis=0, concat_axis=0, tiled=True)
+
+
 def everyone(value, axis):
     count = lax.axis_size(axis)
     spread = jnp.broadcast_to(value[None], (count, *value.shape))
-    return lax.all_to_all(spread, axis, split_axis=0, concat_axis=0, tiled=True)
+    return exchange(spread, axis)
 
 
 def window(delta, length):
@@ -52,142 +56,92 @@
     return dense.reshape(x_cells.shape[0], y_cells.shape[0], z_cells.shape[0])
 
 
-def select_kernel(base, codes, counts, held, *rest):
-    outs, sems = rest[: NX - 1], rest[NX - 1]
-
+SMEM = pl.BlockSpec(memory_space=pltpu.SMEM)
+ANYWHERE = pl.BlockSpec(memory_space=pl.ANY)
+VMEM = pl.BlockSpec(memory_space=pltpu.VMEM)
+
+
+def select_kernel(base, codes, counts, held, out, sems):
     def copy(d, j):
         return pltpu.make_async_copy(
-            held.at[codes[d * FULL + base + j]], outs[d].at[j], sems.at[d, j]
+            held.at[codes[d * FULL + base + j]], out.at[d, j], sems.at[d, j]
         )
 
-    fills = [jnp.clip(counts[d] - base, 0, CAP) for d in range(NX - 1)]
-    for d in range(NX - 1):
+    fills = [jnp.clip(counts[d] - base, 0, CAP) for d in range(NX)]
+    for d in range(NX):
         lax.fori_loop(0, fills[d], lambda j, _, d=d: copy(d, j).start(), None)
-    for d in range(NX - 1):
+    for d in range(NX):
         lax.fori_loop(0, fills[d], lambda j, _, d=d: copy(d, j).wait(), None)
 
 
 def select(codes, counts, held, base):
-    block = jax.ShapeDtypeStruct((CAP, BS, BS), jnp.bfloat16)
     return pl.pallas_call(
         functools.partial(select_kernel, base),
-        out_shape=[block] * (NX - 1),
-        in_specs=[
-            pl.BlockSpec(memory_space=pltpu.SMEM),
-            pl.BlockSpec(memory_space=pltpu.SMEM),
-            pl.BlockSpec(memory_space=pl.ANY),
-        ],
-        out_specs=[pl.BlockSpec(memory_space=pltpu.VMEM)] * (NX - 1),
-        scratch_shapes=[pltpu.SemaphoreType.DMA((NX - 1, CAP))],
+        out_shape=jax.ShapeDtypeStruct((NX, CAP, BS, BS), jnp.bfloat16),
+        in_specs=[SMEM, SMEM, ANYWHERE],
+        out_specs=VMEM,
+        scratch_shapes=[pltpu.SemaphoreType.DMA((NX, CAP))],
         name="select",
     )(codes, counts, held)
 
 
-def run_items(items, total, lefts, rights, sums, left_buf, right_buf, left_sem, right_sem):
-    def begin(n, _):
-        code = items[n]
-        left = lax.rem(code, 128)
-        source = lax.div(code, 1024)
-        group = lax.div(source, 128)
-        place = lax.rem(source, 128)
-        for g in range(NCORE):
-
-            @pl.when(lax.div(left, 32) == g)
-            def _():
-                pltpu.make_async_copy(
-                    lefts[g].at[lax.rem(left, 32)], left_buf.at[n], left_sem.at[n]
-                ).start()
-
-        for g in range(len(rights)):
-
-            @pl.when(group == g)
-            def _():
-                pltpu.make_async_copy(
-                    rights[g].at[place], right_buf.at[n], right_sem.at[n]
-                ).start()
-
+def run_items(items, total, lefts, rights, stride, sums):
     def multiply(q, _):
-        places = [q * GROUP + k for k in range(GROUP)]
-        for n in places:
-
-            @pl.when(n < total)
-            def _():
-                pltpu.make_async_copy(
-                    lefts[0].at[0], left_buf.at[n], left_sem.at[n]
-                ).wait()
-                pltpu.make_async_copy(
-                    rights[0].at[0], right_buf.at[n], right_sem.at[n]
-                ).wait()
-
+        codes = [items[q * GROUP + k] for k in range(GROUP)]
         terms = [
-            jnp.dot(left_buf[n], right_buf[n], preferred_element_type=jnp.float32)
-            for n in places
+            jnp.dot(
+                lefts[code & 127],
+                rights[((code >> 10) & 127) + (code >> 17) * stride],
+                preferred_element_type=jnp.float32,
+            )
+            for code in codes
         ]
-        for n, term in zip(places, terms):
-            target = lax.rem(lax.div(items[n], 128), 8)
-            sums[jnp.where(n < total, target, BR * KC)] += term
-
-    lax.fori_loop(0, total, begin, None)
-    yield
+        for k, (code, term) in enumerate(zip(codes, terms)):
+            target = (code >> 7) & 7
+            sums[jnp.where(q * GROUP + k < total, target, BR * KC)] += term
+
     lax.fori_loop(0, lax.div(total + GROUP - 1, GROUP), multiply, None)
 
 
-def home_kernel(items, count, left0, left1, held, sums, *scratch):
-    steps = run_items(items, count[0], (left0, left1), (held,), sums, *scratch)
-    next(steps)
+def home_kernel(items, count, lefts, held, sums):
     sums[...] = jnp.zeros_like(sums)
-    next(steps, None)
-
-
-def away_kernel(items, count, scale, left0, left1, *rest):
-    rights, begun, mine, out = rest[: NX - 1], rest[NX - 1], rest[NX], rest[NX + 1]
-    *scratch, sums = rest[NX + 2 :]
-    steps = run_items(items, count[0], (left0, left1), rights, sums, *scratch)
-    next(steps)
+    run_items(items, count[0], lefts, held, 0, sums)
+
+
+def away_kernel(items, count, scale, lefts, rights, begun, mine, out, sums):
     sums[...] = begun[...]
-    next(steps, None)
+    run_items(items, count[0], lefts, rights, rights.shape[0] // NX, sums)
     twice = scale[0]
     for o in range(BR * KC):
         value = sums[o]
         out[o] = value + twice * (mine[o].astype(jnp.float32) - value)
 
 
-SMEM = pl.BlockSpec(memory_space=pltpu.SMEM)
-ANYWHERE = pl.BlockSpec(memory_space=pl.ANY)
-VMEM = pl.BlockSpec(memory_space=pltpu.VMEM)
-
-
-def items_call(kernel, name, in_specs, size, more):
+def items_call(kernel, name, in_specs, size, scratch):
     return pl.pallas_call(
         kernel,
         out_shape=jax.ShapeDtypeStruct((size, BS, BS), jnp.float32),
         in_specs=in_specs,
         out_specs=VMEM,
-        scratch_shapes=[
-            pltpu.VMEM((ITEMS, BS, BS), jnp.bfloat16),
-            pltpu.VMEM((ITEMS, BS, BS), jnp.bfloat16),
-            pltpu.SemaphoreType.DMA((ITEMS,)),
-            pltpu.SemaphoreType.DMA((ITEMS,)),
-            *more,
-        ],
+        scratch_shapes=scratch,
         compiler_params=pltpu.CompilerParams(vmem_limit_bytes=24 * 1024 * 1024),
         cost_estimate=pl.CostEstimate(
-            flops=2 * 16 * BS**3, bytes_accessed=16 * 4 * BS * BS, transcendentals=0
+            flops=2 * 16 * BS**3, bytes_accessed=6 << 20, transcendentals=0
         ),
         name=name,
     )
 
 
 def home_products(items, count, lefts, held):
-    call = items_call(home_kernel, "home", [SMEM] * 2 + [ANYWHERE] * 3, SUMS, [])
-    return call(items, count, *lefts, held)
+    call = items_call(home_kernel, "home", [SMEM] * 2 + [VMEM] * 2, SUMS, [])
+    return call(items, count, lefts, held)
 
 
 def away_products(items, count, scale, lefts, rights, begun, mine):
-    specs = [SMEM] * 3 + [ANYWHERE] * (NX + 1) + [VMEM] * 2
+    specs = [SMEM] * 3 + [VMEM] * 4
     sums = pltpu.VMEM((SUMS, BS, BS), jnp.float32)
     call = items_call(away_kernel, "away", specs, BR * KC, [sums])
-    return call(items, count, scale, *lefts, *rights, begun, mine)
+    return call(items, count, scale, lefts, rights, begun, mine)
 
 
 def compact(wanted, places, codes, slots):
@@ -245,10 +199,7 @@
     own_counts = lax.dynamic_index_in_dim(counts, x, 1, False)
     codes = (zs * BR + own_within[:, :, None]) * KC + us
     sends = compact(own_table, own_place, codes.reshape(NX, FULL), FULL)
-    to = (x + jnp.arange(1, NX)) % NX
-    pick = (to[:, None] == jnp.arange(NX)[None, :]).astype(jnp.int32)
-    sends = jnp.sum(pick[:, :, None] * sends[None], axis=1)
-    send_counts = jnp.sum(pick * own_counts[None], axis=1)
+    send_counts = jnp.where(jnp.arange(NX) == x, 0, own_counts)
 
     my_refs = lax.dynamic_index_in_dim(refs, x, 0, False)
     my_match = lax.dynamic_slice_in_dim(match, x * BR, BR, 0)
@@ -259,8 +210,8 @@
     from_x = my_owner % NX
     us = jnp.arange(KC, dtype=jnp.int32)[None, :]
     at_home = ((my_owner // NX * BR + my_refs % BR) * KC)[:, None] + us
-    away = (x - from_x) % NX
-    source = jnp.where((away == 0)[:, None], at_home, (away[:, None] - 1) * 128 + there)
+    away = from_x != x
+    source = jnp.where(away[:, None], from_x[:, None] * 128 + there, at_home)
     slot = jnp.arange(SLOTS, dtype=jnp.int32)
     left_y = (y - slot // (KC * NCORE)) % NY
     left_core = (slot // KC + core) % NCORE
@@ -269,7 +220,7 @@
     wanted = jnp.any(my_match, axis=-1)
     aim = rows[:, :, None] * KC + my_match[..., 1].astype(jnp.int32)
     code = left[:, :, None] + 128 * aim + 1024 * source.reshape(BR, SLOTS, KC)
-    wanted = wanted & jnp.stack([away == 0, away > 0]).reshape(2, BR, SLOTS, 1)
+    wanted = wanted & jnp.stack([~away, away]).reshape(2, BR, SLOTS, 1)
     wanted = wanted.reshape(2, ITEMS)
     items = compact(wanted, places_of(wanted), code.reshape(1, ITEMS), ITEMS)
     totals = jnp.sum(wanted.astype(jnp.int32), axis=-1)
@@ -301,7 +252,7 @@
     blocks, packed = lax.optimization_barrier((matrix, packed))
     lefts = jnp.concatenate([blocks] + [shift(blocks, "y", d) for d in range(1, NY)])
     lefts = lefts.reshape(NY * BR * KC, BS, BS)
-    lefts = (lefts, shift(lefts, "core", 1))
+    lefts = jnp.concatenate([lefts, shift(lefts, "core", 1)])
     set_charge = packed[: BR * sets]
 
     atoms_here = atom_set.shape[0]
@@ -322,14 +273,6 @@
     near = lax.dynamic_slice_in_dim(packed, row, 5, 0)[:, :4]
     near = near.transpose(1, 0, 2).reshape(4, 5 * atoms_here)
 
-    mine = matrix.reshape(BR * KC, BS, BS)
-    outgoing = select(sends, send_counts, held, 0)
-    first = [None] * (NX - 1)
-    for d in (2, 3, 1):
-        items, outgoing = lax.optimization_barrier((items, outgoing))
-        first[d - 1] = shift(outgoing[d - 1], "x", d)
-    begun = home_products(items[0], totals[:1], lefts, held)
-
     x_cells = (row * PLANES + jnp.arange(PLANES, dtype=jnp.int32)).astype(jnp.float32)
     y_cells = (col * YC + jnp.arange(YC, dtype=jnp.int32)).astype(jnp.float32)
     z_cells = jnp.arange(GZ, dtype=jnp.int32).astype(jnp.float32)
@@ -337,22 +280,26 @@
         near, x_cells, y_cells, z_cells, PLANES * NZ * NX, YC * NY * NCORE, GZ
     )
 
+    mine = matrix.reshape(BR * KC, BS, BS)
+    sends, lefts, density = lax.optimization_barrier((sends, lefts, density))
+    outgoing = select(sends, send_counts, held, 0)
+    first = exchange(outgoing, "x")
+    begun = home_products(items[0], totals[:1], lefts, held)
+
     def finish(rights):
+        rights = rights.reshape(-1, BS, BS)
         return away_products(items[1], totals[1:], scale, lefts, rights, begun, mine)
 
-    def one_round(*first):
+    def one_round(first):
         return finish(first)
 
-    def two_rounds(*first):
-        both = list(first)
+    def two_rounds(first):
+        rounds = [first]
         for base in range(CAP, FULL, CAP):
-            more = select(sends, send_counts, held, base)
-            for d in range(1, NX):
-                coming = shift(more[d - 1], "x", d)
-                both[d - 1] = jnp.concatenate([both[d - 1], coming])
-        return finish(both)
-
-    purified = lax.cond(over > 0, two_rounds, one_round, *first)
+            rounds.append(exchange(select(sends, send_counts, held, base), "x"))
+        return finish(jnp.concatenate(rounds, axis=1))
+
+    purified = lax.cond(over > 0, two_rounds, one_round, first)
     return purified.reshape(matrix.shape), density
 
 

time: 134 us -> 130 us (0.970)
  Pallas kernels: 13.9 us -> 8.85 us
  other arithmetic: 8.46 us -> 11.8 us
  starting transfers between devices: 44.2 us -> 40.9 us
    ppermute x7 -> x4, starting transfers between devices: 21.1 us -> 12.9 us  [shift(): lax.ppermute(value, axis, [(s, (s + steps) % count) for s in range(count)])]
    all_to_all x2 -> x3, waiting for transfers between devices: 13.2 us -> 18.6 us  [exchange(): return lax.all_to_all(value, axis, split_axis=0, concat_axis=0, tiled=True)]
    pallas_call x3, Pallas kernels: 13.9 us -> 8.85 us  [the longest x1 3.07 us: select(): pl.pallas_call(functools.partial(select_kernel, base), out_shape=jax.Shap...]
    all_to_all x2 -> x3, starting transfers between devices: 23 us -> 28 us  [exchange(): return lax.all_to_all(value, axis, split_axis=0, concat_axis=0, tiled=True)]
    all_gather x1, waiting for transfers between devices: 20.1 us -> 16.7 us  [shards(): held = lax.all_gather(matrix, 'z', axis=0, tiled=True)]
    ppermute x7 -> x4, waiting for transfers between devices: 1.92 us -> 0.01 us  [shift(): lax.ppermute(value, axis, [(s, (s + steps) % count) for s in range(count)])]
    concatenate x0 -> x1, other arithmetic: none -> 1.41 us  [shards(): lefts = jnp.concatenate([lefts, shift(lefts, 'core', 1)])]
  transfers between devices with their start and end apart: 10 -> 8, of which waited for: 4 -> 4; matrix products, arithmetic and copies ran while one was open for 16% -> 19% of each run, Pallas kernels for 5% -> 2%
where the time goes in v4:
time: 130 us; the launch traced here: 128 us
  starting transfers between devices  40.9 us (31%)
  waiting for transfers between devices  36 us (28%)
  between operations  16.6 us (13%)
  other arithmetic  11.8 us (9%)
  local copies, waits for them, and re-layouts  9.34 us (7%)
  Pallas kernels  8.85 us (7%)
  matrix products  4.64 us (4%)
    all_to_all x3, starting transfers between devices, exchange(): return lax.all_to_all(value, axis, split_axis=0, concat_axis=0, tiled=True)  28 us
    all_to_all x3, waiting for transfers between devices, exchange(): return lax.all_to_all(value, axis, split_axis=0, concat_axis=0, tiled=True)  18.6 us
    all_gather x1, waiting for transfers between devices, shards(): held = lax.all_gather(matrix, 'z', axis=0, tiled=True)  16.7 us
    ppermute x4, starting transfers between devices, shift(): lax.ppermute(value, axis, [(s, (s + steps) % count) for s in range(count)])  12.9 us
    dot_general x1, matrix products, collocate(): dense = jnp.dot(plane.T, along_z, precision=lax.Precision.HIGHEST)  3.13 us
    pallas_call x1, Pallas kernels, select(): pl.pallas_call(functools.partial(select_kernel, base), out_shape=jax.Shap...  3.07 us
    pallas_call x1, Pallas kernels, away_products(): return call(items, count, scale, lefts, rights, begun, mine)  2.95 us
    pallas_call x1, Pallas kernels, home_products(): return call(items, count, lefts, held)  2.82 us
  transfers between devices with their start and end apart: 8, of which 4 were waited for; matrix products, arithmetic and copies ran while one was open for 19% of the time, Pallas kernels for 2%

profile of v4, /device:TPU:6, one launch (start us, length us, event | category | flops | bytes accessed | tf_op | source)
XLA Modules:
  0.0 128.2 jit_solution(7611045535308683558)
XLA Ops:
  7.2 0.7 all-gather.2.cloned.1.call-update
  7.9 0.8 broadcast_compare_fusion
  8.9 0.9 convolution_convert_fusion
  10.1 0.8 broadcast_compare_fusion.2
  10.9 0.2 fusion.88
  11.5 0.2 fusion.31
  12.1 0.2 convert_reduce_fusion.3
  12.3 0.6 convert_reduce_fusion.4
  13.6 0.8 dynamic-slice_compare_fusion
  14.5 1.1 select_reduce_fusion
  15.6 0.2 fusion.44
  16.0 0.6 broadcast_in_dim.59
  16.6 4.4 %all-to-all-start.2 = ((f32[8,1,65]{2,1,0:T(1,128)}), f32[8,1,65]{2,1,0:T(1,128)S(1)}, u32[]{:S(2)}, u32[]{:S(2)}) async-start(f32[8,1,65]{2,1,0:T(1,128)} %broadcast_in_dim.59), calls=%async_computation.2 | async-start | bytes 8192 | tf_op jit(solution)/shard_map/all_to_all | solution.py:34
  21.6 0.2 select_reduce_fusion.1
  21.9 0.2 copy.136
  22.4 0.4 convert_reduce_fusion
  23.5 0.7 broadcast_subtract_fusion
  24.2 0.7 fusion.79
  24.9 0.2 fusion.2
  25.1 0.2 fusion.65
  25.4 0.9 all-to-all-done.2
  26.3 3.0 %collective-permute-start = (bf16[4,2,128,128]{3,2,1,0:T(8,128)(2,1)S(1)}, bf16[4,2,128,128]{3,2,1,0:T(8,128)(2,1)S(1)}, u32[]{:S(2)}, u32[]{:S(2)}) collective-permute-start(bf16[4,2,128,128]{3,2,1,0:T(8,128)(2,1)S(1)} %copy-done), channel_id=1, source_target_pairs={{0,2},{2,4},{4,6},{6,0},{1,3},{3,5},{5,7},{7,1},{8,10},{10,12},{12... | collective-permute-start | bytes 786440 | tf_op jit(solution)/shard_map/ppermute | solution.py:30
  29.3 4.6 %collective-permute-start.1 = (bf16[4,2,128,128]{3,2,1,0:T(8,128)(2,1)S(1)}, bf16[4,2,128,128]{3,2,1,0:T(8,128)(2,1)S(1)}, u32[]{:S(2)}, u32[]{:S(2)}) collective-permute-start(bf16[4,2,128,128]{3,2,1,0:T(8,128)(2,1)S(1)} %copy-done), channel_id=1, source_target_pairs={{0,4},{2,6},{4,0},{6,2},{1,5},{3,7},{5,1},{7,3},{8,12},{10,14},{12... | collective-permute-start | bytes 786440 | tf_op jit(solution)/shard_map/ppermute | solution.py:30
  33.9 3.4 %collective-permute-start.2 = (bf16[4,2,128,128]{3,2,1,0:T(8,128)(2,1)S(1)}, bf16[4,2,128,128]{3,2,1,0:T(8,128)(2,1)S(1)}, u32[]{:S(2)}, u32[]{:S(2)}) collective-permute-start(bf16[4,2,128,128]{3,2,1,0:T(8,128)(2,1)S(1)} %copy-done), channel_id=1, source_target_pairs={{0,6},{2,0},{4,2},{6,4},{1,7},{3,1},{5,3},{7,5},{8,14},{10,8},{12,... | collective-permute-start | bytes 786440 | tf_op jit(solution)/shard_map/ppermute | solution.py:30
  37.3 0.6 slice.77
  37.9 0.7 pad.17.clone
  38.6 0.2 fusion.46
  38.9 0.8 reshape.629
  39.7 18.6 %all-to-all-start.3 = ((f32[64,1,320]{2,1,0:T(1,128)}), f32[64,1,320]{2,1,0:T(1,128)S(1)}, u32[]{:S(2)}, u32[]{:S(2)}) async-start(f32[64,1,320]{2,1,0:T(1,128)} %reshape.629), calls=%async_computation.3 | async-start | bytes 196608 | tf_op jit(solution)/shard_map/all_to_all | solution.py:34
  58.5 1.9 %collective-permute-start.3 = (bf16[32,128,128]{2,1,0:T(8,128)(2,1)S(1)}, bf16[32,128,128]{2,1,0:T(8,128)(2,1)}, u32[]{:S(2)}, u32[]{:S(2)}) collective-permute-start(bf16[32,128,128]{2,1,0:T(8,128)(2,1)S(1)} %bitcast.82), channel_id=1, source_target_pairs={{0,1},{1,0},{2,3},{3,2},{4,5},{5,4},{6,7},{7,6},{8,9},{9,8},{10,11... | collective-permute-start | bytes 3145736 | tf_op jit(solution)/shard_map/ppermute | solution.py:30
  60.4 13.3 %all-to-all-done.3 = f32[64,1,320]{2,1,0:T(1,128)S(1)} async-done(((f32[64,1,320]{2,1,0:T(1,128)}), f32[64,1,320]{2,1,0:T(1,128)S(1)}, u32[]{:S(2)}, u32[]{:S(2)}) %all-to-all-start.3) | async-done | bytes 81952 | tf_op jit(solution)/shard_map/all_to_all | solution.py:34
  73.7 0.5 broadcast.794
  74.2 0.9 reduce.23
  75.7 0.2 fusion.39
  75.9 3.1 %fusion.10 = f32[4,80,640]{2,1,0:T(8,128)} fusion(f32[320]{0:T(512)S(1)} %sub.166, f32[640]{0:T(1024)S(1)} %iota_convert_fusion, f32[320,80]{0,1:T(8,128)S(1)} %fusion.39, f32[320,4]{0,1:T(4,128)S(1)} %fusion.58), kind=kOutput, calls=%fused_computation.18 | convolution fusion | flops 789401600 | bytes 930560 | tf_op jit(solution)/shard_map/dot_general | solution.py:55
  79.0 1.4 %pad_maximum_fusion.1.lefts = bf16[64,128,128]{2,1,0:T(8,128)(2,1)S(1)} fusion(bf16[32,128,128]{2,1,0:T(8,128)(2,1)} %collective-permute-done.3, bf16[32,128,128]{2,1,0:T(8,128)(2,1)S(1)} %bitcast.83), kind=kLoop, calls=%fused_computation.3 | loop fusion | flops 1048576 | bytes 4194304 | tf_op jit(solution)/shard_map/concatenate | solution.py:255
  80.4 16.7 %all-gather.2.cloned.1.call-done = bf16[64,2,128,128]{3,2,1,0:T(8,128)(2,1)} async-done(((bf16[4,2,128,128]{3,2,1,0:T(8,128)(2,1)}), bf16[64,2,128,128]{3,2,1,0:T(8,128)(2,1)}) %all-gather.2.cloned.1.call-update) | async-done | bytes 4194320 | tf_op jit(solution)/shard_map/all_gather | solution.py:235
  97.1 3.1 %select.143 = bf16[4,12,128,128]{3,2,1,0:T(8,128)(2,1)} custom-call(s32[128]{0:T(128)S(1)} %reshape.602.codes, s32[4]{0:T(128)S(1)} %compare_select_fusion.8.counts, bf16[128,128,128]{2,1,0:T(8,128)(2,1)} %bitcast.77), custom_call_target="tpu_custom_call" | custom-call | tf_op jit(solution)/shard_map/select/pallas_call | solution.py:78
  100.2 5.0 %all-to-all-start.4 = ((bf16[4,12,128,128]{3,2,1,0:T(8,128)(2,1)}), bf16[4,12,128,128]{3,2,1,0:T(8,128)(2,1)}, u32[]{:S(2)}, u32[]{:S(2)}) async-start(bf16[4,12,128,128]{3,2,1,0:T(8,128)(2,1)} %select.143), calls=%async_computation.4 | async-start | bytes 3145728 | tf_op jit(solution)/shard_map/all_to_all | solution.py:34
  106.6 0.2 convert_reduce_fusion.2
  106.9 0.7 reduce_sum.109
  108.4 0.7 slice_reduce_fusion
  109.7 2.8 %home.1 = f32[9,128,128]{2,1,0:T(8,128)S(1)} custom-call(s32[128]{0:T(128)S(1)} %slice_bitcast_fusion.2.items, s32[1]{0:T(128)S(1)} %bitcast.96, bf16[64,128,128]{2,1,0:T(8,128)(2,1)S(1)} %pad_maximum_fusion.1.lefts, bf16[128,128,128]{2,1,0:T(8,128)(2,1)} %bitcast.78), custom_call_target="tpu_custom_call" | custom-call | flops 67108864 | bytes 6291456 | tf_op jit(solution)/shard_map/home/pallas_call | solution.py:137
  112.5 4.4 %all-to-all-done.4 = bf16[4,12,128,128]{3,2,1,0:T(8,128)(2,1)} async-done(((bf16[4,12,128,128]{3,2,1,0:T(8,128)(2,1)}), bf16[4,12,128,128]{3,2,1,0:T(8,128)(2,1)}, u32[]{:S(2)}, u32[]{:S(2)}) %all-to-all-start.4) | async-done | bytes 1572896 | tf_op jit(solution)/shard_map/all_to_all | solution.py:34
  116.9 3.6 %conditional.1 = (f32[4,2,128,128]{3,2,1,0:T(8,128)S(1)}) conditional(s32[]{:T(128)} %convert_element_type.98, (s32[2,128]{1,0:T(2,128)S(1)}, s32[2]{0:T(128)S(1)}, bf16[4,12,128,128]{3,2,1,0:T(8,128)(2,1)}, f32[1]{0:T(128)}, bf16[64,128,128]{2,1,0:T(8,128)(2,1)S(1)}, /*index=5*/f32[9,128,128]{2,1,0:T(8,128)S(1)}, ...), branch_computations={%region_16.17_spmd, %region_17.18_spmd} | conditional | flops 71827456 | bytes 25166928 | solution.py:302
  116.9 0.7 slice.51.count
  117.6 3.0 %away.2 = f32[8,128,128]{2,1,0:T(8,128)S(1)} custom-call(s32[128]{0:T(128)S(1)} %slice_bitcast_fusion.items, s32[1]{0:T(128)} %slice.51.count, f32[1]{0:T(128)} %get-tuple-element.40.scale, bf16[64,128,128]{2,1,0:T(8,128)(2,1)S(1)} %get-tuple-element.41.lefts, bf16[48,128,128]{2,1,0:T(8,128)(2,1)} %bitcast.1.rights, ...), custom_call_target="tpu_custom_call" | custom-call | flops 67108864 | bytes 6291456 | tf_op jit(solution)/shard_map/cond/branch_0_fun/away/pallas_call | solution.py:144
  120.6 0.8 copy-done.3
  (101 shorter events, 5.6 us)
Async XLA Ops:
  7.2 19.1 %copy-start = (bf16[4,2,128,128]{3,2,1,0:T(8,128)(2,1)S(1)}, bf16[4,2,128,128]{3,2,1,0:T(8,128)(2,1)}, u32[]{:S(2)}) copy-start(bf16[4,2,128,128]{3,2,1,0:T(8,128)(2,1)} %param.8) | copy-start | bytes 786436
  7.2 17.9 %copy-start.4 = (f32[3,64]{1,0:T(4,128)S(1)}, f32[3,64]{1,0:T(4,128)}, u32[]{:S(2)}) copy-start(f32[3,64]{1,0:T(4,128)} %param.11) | copy-start | bytes 2308
  7.2 89.9 %all-gather.2.cloned.1.call-start = ((), (), s32[]{:S(2)}) async-start(), calls=%async_computation.5 | async-start | bytes 4456448 | tf_op jit(solution)/shard_map/all_gather | solution.py:235
  16.6 9.6 %all-to-all-start.2 = ((f32[8,1,65]{2,1,0:T(1,128)}), f32[8,1,65]{2,1,0:T(1,128)S(1)}, u32[]{:S(2)}, u32[]{:S(2)}) async-start(f32[8,1,65]{2,1,0:T(1,128)} %broadcast_in_dim.59), calls=%async_computation.2 | async-start | bytes 8192 | tf_op jit(solution)/shard_map/all_to_all | solution.py:34
  26.3 32.0 %collective-permute-start = (bf16[4,2,128,128]{3,2,1,0:T(8,128)(2,1)S(1)}, bf16[4,2,128,128]{3,2,1,0:T(8,128)(2,1)S(1)}, u32[]{:S(2)}, u32[]{:S(2)}) collective-permute-start(bf16[4,2,128,128]{3,2,1,0:T(8,128)(2,1)S(1)} %copy-done), channel_id=1, source_target_pairs={{0,2},{2,4},{4,6},{6,0},{1,3},{3,5},{5,7},{7,1},{8,10},{10,12},{12... | collective-permute-start | bytes 786440 | tf_op jit(solution)/shard_map/ppermute | solution.py:30
  29.3 29.0 %collective-permute-start.1 = (bf16[4,2,128,128]{3,2,1,0:T(8,128)(2,1)S(1)}, bf16[4,2,128,128]{3,2,1,0:T(8,128)(2,1)S(1)}, u32[]{:S(2)}, u32[]{:S(2)}) collective-permute-start(bf16[4,2,128,128]{3,2,1,0:T(8,128)(2,1)S(1)} %copy-done), channel_id=1, source_target_pairs={{0,4},{2,6},{4,0},{6,2},{1,5},{3,7},{5,1},{7,3},{8,12},{10,14},{12... | collective-permute-start | bytes 786440 | tf_op jit(solution)/shard_map/ppermute | solution.py:30
  33.9 24.4 %collective-permute-start.2 = (bf16[4,2,128,128]{3,2,1,0:T(8,128)(2,1)S(1)}, bf16[4,2,128,128]{3,2,1,0:T(8,128)(2,1)S(1)}, u32[]{:S(2)}, u32[]{:S(2)}) collective-permute-start(bf16[4,2,128,128]{3,2,1,0:T(8,128)(2,1)S(1)} %copy-done), channel_id=1, source_target_pairs={{0,6},{2,0},{4,2},{6,4},{1,7},{3,1},{5,3},{7,5},{8,14},{10,8},{12,... | collective-permute-start | bytes 786440 | tf_op jit(solution)/shard_map/ppermute | solution.py:30
  39.7 34.0 %all-to-all-start.3 = ((f32[64,1,320]{2,1,0:T(1,128)}), f32[64,1,320]{2,1,0:T(1,128)S(1)}, u32[]{:S(2)}, u32[]{:S(2)}) async-start(f32[64,1,320]{2,1,0:T(1,128)} %reshape.629), calls=%async_computation.3 | async-start | bytes 196608 | tf_op jit(solution)/shard_map/all_to_all | solution.py:34
  58.5 20.5 %collective-permute-start.3 = (bf16[32,128,128]{2,1,0:T(8,128)(2,1)S(1)}, bf16[32,128,128]{2,1,0:T(8,128)(2,1)}, u32[]{:S(2)}, u32[]{:S(2)}) collective-permute-start(bf16[32,128,128]{2,1,0:T(8,128)(2,1)S(1)} %bitcast.82), channel_id=1, source_target_pairs={{0,1},{1,0},{2,3},{3,2},{4,5},{5,4},{6,7},{7,6},{8,9},{9,8},{10,11... | collective-permute-start | bytes 3145736 | tf_op jit(solution)/shard_map/ppermute | solution.py:30
  75.2 3.8 %copy-start.1 = (f32[64,5,64]{2,1,0:T(8,128)}, f32[64,5,64]{2,1,0:T(8,128)S(1)}, u32[]{:S(2)}) copy-start(f32[64,5,64]{2,1,0:T(8,128)S(1)} %reshape.630) | copy-start | bytes 245764
  100.2 6.7 %slice-start = ((f32[64,5,64]{2,1,0:T(8,128)}), f32[64,1,64]{2,1,0:T(1,128)S(1)}, s32[]{:S(2)}) async-start(f32[64,5,64]{2,1,0:T(8,128)} %copy-done.1), calls=%async_computation.6 | async-start | bytes 65536 | tf_op jit(solution)/shard_map/slice | solution.py:269
  100.2 8.2 %copy-start.2 = (f32[64,5,64]{2,1,0:T(8,128)S(1)}, f32[64,5,64]{2,1,0:T(8,128)}, u32[]{:S(2)}) copy-start(f32[64,5,64]{2,1,0:T(8,128)} %copy-done.1) | copy-start | bytes 245764
  100.2 16.7 %all-to-all-start.4 = ((bf16[4,12,128,128]{3,2,1,0:T(8,128)(2,1)}), bf16[4,12,128,128]{3,2,1,0:T(8,128)(2,1)}, u32[]{:S(2)}, u32[]{:S(2)}) async-start(bf16[4,12,128,128]{3,2,1,0:T(8,128)(2,1)} %select.143), calls=%async_computation.4 | async-start | bytes 3145728 | tf_op jit(solution)/shard_map/all_to_all | solution.py:34
  120.6 0.8 copy-start.3
Sparse Core Ops, SparseCore 0:
  10.1 86.9 all-gather.1

commit v5 on v4

--- a/solution.py
+++ b/solution.py
@@ -23,11 +23,6 @@
 
 sharpness = 64.0
 half_fill = 0.5
-
-
-def shift(value, axis, steps):
-    count = lax.axis_size(axis)
-    return lax.ppermute(value, axis, [(s, (s + steps) % count) for s in range(count)])
 
 
 def exchange(value, axis):
@@ -213,10 +208,8 @@
     away = from_x != x
     source = jnp.where(away[:, None], from_x[:, None] * 128 + there, at_home)
     slot = jnp.arange(SLOTS, dtype=jnp.int32)
-    left_y = (y - slot // (KC * NCORE)) % NY
-    left_core = (slot // KC + core) % NCORE
     rows = jnp.arange(BR, dtype=jnp.int32)[:, None]
-    left = ((left_core * NY + left_y)[None, :] * BR + rows) * KC + (slot % KC)[None, :]
+    left = ((slot // KC)[None, :] * BR + rows) * KC + (slot % KC)[None, :]
     wanted = jnp.any(my_match, axis=-1)
     aim = rows[:, :, None] * KC + my_match[..., 1].astype(jnp.int32)
     code = left[:, :, None] + 128 * aim + 1024 * source.reshape(BR, SLOTS, KC)
@@ -250,9 +243,7 @@
     packed = jnp.concatenate([set_part.reshape(-1), over.astype(jnp.float32)[None]])
     packed = jnp.sum(everyone(packed[None], COL), axis=0)[0]
     blocks, packed = lax.optimization_barrier((matrix, packed))
-    lefts = jnp.concatenate([blocks] + [shift(blocks, "y", d) for d in range(1, NY)])
-    lefts = lefts.reshape(NY * BR * KC, BS, BS)
-    lefts = jnp.concatenate([lefts, shift(lefts, "core", 1)])
+    lefts = everyone(blocks, COL).reshape(SLOTS * BR, BS, BS)
     set_charge = packed[: BR * sets]
 
     atoms_here = atom_set.shape[0]
@@ -264,7 +255,8 @@
     start_x = atom_slab.astype(jnp.float32) * PLANES + atom_offset[0]
     flag = jnp.broadcast_to(packed[BR * sets], charge.shape)
     packed = jnp.stack([charge, start_x, atom_offset[1], atom_offset[2], flag])
-    packed = everyone(packed, ROW)
+    packed = lax.all_gather(everyone(packed, "x"), "z", axis=0, tiled=False)
+    packed = packed.reshape(NZ * NX, 5, atoms_here)
     over = jnp.sum(packed[:, 4, 0])
     trace = jnp.sum(packed[:, 0])
     weight = jax.nn.sigmoid(sharpness * (half_fill - trace / (NB * BS)))

time: 130 us -> 127 us (0.977)
  blocking collectives: 0 us -> 34.6 us
  starting transfers between devices: 40.9 us -> 21.2 us
  waiting for transfers between devices: 36 us -> 17.5 us
  local copies, waits for them, and re-layouts: 9.34 us -> 11.7 us
  other arithmetic: 11.8 us -> 10.1 us
    all_gather x0 -> x1, blocking collectives: none -> 34.6 us  [shards(): packed = lax.all_gather(everyone(packed, 'x'), 'z', axis=0, tiled=False)]
    ppermute x4 -> x0, starting transfers between devices: 12.9 us -> none  [shift(): lax.ppermute(value, axis, [(s, (s + steps) % count) for s in range(count)])]
    all_to_all x3 -> x4, waiting for transfers between devices: 18.6 us -> 8.17 us  [exchange(): return lax.all_to_all(value, axis, split_axis=0, concat_axis=0, tiled=True)]
    all_gather x1, waiting for transfers between devices: 16.7 us -> 8.63 us  [shards(): held = lax.all_gather(matrix, 'z', axis=0, tiled=True)]
    all_to_all x3 -> x4, starting transfers between devices: 28 us -> 21.2 us  [exchange(): return lax.all_to_all(value, axis, split_axis=0, concat_axis=0, tiled=True)]
    broadcast_in_dim x2 -> x3, local copies, waits for them, and re-layouts: 0.64 us -> 2.46 us  [everyone(): spread = jnp.broadcast_to(value[None], (count, *value.shape))]
    concatenate x2 -> x0, other arithmetic: 1.54 us -> none  [the longest x1 1.41 us: shards(): lefts = jnp.concatenate([lefts, shift(lefts, 'core', 1)])]
  transfers between devices with their start and end apart: 8 -> 5, of which waited for: 4 -> 4; matrix products, arithmetic and copies ran while one was open for 19% -> 20% of each run, Pallas kernels for 2% -> 2%
where the time goes in v5:
time: 127 us; the launch traced here: 125 us
  blocking collectives  34.6 us (27%)
  starting transfers between devices  21.2 us (17%)
  waiting for transfers between devices  17.5 us (14%)
  between operations  16.4 us (13%)
  local copies, waits for them, and re-layouts  11.7 us (9%)
  other arithmetic  10.1 us (8%)
  Pallas kernels  8.78 us (7%)
  matrix products  4.64 us (4%)
    all_gather x1, blocking collectives, shards(): packed = lax.all_gather(everyone(packed, 'x'), 'z', axis=0, tiled=False)  34.6 us
    all_to_all x4, starting transfers between devices, exchange(): return lax.all_to_all(value, axis, split_axis=0, concat_axis=0, tiled=True)  21.2 us
    all_gather x1, waiting for transfers between devices, shards(): held = lax.all_gather(matrix, 'z', axis=0, tiled=True)  8.63 us
    all_to_all x4, waiting for transfers between devices, exchange(): return lax.all_to_all(value, axis, split_axis=0, concat_axis=0, tiled=True)  8.17 us
    dot_general x1, matrix products, collocate(): dense = jnp.dot(plane.T, along_z, precision=lax.Precision.HIGHEST)  3.13 us
    pallas_call x1, Pallas kernels, select(): pl.pallas_call(functools.partial(select_kernel, base), out_shape=jax.Shap...  3 us
    pallas_call x1, Pallas kernels, away_products(): return call(items, count, scale, lefts, rights, begun, mine)  2.95 us
    pallas_call x1, Pallas kernels, home_products(): return call(items, count, lefts, held)  2.82 us
  transfers between devices with their start and end apart: 5, of which 4 were waited for; matrix products, arithmetic and copies ran while one was open for 20% of the time, Pallas kernels for 2%

profile of v5, /device:TPU:6, one launch (start us, length us, event | category | flops | bytes accessed | tf_op | source)
XLA Modules:
  0.0 125.0 jit_solution(1321982088739431618)
XLA Ops:
  7.2 0.7 all-gather.3.cloned.1.call-update
  7.9 0.8 broadcast_compare_fusion
  8.9 0.9 convolution_convert_fusion
  9.9 0.2 copy.113
  10.1 0.8 broadcast_compare_fusion.2
  10.9 0.2 fusion.82
  11.5 0.2 fusion.31
  12.1 0.2 convert_reduce_fusion.3
  12.2 0.6 convert_reduce_fusion.4
  13.6 0.8 dynamic-slice_compare_fusion
  14.5 1.1 select_reduce_fusion
  15.6 0.2 fusion.44
  16.0 0.6 broadcast_in_dim.61
  16.6 4.4 %all-to-all-start.2 = ((f32[8,1,65]{2,1,0:T(1,128)}), f32[8,1,65]{2,1,0:T(1,128)S(1)}, u32[]{:S(2)}, u32[]{:S(2)}) async-start(f32[8,1,65]{2,1,0:T(1,128)} %broadcast_in_dim.61), calls=%async_computation.2 | async-start | bytes 8192 | tf_op jit(solution)/shard_map/all_to_all | solution.py:29
  21.5 0.2 select_reduce_fusion.1
  21.9 0.2 copy.114
  23.0 0.4 convert_reduce_fusion
  23.6 0.7 broadcast_subtract_fusion
  24.3 0.7 fusion.73
  25.0 0.7 slice.76
  25.7 0.5 all-to-all-done.2
  26.3 0.6 slice.77
  26.8 0.7 pad.11.clone
  27.6 0.2 fusion.46
  27.9 0.7 reshape.602
  28.5 7.9 %all-to-all-start.3 = ((f32[4,1,320]{2,1,0:T(1,128)}), f32[4,1,320]{2,1,0:T(1,128)S(1)}, u32[]{:S(2)}, u32[]{:S(2)}) async-start(f32[4,1,320]{2,1,0:T(1,128)} %reshape.602), calls=%async_computation.3 | async-start | bytes 12288 | tf_op jit(solution)/shard_map/all_to_all | solution.py:29
  36.4 0.2 fusion.65
  36.9 2.8 %all-to-all-done.3 = f32[4,1,320]{2,1,0:T(1,128)S(1)} async-done(((f32[4,1,320]{2,1,0:T(1,128)}), f32[4,1,320]{2,1,0:T(1,128)S(1)}, u32[]{:S(2)}, u32[]{:S(2)}) %all-to-all-start.3) | async-done | bytes 5152 | tf_op jit(solution)/shard_map/all_to_all | solution.py:29
  39.7 1.8 %broadcast_in_dim.76 = bf16[8,4,2,128,128]{4,3,2,1,0:T(8,128)(2,1)} broadcast(bf16[4,2,128,128]{3,2,1,0:T(8,128)(2,1)S(1)} %copy-done), dimensions={1,2,3,4} | broadcast | bytes 2359296 | tf_op jit(solution)/shard_map/broadcast_in_dim | solution.py:34
  41.5 4.3 %all-to-all-start.4 = ((bf16[8,4,2,128,128]{4,3,2,1,0:T(8,128)(2,1)}), bf16[8,4,2,128,128]{4,3,2,1,0:T(8,128)(2,1)S(1)}, u32[]{:S(2)}, u32[]{:S(2)}) async-start(bf16[8,4,2,128,128]{4,3,2,1,0:T(8,128)(2,1)} %broadcast_in_dim.76), calls=%async_computation.4 | async-start | bytes 4194304 | tf_op jit(solution)/shard_map/all_to_all | solution.py:29
  45.8 0.2 fusion.2
  46.0 0.5 broadcast.710
  46.5 0.7 reduce.23
  47.3 34.6 %all-gather = f32[64,5,64]{2,1,0:T(8,128)S(1)} all-gather(f32[4,5,64]{2,1,0:T(8,128)S(1)} %reshape.603), channel_id=2, replica_groups=mesh['z'=16,'x'=4,'y'=4,'core'=2] {'z'}, dimensions={0}, use_global_device_ids=true | all-gather | bytes 87040 | tf_op jit(solution)/shard_map/all_gather | solution.py:258
  82.4 0.2 fusion.39
  82.6 3.1 %fusion.10 = f32[4,80,640]{2,1,0:T(8,128)} fusion(f32[320]{0:T(512)S(1)} %sub.150, f32[640]{0:T(1024)S(1)} %iota_convert_fusion, f32[320,80]{0,1:T(8,128)S(1)} %fusion.39, f32[320,4]{0,1:T(4,128)S(1)} %fusion.58), kind=kOutput, calls=%fused_computation.16 | convolution fusion | flops 789401600 | bytes 930560 | tf_op jit(solution)/shard_map/dot_general | solution.py:50
  85.7 8.6 %all-gather.3.cloned.1.call-done = bf16[64,2,128,128]{3,2,1,0:T(8,128)(2,1)} async-done(((bf16[4,2,128,128]{3,2,1,0:T(8,128)(2,1)}), bf16[64,2,128,128]{3,2,1,0:T(8,128)(2,1)}) %all-gather.3.cloned.1.call-update) | async-done | bytes 4194320 | tf_op jit(solution)/shard_map/all_gather | solution.py:228
  94.3 3.0 %select.119 = bf16[4,12,128,128]{3,2,1,0:T(8,128)(2,1)} custom-call(s32[128]{0:T(128)S(1)} %reshape.573.codes, s32[4]{0:T(128)S(1)} %compare_select_fusion.4.counts, bf16[128,128,128]{2,1,0:T(8,128)(2,1)} %bitcast.76), custom_call_target="tpu_custom_call" | custom-call | tf_op jit(solution)/shard_map/select/pallas_call | solution.py:73
  97.3 4.6 %all-to-all-start.5 = ((bf16[4,12,128,128]{3,2,1,0:T(8,128)(2,1)}), bf16[4,12,128,128]{3,2,1,0:T(8,128)(2,1)}, u32[]{:S(2)}, u32[]{:S(2)}) async-start(bf16[4,12,128,128]{3,2,1,0:T(8,128)(2,1)} %select.119), calls=%async_computation.5 | async-start | bytes 3145728 | tf_op jit(solution)/shard_map/all_to_all | solution.py:29
  102.9 0.2 convert_reduce_fusion.2
  103.2 0.7 slice_reduce_fusion
  104.6 0.7 slice_reduce_fusion.1
  106.0 2.8 %home.1 = f32[9,128,128]{2,1,0:T(8,128)S(1)} custom-call(s32[128]{0:T(128)S(1)} %slice_bitcast_fusion.2.items, s32[1]{0:T(128)S(1)} %bitcast.95, bf16[64,128,128]{2,1,0:T(8,128)(2,1)S(1)} %bitcast.79, bf16[128,128,128]{2,1,0:T(8,128)(2,1)} %bitcast.77), custom_call_target="tpu_custom_call" | custom-call | flops 67108864 | bytes 6291456 | tf_op jit(solution)/shard_map/home/pallas_call | solution.py:132
  108.8 4.9 %all-to-all-done.5 = bf16[4,12,128,128]{3,2,1,0:T(8,128)(2,1)} async-done(((bf16[4,12,128,128]{3,2,1,0:T(8,128)(2,1)}), bf16[4,12,128,128]{3,2,1,0:T(8,128)(2,1)}, u32[]{:S(2)}, u32[]{:S(2)}) %all-to-all-start.5) | async-done | bytes 1572896 | tf_op jit(solution)/shard_map/all_to_all | solution.py:29
  113.7 3.6 %conditional.1 = (f32[4,2,128,128]{3,2,1,0:T(8,128)S(1)}) conditional(s32[]{:T(128)} %convert_element_type.98, (s32[2,128]{1,0:T(2,128)S(1)}, s32[2]{0:T(128)S(1)}, bf16[4,12,128,128]{3,2,1,0:T(8,128)(2,1)}, f32[1]{0:T(128)}, bf16[64,128,128]{2,1,0:T(8,128)(2,1)S(1)}, /*index=5*/f32[9,128,128]{2,1,0:T(8,128)S(1)}, ...), branch_computations={%region_16.17_spmd, %region_17.18_spmd} | conditional | flops 71827456 | bytes 25166928 | solution.py:294
  113.7 0.7 slice.51.count
  114.3 3.0 %away.2 = f32[8,128,128]{2,1,0:T(8,128)S(1)} custom-call(s32[128]{0:T(128)S(1)} %slice_bitcast_fusion.items, s32[1]{0:T(128)} %slice.51.count, f32[1]{0:T(128)} %get-tuple-element.40.scale, bf16[64,128,128]{2,1,0:T(8,128)(2,1)S(1)} %get-tuple-element.41.lefts, bf16[48,128,128]{2,1,0:T(8,128)(2,1)} %bitcast.1.rights, ...), custom_call_target="tpu_custom_call" | custom-call | flops 67108864 | bytes 6291456 | tf_op jit(solution)/shard_map/cond/branch_0_fun/away/pallas_call | solution.py:139
  117.3 0.8 copy-done.1
  (87 shorter events, 5.2 us)
Async XLA Ops:
  7.2 32.5 %copy-start = (bf16[4,2,128,128]{3,2,1,0:T(8,128)(2,1)S(1)}, bf16[4,2,128,128]{3,2,1,0:T(8,128)(2,1)}, u32[]{:S(2)}) copy-start(bf16[4,2,128,128]{3,2,1,0:T(8,128)(2,1)} %param.8) | copy-start | bytes 786436
  7.2 87.1 %all-gather.3.cloned.1.call-start = ((), (), s32[]{:S(2)}) async-start(), calls=%async_computation.6 | async-start | bytes 4456448 | tf_op jit(solution)/shard_map/all_gather | solution.py:228
  16.6 9.6 %all-to-all-start.2 = ((f32[8,1,65]{2,1,0:T(1,128)}), f32[8,1,65]{2,1,0:T(1,128)S(1)}, u32[]{:S(2)}, u32[]{:S(2)}) async-start(f32[8,1,65]{2,1,0:T(1,128)} %broadcast_in_dim.61), calls=%async_computation.2 | async-start | bytes 8192 | tf_op jit(solution)/shard_map/all_to_all | solution.py:29
  28.5 11.1 %all-to-all-start.3 = ((f32[4,1,320]{2,1,0:T(1,128)}), f32[4,1,320]{2,1,0:T(1,128)S(1)}, u32[]{:S(2)}, u32[]{:S(2)}) async-start(f32[4,1,320]{2,1,0:T(1,128)} %reshape.602), calls=%async_computation.3 | async-start | bytes 12288 | tf_op jit(solution)/shard_map/all_to_all | solution.py:29
  41.5 44.2 %all-to-all-start.4 = ((bf16[8,4,2,128,128]{4,3,2,1,0:T(8,128)(2,1)}), bf16[8,4,2,128,128]{4,3,2,1,0:T(8,128)(2,1)S(1)}, u32[]{:S(2)}, u32[]{:S(2)}) async-start(bf16[8,4,2,128,128]{4,3,2,1,0:T(8,128)(2,1)} %broadcast_in_dim.76), calls=%async_computation.4 | async-start | bytes 4194304 | tf_op jit(solution)/shard_map/all_to_all | solution.py:29
  97.3 16.3 %all-to-all-start.5 = ((bf16[4,12,128,128]{3,2,1,0:T(8,128)(2,1)}), bf16[4,12,128,128]{3,2,1,0:T(8,128)(2,1)}, u32[]{:S(2)}, u32[]{:S(2)}) async-start(bf16[4,12,128,128]{3,2,1,0:T(8,128)(2,1)} %select.119), calls=%async_computation.5 | async-start | bytes 3145728 | tf_op jit(solution)/shard_map/all_to_all | solution.py:29
  117.3 0.8 copy-start.1
Sparse Core Ops, SparseCore 0:
  10.1 84.1 all-gather.2

commit v6 on v5

--- a/solution.py
+++ b/solution.py
@@ -56,31 +56,46 @@
 VMEM = pl.BlockSpec(memory_space=pltpu.VMEM)
 
 
-def select_kernel(base, codes, counts, held, out, sems):
-    def copy(d, j):
+def select_kernel(base, codes, held, out, stage, in_sems, out_sems):
+    def fetch(d, j):
         return pltpu.make_async_copy(
-            held.at[codes[d * FULL + base + j]], out.at[d, j], sems.at[d, j]
+            held.at[codes[d * FULL + base + j]], stage.at[d, j], in_sems.at[d, j]
         )
 
-    fills = [jnp.clip(counts[d] - base, 0, CAP) for d in range(NX)]
+    def store(d, j):
+        return pltpu.make_async_copy(stage.at[d, j], out.at[d, j], out_sems.at[d, j])
+
+    def pass_on(d, j):
+        fetch(d, j).wait()
+        store(d, j).start()
+
+    fills = [jnp.clip(codes[NX * FULL + d] - base, 0, CAP) for d in range(NX)]
     for d in range(NX):
-        lax.fori_loop(0, fills[d], lambda j, _, d=d: copy(d, j).start(), None)
+        lax.fori_loop(0, fills[d], lambda j, _, d=d: fetch(d, j).start(), None)
     for d in range(NX):
-        lax.fori_loop(0, fills[d], lambda j, _, d=d: copy(d, j).wait(), None)
-
-
-def select(codes, counts, held, base):
+        lax.fori_loop(0, fills[d], lambda j, _, d=d: pass_on(d, j), None)
+    for d in range(NX):
+        lax.fori_loop(0, fills[d], lambda j, _, d=d: store(d, j).wait(), None)
+
+
+def select(codes, held, base):
     return pl.pallas_call(
         functools.partial(select_kernel, base),
         out_shape=jax.ShapeDtypeStruct((NX, CAP, BS, BS), jnp.bfloat16),
-        in_specs=[SMEM, SMEM, ANYWHERE],
-        out_specs=VMEM,
-        scratch_shapes=[pltpu.SemaphoreType.DMA((NX, CAP))],
+        in_specs=[SMEM, ANYWHERE],
+        out_specs=ANYWHERE,
+        scratch_shapes=[
+            pltpu.VMEM((NX, CAP, BS, BS), jnp.bfloat16),
+            pltpu.SemaphoreType.DMA((NX, CAP)),
+            pltpu.SemaphoreType.DMA((NX, CAP)),
+        ],
         name="select",
-    )(codes, counts, held)
-
-
-def run_items(items, total, lefts, rights, stride, sums):
+    )(codes, held)
+
+
+def run_items(items, lefts, rights, stride, sums):
+    total = items[ITEMS]
+
     def multiply(q, _):
         codes = [items[q * GROUP + k] for k in range(GROUP)]
         terms = [
@@ -98,26 +113,33 @@
     lax.fori_loop(0, lax.div(total + GROUP - 1, GROUP), multiply, None)
 
 
-def home_kernel(items, count, lefts, held, sums):
+def home_kernel(items, lefts, held, sums):
     sums[...] = jnp.zeros_like(sums)
-    run_items(items, count[0], lefts, held, 0, sums)
-
-
-def away_kernel(items, count, scale, lefts, rights, begun, mine, out, sums):
+    run_items(items, lefts, held, 0, sums)
+
+
+def away_kernel(items, scale, lefts, rights, begun, mine, out, sums, sems):
     sums[...] = begun[...]
-    run_items(items, count[0], lefts, rights, rights.shape[0] // NX, sums)
+    run_items(items, lefts, rights, rights.shape[0] // NX, sums)
     twice = scale[0]
+
+    def store(o):
+        return pltpu.make_async_copy(sums.at[o], out.at[o], sems.at[o])
+
     for o in range(BR * KC):
         value = sums[o]
-        out[o] = value + twice * (mine[o].astype(jnp.float32) - value)
-
-
-def items_call(kernel, name, in_specs, size, scratch):
+        sums[o] = value + twice * (mine[o].astype(jnp.float32) - value)
+        store(o).start()
+    for o in range(BR * KC):
+        store(o).wait()
+
+
+def items_call(kernel, name, in_specs, out_spec, size, scratch):
     return pl.pallas_call(
         kernel,
         out_shape=jax.ShapeDtypeStruct((size, BS, BS), jnp.float32),
         in_specs=in_specs,
-        out_specs=VMEM,
+        out_specs=out_spec,
         scratch_shapes=scratch,
         compiler_params=pltpu.CompilerParams(vmem_limit_bytes=24 * 1024 * 1024),
         cost_estimate=pl.CostEstimate(
@@ -127,16 +149,20 @@
     )
 
 
-def home_products(items, count, lefts, held):
-    call = items_call(home_kernel, "home", [SMEM] * 2 + [VMEM] * 2, SUMS, [])
-    return call(items, count, lefts, held)
-
-
-def away_products(items, count, scale, lefts, rights, begun, mine):
-    specs = [SMEM] * 3 + [VMEM] * 4
-    sums = pltpu.VMEM((SUMS, BS, BS), jnp.float32)
-    call = items_call(away_kernel, "away", specs, BR * KC, [sums])
-    return call(items, count, scale, lefts, rights, begun, mine)
+def home_products(items, lefts, held):
+    call = items_call(home_kernel, "home", [SMEM] + [VMEM] * 2, VMEM, SUMS, [])
+    return call(items, lefts, held)
+
+
+def away_products(items, scale, lefts, rights, begun, mine):
+    scratch = [
+        pltpu.VMEM((SUMS, BS, BS), jnp.float32),
+        pltpu.SemaphoreType.DMA((BR * KC,)),
+    ]
+    specs = [SMEM] * 2 + [VMEM] * 4
+    out_spec = pl.BlockSpec(memory_space=pltpu.HBM)
+    call = items_call(away_kernel, "away", specs, out_spec, BR * KC, scratch)
+    return call(items, scale, lefts, rights, begun, mine)
 
 
 def compact(wanted, places, codes, slots):
@@ -217,7 +243,9 @@
     wanted = wanted.reshape(2, ITEMS)
     items = compact(wanted, places_of(wanted), code.reshape(1, ITEMS), ITEMS)
     totals = jnp.sum(wanted.astype(jnp.int32), axis=-1)
-    return sends.reshape(-1), send_counts, items, totals, over, targets
+    sends = jnp.concatenate([sends.reshape(-1), send_counts])
+    items = jnp.concatenate([items, totals[:, None]], axis=1)
+    return sends, items, over, targets
 
 
 def shards(pattern, matrix, atom_set, atom_slab, atom_offset):
@@ -228,7 +256,7 @@
     held = lax.all_gather(matrix, "z", axis=0, tiled=True)
     held = held.reshape(NZ * BR * KC, BS, BS)
 
-    sends, send_counts, items, totals, over, plane_targets = plan(pattern, z, x, y, core)
+    sends, items, over, plane_targets = plan(pattern, z, x, y, core)
     targets = lax.dynamic_slice_in_dim(plane_targets, x * BR, BR, 0)
 
     own_ids = row * BR + jnp.arange(BR, dtype=jnp.int32)
@@ -274,13 +302,13 @@
 
     mine = matrix.reshape(BR * KC, BS, BS)
     sends, lefts, density = lax.optimization_barrier((sends, lefts, density))
-    outgoing = select(sends, send_counts, held, 0)
+    outgoing = select(sends, held, 0)
     first = exchange(outgoing, "x")
-    begun = home_products(items[0], totals[:1], lefts, held)
+    begun = home_products(items[0], lefts, held)
 
     def finish(rights):
         rights = rights.reshape(-1, BS, BS)
-        return away_products(items[1], totals[1:], scale, lefts, rights, begun, mine)
+        return away_products(items[1], scale, lefts, rights, begun, mine)
 
     def one_round(first):
         return finish(first)
@@ -288,7 +316,7 @@
     def two_rounds(first):
         rounds = [first]
         for base in range(CAP, FULL, CAP):
-            rounds.append(exchange(select(sends, send_counts, held, base), "x"))
+            rounds.append(exchange(select(sends, held, base), "x"))
         return finish(jnp.concatenate(rounds, axis=1))
 
     purified = lax.cond(over > 0, two_rounds, one_round, first)

time: 127 us -> 127 us (level)
  no operation moved by 1% of the time
where the time goes in v6:
time: 127 us; the launch traced here: 124 us
  blocking collectives  34.4 us (27%)
  starting transfers between devices  22.1 us (17%)
  waiting for transfers between devices  17.2 us (14%)
  between operations  16.4 us (13%)
  local copies, waits for them, and re-layouts  11.2 us (9%)
  other arithmetic  10.1 us (8%)
  Pallas kernels  8.48 us (7%)
  matrix products  4.64 us (4%)
    all_gather x1, blocking collectives, shards(): packed = lax.all_gather(everyone(packed, 'x'), 'z', axis=0, tiled=False)  34.4 us
    all_to_all x4, starting transfers between devices, exchange(): return lax.all_to_all(value, axis, split_axis=0, concat_axis=0, tiled=True)  22 us
    all_gather x1, waiting for transfers between devices, shards(): held = lax.all_gather(matrix, 'z', axis=0, tiled=True)  8.44 us
    all_to_all x4, waiting for transfers between devices, exchange(): return lax.all_to_all(value, axis, split_axis=0, concat_axis=0, tiled=True)  8.07 us
    dot_general x1, matrix products, collocate(): dense = jnp.dot(plane.T, along_z, precision=lax.Precision.HIGHEST)  3.13 us
    pallas_call x1, Pallas kernels, away_products(): return call(items, scale, lefts, rights, begun, mine)  2.86 us
    pallas_call x1, Pallas kernels, select(): pl.pallas_call(functools.partial(select_kernel, base), out_shape=jax.Shap...  2.83 us
    pallas_call x1, Pallas kernels, home_products(): return call(items, lefts, held)  2.79 us
  transfers between devices with their start and end apart: 5, of which 4 were waited for; matrix products, arithmetic and copies ran while one was open for 20% of the time, Pallas kernels for 2%

profile of v6, /device:TPU:6, one launch (start us, length us, event | category | flops | bytes accessed | tf_op | source)
XLA Modules:
  0.0 124.5 jit_solution(3955202842268778020)
XLA Ops:
  7.2 0.7 all-gather.3.cloned.1.call-update
  7.9 0.8 broadcast_compare_fusion
  8.9 0.9 convolution_convert_fusion
  9.9 0.2 copy.120
  10.1 0.8 broadcast_compare_fusion.2
  10.9 0.2 fusion.83
  11.5 0.2 fusion.31
  12.1 0.2 convert_reduce_fusion.3
  12.2 0.6 convert_reduce_fusion.4
  13.6 0.8 dynamic-slice_compare_fusion
  14.5 1.1 select_reduce_fusion
  15.6 0.2 fusion.44
  16.0 0.6 broadcast_in_dim.67
  16.6 4.4 %all-to-all-start.2 = ((f32[8,1,65]{2,1,0:T(1,128)}), f32[8,1,65]{2,1,0:T(1,128)S(1)}, u32[]{:S(2)}, u32[]{:S(2)}) async-start(f32[8,1,65]{2,1,0:T(1,128)} %broadcast_in_dim.67), calls=%async_computation.2 | async-start | bytes 8192 | tf_op jit(solution)/shard_map/all_to_all | solution.py:29
  21.1 0.1 copy.111
  21.3 0.2 fusion.65
  21.7 0.2 select_reduce_fusion.1
  22.1 0.2 copy.121
  22.6 0.4 convert_reduce_fusion
  23.5 0.2 convert_reduce_fusion.2
  23.8 0.7 broadcast_subtract_fusion
  24.4 0.7 fusion.74
  25.1 0.7 slice.67
  25.8 0.4 all-to-all-done.2
  26.3 0.6 slice.68
  26.9 0.7 pad.15.clone
  27.6 0.2 fusion.46
  27.9 0.7 reshape.602
  28.5 7.9 %all-to-all-start.3 = ((f32[4,1,320]{2,1,0:T(1,128)}), f32[4,1,320]{2,1,0:T(1,128)S(1)}, u32[]{:S(2)}, u32[]{:S(2)}) async-start(f32[4,1,320]{2,1,0:T(1,128)} %reshape.602), calls=%async_computation.3 | async-start | bytes 12288 | tf_op jit(solution)/shard_map/all_to_all | solution.py:29
  36.6 3.0 %all-to-all-done.3 = f32[4,1,320]{2,1,0:T(1,128)S(1)} async-done(((f32[4,1,320]{2,1,0:T(1,128)}), f32[4,1,320]{2,1,0:T(1,128)S(1)}, u32[]{:S(2)}, u32[]{:S(2)}) %all-to-all-start.3) | async-done | bytes 5152 | tf_op jit(solution)/shard_map/all_to_all | solution.py:29
  39.7 1.8 %broadcast_in_dim.80 = bf16[8,4,2,128,128]{4,3,2,1,0:T(8,128)(2,1)} broadcast(bf16[4,2,128,128]{3,2,1,0:T(8,128)(2,1)S(1)} %copy-done), dimensions={1,2,3,4} | broadcast | bytes 2359296 | tf_op jit(solution)/shard_map/broadcast_in_dim | solution.py:34
  41.5 4.4 %all-to-all-start.4 = ((bf16[8,4,2,128,128]{4,3,2,1,0:T(8,128)(2,1)}), bf16[8,4,2,128,128]{4,3,2,1,0:T(8,128)(2,1)S(1)}, u32[]{:S(2)}, u32[]{:S(2)}) async-start(bf16[8,4,2,128,128]{4,3,2,1,0:T(8,128)(2,1)} %broadcast_in_dim.80), calls=%async_computation.4 | async-start | bytes 4194304 | tf_op jit(solution)/shard_map/all_to_all | solution.py:29
  45.9 0.2 fusion.2
  46.1 0.5 broadcast.710
  46.6 0.7 reduce.23
  47.4 34.4 %all-gather = f32[64,5,64]{2,1,0:T(8,128)S(1)} all-gather(f32[4,5,64]{2,1,0:T(8,128)S(1)} %reshape.603), channel_id=2, replica_groups=mesh['z'=16,'x'=4,'y'=4,'core'=2] {'z'}, dimensions={0}, use_global_device_ids=true | all-gather | bytes 87040 | tf_op jit(solution)/shard_map/all_gather | solution.py:286
  82.3 0.2 fusion.39
  82.5 3.1 %fusion.10 = f32[4,80,640]{2,1,0:T(8,128)} fusion(f32[320]{0:T(512)S(1)} %sub.150, f32[640]{0:T(1024)S(1)} %iota_convert_fusion, f32[320,80]{0,1:T(8,128)S(1)} %fusion.39, f32[320,4]{0,1:T(4,128)S(1)} %fusion.58), kind=kOutput, calls=%fused_computation.14 | convolution fusion | flops 789401600 | bytes 930560 | tf_op jit(solution)/shard_map/dot_general | solution.py:50
  85.6 8.4 %all-gather.3.cloned.1.call-done = bf16[64,2,128,128]{3,2,1,0:T(8,128)(2,1)} async-done(((bf16[4,2,128,128]{3,2,1,0:T(8,128)(2,1)}), bf16[64,2,128,128]{3,2,1,0:T(8,128)(2,1)}) %all-gather.3.cloned.1.call-update) | async-done | bytes 4194320 | tf_op jit(solution)/shard_map/all_gather | solution.py:256
  94.0 2.8 %select.119 = bf16[4,12,128,128]{3,2,1,0:T(8,128)(2,1)} custom-call(s32[132]{0:T(256)S(1)} %pad_add_fusion.1.codes, bf16[128,128,128]{2,1,0:T(8,128)(2,1)} %bitcast.76), custom_call_target="tpu_custom_call" | custom-call | tf_op jit(solution)/shard_map/select/pallas_call | solution.py:82
  96.9 5.3 %all-to-all-start.5 = ((bf16[4,12,128,128]{3,2,1,0:T(8,128)(2,1)}), bf16[4,12,128,128]{3,2,1,0:T(8,128)(2,1)}, u32[]{:S(2)}, u32[]{:S(2)}) async-start(bf16[4,12,128,128]{3,2,1,0:T(8,128)(2,1)} %select.119), calls=%async_computation.5 | async-start | bytes 3145728 | tf_op jit(solution)/shard_map/all_to_all | solution.py:29
  103.8 0.7 slice_reduce_fusion
  105.2 0.7 slice_reduce_fusion.1
  106.5 2.8 %home.1 = f32[9,128,128]{2,1,0:T(8,128)S(1)} custom-call(s32[129]{0:T(256)S(1)} %bitcast.73, bf16[64,128,128]{2,1,0:T(8,128)(2,1)S(1)} %bitcast.79, bf16[128,128,128]{2,1,0:T(8,128)(2,1)} %bitcast.77), custom_call_target="tpu_custom_call" | custom-call | flops 67108864 | bytes 6291456 | tf_op jit(solution)/shard_map/home/pallas_call | solution.py:154
  109.3 4.6 %all-to-all-done.5 = bf16[4,12,128,128]{3,2,1,0:T(8,128)(2,1)} async-done(((bf16[4,12,128,128]{3,2,1,0:T(8,128)(2,1)}), bf16[4,12,128,128]{3,2,1,0:T(8,128)(2,1)}, u32[]{:S(2)}, u32[]{:S(2)}) %all-to-all-start.5) | async-done | bytes 1572896 | tf_op jit(solution)/shard_map/all_to_all | solution.py:29
  113.9 2.9 %conditional.1 = (f32[4,2,128,128]{3,2,1,0:T(8,128)S(1)}) conditional(s32[]{:T(128)} %convert_element_type.98, (s32[2,129]{1,0:T(2,128)S(1)}, bf16[4,12,128,128]{3,2,1,0:T(8,128)(2,1)}, f32[1]{0:T(128)}, bf16[64,128,128]{2,1,0:T(8,128)(2,1)S(1)}, f32[9,128,128]{2,1,0:T(8,128)S(1)}, /*index=5*/bf16[8,128,128]{2,1,0:T(8,128)(2,1)S(1)}) %tuple.46, ...), branch_computations={%region_16.17_spmd, %region_17.18_spmd} | conditional | flops 71827456 | bytes 25166928 | solution.py:322
  113.9 2.9 %away.2 = f32[8,128,128]{2,1,0:T(8,128)S(1)} custom-call(s32[129]{0:T(256)S(1)} %bitcast.75, f32[1]{0:T(128)} %get-tuple-element.33.scale, bf16[64,128,128]{2,1,0:T(8,128)(2,1)S(1)} %get-tuple-element.34.lefts, bf16[48,128,128]{2,1,0:T(8,128)(2,1)} %bitcast.1.rights, f32[9,128,128]{2,1,0:T(8,128)S(1)} %get-tuple-element.36.begun, ...), custom_call_target="tpu_custom_call" | custom-call | flops 67108864 | bytes 6291456 | tf_op jit(solution)/shard_map/cond/branch_0_fun/away/pallas_call | solution.py:165
  116.8 0.8 copy-done.1
  (89 shorter events, 5.2 us)
Async XLA Ops:
  7.2 32.5 %copy-start = (bf16[4,2,128,128]{3,2,1,0:T(8,128)(2,1)S(1)}, bf16[4,2,128,128]{3,2,1,0:T(8,128)(2,1)}, u32[]{:S(2)}) copy-start(bf16[4,2,128,128]{3,2,1,0:T(8,128)(2,1)} %param.8) | copy-start | bytes 786436
  7.2 86.9 %all-gather.3.cloned.1.call-start = ((), (), s32[]{:S(2)}) async-start(), calls=%async_computation.6 | async-start | bytes 4456448 | tf_op jit(solution)/shard_map/all_gather | solution.py:256
  16.6 9.6 %all-to-all-start.2 = ((f32[8,1,65]{2,1,0:T(1,128)}), f32[8,1,65]{2,1,0:T(1,128)S(1)}, u32[]{:S(2)}, u32[]{:S(2)}) async-start(f32[8,1,65]{2,1,0:T(1,128)} %broadcast_in_dim.67), calls=%async_computation.2 | async-start | bytes 8192 | tf_op jit(solution)/shard_map/all_to_all | solution.py:29
  28.5 11.1 %all-to-all-start.3 = ((f32[4,1,320]{2,1,0:T(1,128)}), f32[4,1,320]{2,1,0:T(1,128)S(1)}, u32[]{:S(2)}, u32[]{:S(2)}) async-start(f32[4,1,320]{2,1,0:T(1,128)} %reshape.602), calls=%async_computation.3 | async-start | bytes 12288 | tf_op jit(solution)/shard_map/all_to_all | solution.py:29
  41.5 44.1 %all-to-all-start.4 = ((bf16[8,4,2,128,128]{4,3,2,1,0:T(8,128)(2,1)}), bf16[8,4,2,128,128]{4,3,2,1,0:T(8,128)(2,1)S(1)}, u32[]{:S(2)}, u32[]{:S(2)}) async-start(bf16[8,4,2,128,128]{4,3,2,1,0:T(8,128)(2,1)} %broadcast_in_dim.80), calls=%async_computation.4 | async-start | bytes 4194304 | tf_op jit(solution)/shard_map/all_to_all | solution.py:29
  96.9 17.1 %all-to-all-start.5 = ((bf16[4,12,128,128]{3,2,1,0:T(8,128)(2,1)}), bf16[4,12,128,128]{3,2,1,0:T(8,128)(2,1)}, u32[]{:S(2)}, u32[]{:S(2)}) async-start(bf16[4,12,128,128]{3,2,1,0:T(8,128)(2,1)} %select.119), calls=%async_computation.5 | async-start | bytes 3145728 | tf_op jit(solution)/shard_map/all_to_all | solution.py:29
  116.8 0.8 copy-start.1
Sparse Core Ops, SparseCore 0:
  10.1 83.8 all-gather.2

commit v7 on v6

--- a/solution.py
+++ b/solution.py
@@ -1,5 +1,3 @@
-import functools
-
 import jax
 import jax.numpy as jnp
 from jax import lax
@@ -13,7 +11,7 @@
 GZ = 640
 NZ, NX, NY, NCORE = 16, 4, 4, 2
 BR, KC, SLOTS, BS, NB = 4, 2, 16, 128, 256
-CAP = 12
+CAPS = (8, 9, 10, 11, 12, 16, 24, 32)
 FULL = NZ * KC
 ITEMS = BR * SLOTS * KC
 GROUP = 4
@@ -56,10 +54,10 @@
 VMEM = pl.BlockSpec(memory_space=pltpu.VMEM)
 
 
-def select_kernel(base, codes, held, out, stage, in_sems, out_sems):
+def select_kernel(codes, held, out, stage, in_sems, out_sems):
     def fetch(d, j):
         return pltpu.make_async_copy(
-            held.at[codes[d * FULL + base + j]], stage.at[d, j], in_sems.at[d, j]
+            held.at[codes[d * FULL + j]], stage.at[d, j], in_sems.at[d, j]
         )
 
     def store(d, j):
@@ -69,7 +67,7 @@
         fetch(d, j).wait()
         store(d, j).start()
 
-    fills = [jnp.clip(codes[NX * FULL + d] - base, 0, CAP) for d in range(NX)]
+    fills = [jnp.minimum(codes[NX * FULL + d], out.shape[1]) for d in range(NX)]
     for d in range(NX):
         lax.fori_loop(0, fills[d], lambda j, _, d=d: fetch(d, j).start(), None)
     for d in range(NX):
@@ -78,16 +76,16 @@
         lax.fori_loop(0, fills[d], lambda j, _, d=d: store(d, j).wait(), None)
 
 
-def select(codes, held, base):
+def select(codes, held, cap):
     return pl.pallas_call(
-        functools.partial(select_kernel, base),
-        out_shape=jax.ShapeDtypeStruct((NX, CAP, BS, BS), jnp.bfloat16),
+        select_kernel,
+        out_shape=jax.ShapeDtypeStruct((NX, cap, BS, BS), jnp.bfloat16),
         in_specs=[SMEM, ANYWHERE],
         out_specs=ANYWHERE,
         scratch_shapes=[
-            pltpu.VMEM((NX, CAP, BS, BS), jnp.bfloat16),
-            pltpu.SemaphoreType.DMA((NX, CAP)),
-            pltpu.SemaphoreType.DMA((NX, CAP)),
+            pltpu.VMEM((NX, cap, BS, BS), jnp.bfloat16),
+            pltpu.SemaphoreType.DMA((NX, cap)),
+            pltpu.SemaphoreType.DMA((NX, cap)),
         ],
         name="select",
     )(codes, held)
@@ -210,7 +208,7 @@
     place = places_of(table)
     counts = jnp.sum(table.astype(jnp.int32), axis=-1)
     apart = jnp.arange(NX)[:, None] != jnp.arange(NX)[None, :]
-    over = jnp.sum((apart & (counts > CAP)).astype(jnp.int32))
+    most = jnp.max(jnp.where(apart, counts, 0))
 
     zs = jnp.arange(NZ, dtype=jnp.int32)[None, :, None]
     us = jnp.arange(KC, dtype=jnp.int32)[None, None, :]
@@ -245,7 +243,7 @@
     totals = jnp.sum(wanted.astype(jnp.int32), axis=-1)
     sends = jnp.concatenate([sends.reshape(-1), send_counts])
     items = jnp.concatenate([items, totals[:, None]], axis=1)
-    return sends, items, over, targets
+    return sends, items, most, targets
 
 
 def shards(pattern, matrix, atom_set, atom_slab, atom_offset):
@@ -256,7 +254,7 @@
     held = lax.all_gather(matrix, "z", axis=0, tiled=True)
     held = held.reshape(NZ * BR * KC, BS, BS)
 
-    sends, items, over, plane_targets = plan(pattern, z, x, y, core)
+    sends, items, most, plane_targets = plan(pattern, z, x, y, core)
     targets = lax.dynamic_slice_in_dim(plane_targets, x * BR, BR, 0)
 
     own_ids = row * BR + jnp.arange(BR, dtype=jnp.int32)
@@ -268,8 +266,10 @@
         jnp.arange(BS)[:, None] // ORB == jnp.arange(sets)[None, :]
     ).astype(jnp.float32)
     set_part = jnp.dot(own_diag, gather_sets, precision=lax.Precision.HIGHEST)
-    packed = jnp.concatenate([set_part.reshape(-1), over.astype(jnp.float32)[None]])
-    packed = jnp.sum(everyone(packed[None], COL), axis=0)[0]
+    packed = jnp.concatenate([set_part.reshape(-1), most.astype(jnp.float32)[None]])
+    packed = everyone(packed[None], COL)[:, 0]
+    most = jnp.max(packed[:, BR * sets])
+    packed = jnp.sum(packed, axis=0)
     blocks, packed = lax.optimization_barrier((matrix, packed))
     lefts = everyone(blocks, COL).reshape(SLOTS * BR, BS, BS)
     set_charge = packed[: BR * sets]
@@ -281,11 +281,11 @@
     ).astype(jnp.float32)
     charge = jnp.dot(find, set_charge, precision=lax.Precision.HIGHEST)
     start_x = atom_slab.astype(jnp.float32) * PLANES + atom_offset[0]
-    flag = jnp.broadcast_to(packed[BR * sets], charge.shape)
+    flag = jnp.broadcast_to(most, charge.shape)
     packed = jnp.stack([charge, start_x, atom_offset[1], atom_offset[2], flag])
     packed = lax.all_gather(everyone(packed, "x"), "z", axis=0, tiled=False)
     packed = packed.reshape(NZ * NX, 5, atoms_here)
-    over = jnp.sum(packed[:, 4, 0])
+    most = jnp.max(packed[:, 4, 0])
     trace = jnp.sum(packed[:, 0])
     weight = jax.nn.sigmoid(sharpness * (half_fill - trace / (NB * BS)))
     scale = (2.0 * weight).reshape(1)
@@ -302,24 +302,19 @@
 
     mine = matrix.reshape(BR * KC, BS, BS)
     sends, lefts, density = lax.optimization_barrier((sends, lefts, density))
-    outgoing = select(sends, held, 0)
-    first = exchange(outgoing, "x")
-    begun = home_products(items[0], lefts, held)
-
-    def finish(rights):
-        rights = rights.reshape(-1, BS, BS)
-        return away_products(items[1], scale, lefts, rights, begun, mine)
-
-    def one_round(first):
-        return finish(first)
-
-    def two_rounds(first):
-        rounds = [first]
-        for base in range(CAP, FULL, CAP):
-            rounds.append(exchange(select(sends, held, base), "x"))
-        return finish(jnp.concatenate(rounds, axis=1))
-
-    purified = lax.cond(over > 0, two_rounds, one_round, first)
+
+    def with_slots(cap):
+        def run(sends, items, scale, lefts, held, mine):
+            rights = exchange(select(sends, held, cap), "x").reshape(-1, BS, BS)
+            begun = home_products(items[0], lefts, held)
+            return away_products(items[1], scale, lefts, rights, begun, mine)
+
+        return run
+
+    size = sum((most > cap).astype(jnp.int32) for cap in CAPS[:-1])
+    purified = lax.switch(
+        size, [with_slots(cap) for cap in CAPS], sends, items, scale, lefts, held, mine
+    )
     return purified.reshape(matrix.shape), density
 
 

time: 127 us -> 125 us (0.984)
  waiting for transfers between devices: 17.2 us -> 13.1 us
  between operations: 16.4 us -> 19.6 us
  local copies, waits for them, and re-layouts: 11.2 us -> 9.09 us
    all_gather x1, waiting for transfers between devices: 8.44 us -> 3.22 us  [shards(): held = lax.all_gather(matrix, 'z', axis=0, tiled=True)]
    reduce_max x0 -> x3, other arithmetic: none -> 1.97 us  [the longest x1 0.67 us: shards(): most = jnp.max(packed[:, BR * sets])]
    reduce_sum x3 -> x1, other arithmetic: 1.32 us -> 0.02 us  [shards(): packed = jnp.sum(packed, axis=0)]
  transfers between devices with their start and end apart: 5 -> 5, of which waited for: 4 -> 4; matrix products, arithmetic and copies ran while one was open for 20% -> 19% of each run, Pallas kernels for 2% -> 3%
where the time goes in v7:
time: 125 us; the launch traced here: 122 us
  blocking collectives  34.5 us (28%)
  starting transfers between devices  21.8 us (17%)
  between operations  19.6 us (16%)
  waiting for transfers between devices  13.1 us (10%)
  other arithmetic  9.43 us (8%)
  Pallas kernels  9.18 us (7%)
  local copies, waits for them, and re-layouts  9.09 us (7%)
  matrix products  4.63 us (4%)
    all_gather x1, blocking collectives, shards(): packed = lax.all_gather(everyone(packed, 'x'), 'z', axis=0, tiled=False)  34.5 us
    all_to_all x4, starting transfers between devices, exchange(): return lax.all_to_all(value, axis, split_axis=0, concat_axis=0, tiled=True)  21.8 us
    all_to_all x4, waiting for transfers between devices, exchange(): return lax.all_to_all(value, axis, split_axis=0, concat_axis=0, tiled=True)  9.15 us
    pallas_call x1, Pallas kernels, home_products(): return call(items, lefts, held)  3.43 us
    all_gather x1, waiting for transfers between devices, shards(): held = lax.all_gather(matrix, 'z', axis=0, tiled=True)  3.22 us
    dot_general x1, matrix products, collocate(): dense = jnp.dot(plane.T, along_z, precision=lax.Precision.HIGHEST)  3.13 us
    pallas_call x1, Pallas kernels, away_products(): return call(items, scale, lefts, rights, begun, mine)  3.05 us
    pallas_call x1, Pallas kernels, select(): pl.pallas_call(select_kernel, out_shape=jax.ShapeDtypeStruct((NX, cap, BS...  2.7 us
  transfers between devices with their start and end apart: 5, of which 4 were waited for; matrix products, arithmetic and copies ran while one was open for 19% of the time, Pallas kernels for 3%

profile of v7, /device:TPU:6, one launch (start us, length us, event | category | flops | bytes accessed | tf_op | source)
XLA Modules:
  0.0 122.4 jit_solution(3873740795044068049)
XLA Ops:
  7.3 0.7 all-gather.3.cloned.1.call-update
  8.0 0.8 broadcast_compare_fusion
  9.1 0.9 convolution_convert_fusion
  10.0 0.2 copy.122
  10.2 0.8 broadcast_compare_fusion.2
  11.0 0.2 fusion.81
  11.5 0.2 fusion.31
  12.1 0.2 convert_reduce_fusion.3
  12.3 0.6 select_reduce_fusion.4
  13.6 0.8 dynamic-slice_compare_fusion
  14.5 1.1 select_reduce_fusion
  15.7 0.2 fusion.44
  16.1 0.6 broadcast_in_dim.72
  16.7 4.4 %all-to-all-start.8 = ((f32[8,1,65]{2,1,0:T(1,128)}), f32[8,1,65]{2,1,0:T(1,128)S(1)}, u32[]{:S(2)}, u32[]{:S(2)}) async-start(f32[8,1,65]{2,1,0:T(1,128)} %broadcast_in_dim.72), calls=%async_computation.8 | async-start | bytes 8192 | tf_op jit(solution)/shard_map/all_to_all | solution.py:27
  21.1 0.2 fusion.65
  21.5 0.1 copy.113
  21.8 0.4 convert_reduce_fusion
  22.5 0.1 and.312
  22.7 0.1 and.306
  22.8 0.2 select_reduce_fusion.1
  23.1 0.2 copy.123
  23.8 0.2 select_reduce_fusion.3
  24.3 0.2 convert_reduce_fusion.2
  24.6 0.2 fusion.2
  24.9 1.4 %all-to-all-done.8 = f32[8,1,65]{2,1,0:T(1,128)S(1)} async-done(((f32[8,1,65]{2,1,0:T(1,128)}), f32[8,1,65]{2,1,0:T(1,128)S(1)}, u32[]{:S(2)}, u32[]{:S(2)}) %all-to-all-start.8) | async-done | bytes 2112 | tf_op jit(solution)/shard_map/all_to_all | solution.py:27
  26.3 0.7 slice_reduce_fusion.9
  27.0 0.7 pad.12.clone
  27.7 0.2 fusion.46
  28.0 0.7 reshape.699
  28.7 7.9 %all-to-all-start.9 = ((f32[4,1,320]{2,1,0:T(1,128)}), f32[4,1,320]{2,1,0:T(1,128)S(1)}, u32[]{:S(2)}, u32[]{:S(2)}) async-start(f32[4,1,320]{2,1,0:T(1,128)} %reshape.699), calls=%async_computation.9 | async-start | bytes 12288 | tf_op jit(solution)/shard_map/all_to_all | solution.py:27
  37.0 0.1 add.397
  37.5 2.3 %all-to-all-done.9 = f32[4,1,320]{2,1,0:T(1,128)S(1)} async-done(((f32[4,1,320]{2,1,0:T(1,128)}), f32[4,1,320]{2,1,0:T(1,128)S(1)}, u32[]{:S(2)}, u32[]{:S(2)}) %all-to-all-start.9) | async-done | bytes 5152 | tf_op jit(solution)/shard_map/all_to_all | solution.py:27
  39.8 1.8 %broadcast_in_dim.85 = bf16[8,4,2,128,128]{4,3,2,1,0:T(8,128)(2,1)} broadcast(bf16[4,2,128,128]{3,2,1,0:T(8,128)(2,1)S(1)} %copy-done.3), dimensions={1,2,3,4} | broadcast | bytes 2359296 | tf_op jit(solution)/shard_map/broadcast_in_dim | solution.py:32
  41.6 4.4 %all-to-all-start.10 = ((bf16[8,4,2,128,128]{4,3,2,1,0:T(8,128)(2,1)}), bf16[8,4,2,128,128]{4,3,2,1,0:T(8,128)(2,1)}, u32[]{:S(2)}, u32[]{:S(2)}) async-start(bf16[8,4,2,128,128]{4,3,2,1,0:T(8,128)(2,1)} %broadcast_in_dim.85), calls=%async_computation.10 | async-start | bytes 4194304 | tf_op jit(solution)/shard_map/all_to_all | solution.py:27
  46.1 0.5 broadcast.705
  46.7 0.7 reduce.24
  47.4 34.5 %all-gather = f32[64,5,64]{2,1,0:T(8,128)S(1)} all-gather(f32[4,5,64]{2,1,0:T(8,128)S(1)} %reshape.700), channel_id=2, replica_groups=mesh['z'=16,'x'=4,'y'=4,'core'=2] {'z'}, dimensions={0}, use_global_device_ids=true | all-gather | bytes 87040 | tf_op jit(solution)/shard_map/all_gather | solution.py:286
  81.9 0.7 slice_reduce_fusion.8
  87.6 0.2 fusion.39
  87.8 3.1 %fusion.10 = f32[4,80,640]{2,1,0:T(8,128)} fusion(f32[320]{0:T(512)S(1)} %sub.172, f32[640]{0:T(1024)S(1)} %iota_convert_fusion, f32[320,80]{0,1:T(8,128)S(1)} %fusion.39, f32[320,4]{0,1:T(4,128)S(1)} %fusion.58), kind=kOutput, calls=%fused_computation.21 | convolution fusion | flops 789401600 | bytes 930560 | tf_op jit(solution)/shard_map/dot_general | solution.py:48
  90.9 3.2 %all-gather.3.cloned.1.call-done = bf16[64,2,128,128]{3,2,1,0:T(8,128)(2,1)} async-done(((bf16[4,2,128,128]{3,2,1,0:T(8,128)(2,1)}), bf16[64,2,128,128]{3,2,1,0:T(8,128)(2,1)}) %all-gather.3.cloned.1.call-update) | async-done | bytes 4194320 | tf_op jit(solution)/shard_map/all_gather | solution.py:254
  94.1 21.4 %conditional.1 = (f32[4,2,128,128]{3,2,1,0:T(8,128)}) conditional(s32[]{:T(128)} %clamp.11, (s32[2,129]{1,0:T(2,128)S(1)}, f32[64,5,64]{2,1,0:T(8,128)S(1)}, bf16[64,2,128,128]{3,2,1,0:T(8,128)(2,1)}, s32[132]{0:T(256)S(1)}, bf16[64,128,128]{2,1,0:T(8,128)(2,1)}, ...), branch_computations={%region_16.18_spmd, %region_18.20_spmd, %region_20.22_spmd, %regio... | conditional | flops 134221824 | bytes 33573040 | solution.py:315
  94.1 2.7 %select.124 = bf16[4,10,128,128]{3,2,1,0:T(8,128)(2,1)} custom-call(s32[132]{0:T(256)S(1)} %get-tuple-element.281.codes, bf16[128,128,128]{2,1,0:T(8,128)(2,1)} %bitcast.146), custom_call_target="tpu_custom_call" | custom-call | tf_op jit(solution)/shard_map/cond/branch_2_fun/select/pallas_call | solution.py:80
  96.8 5.1 %all-to-all-start.2 = ((bf16[4,10,128,128]{3,2,1,0:T(8,128)(2,1)}), bf16[4,10,128,128]{3,2,1,0:T(8,128)(2,1)S(1)}, u32[]{:S(2)}, u32[]{:S(2)}) async-start(bf16[4,10,128,128]{3,2,1,0:T(8,128)(2,1)} %select.124), calls=%async_computation.2 | async-start | bytes 2621440 | tf_op jit(solution)/shard_map/cond/branch_2_fun/all_to_all | solution.py:27
  102.0 0.7 slice_reduce_fusion.2
  103.4 3.4 %home.10.begun = f32[9,128,128]{2,1,0:T(8,128)S(1)} custom-call(s32[129]{0:T(256)S(1)} %bitcast.132, bf16[64,128,128]{2,1,0:T(8,128)(2,1)} %get-tuple-element.280.lefts, bf16[128,128,128]{2,1,0:T(8,128)(2,1)} %bitcast.147), custom_call_target="tpu_custom_call" | custom-call | flops 67108864 | bytes 6291456 | tf_op jit(solution)/shard_map/cond/branch_2_fun/home/pallas_call | solution.py:152
  106.8 5.4 %all-to-all-done.2 = bf16[4,10,128,128]{3,2,1,0:T(8,128)(2,1)S(1)} async-done(((bf16[4,10,128,128]{3,2,1,0:T(8,128)(2,1)}), bf16[4,10,128,128]{3,2,1,0:T(8,128)(2,1)S(1)}, u32[]{:S(2)}, u32[]{:S(2)}) %all-to-all-start.2) | async-done | bytes 1310752 | tf_op jit(solution)/shard_map/cond/branch_2_fun/all_to_all | solution.py:27
  112.2 3.1 %away.10 = f32[8,128,128]{2,1,0:T(8,128)} custom-call(s32[129]{0:T(256)S(1)} %bitcast.140, f32[1]{0:T(128)} %bitcast.15.scale, bf16[64,128,128]{2,1,0:T(8,128)(2,1)} %get-tuple-element.280.lefts, bf16[40,128,128]{2,1,0:T(8,128)(2,1)S(1)} %bitcast.123, f32[9,128,128]{2,1,0:T(8,128)S(1)} %home.10.begun, bf16[8,128,128]{2,1,0:T(8,128)(2,1)S(1)} %bitcast.168), custom_call_target="tpu_custom_call" | custom-call | flops 67108864 | bytes 6291456 | tf_op jit(solution)/shard_map/cond/branch_2_fun/away/pallas_call | solution.py:163
  (92 shorter events, 4.6 us)
Async XLA Ops:
  7.2 32.6 %copy-start.3 = (bf16[4,2,128,128]{3,2,1,0:T(8,128)(2,1)S(1)}, bf16[4,2,128,128]{3,2,1,0:T(8,128)(2,1)}, u32[]{:S(2)}) copy-start(bf16[4,2,128,128]{3,2,1,0:T(8,128)(2,1)} %param.14) | copy-start | bytes 786436
  7.2 17.4 %copy-start.6 = (s32[64]{0:T(128)S(1)}, s32[64]{0:T(128)}, u32[]{:S(2)}) copy-start(s32[64]{0:T(128)} %param.15) | copy-start | bytes 772
  7.2 17.4 %copy-start.5 = (f32[3,64]{1,0:T(4,128)S(1)}, f32[3,64]{1,0:T(4,128)}, u32[]{:S(2)}) copy-start(f32[3,64]{1,0:T(4,128)} %param.17) | copy-start | bytes 2308
  7.2 17.4 %copy-start.7 = (s32[64]{0:T(128)S(1)}, s32[64]{0:T(128)}, u32[]{:S(2)}) copy-start(s32[64]{0:T(128)} %param.16) | copy-start | bytes 772
  7.2 86.9 %all-gather.3.cloned.1.call-start = ((), (), s32[]{:S(2)}) async-start(), calls=%async_computation.11 | async-start | bytes 4456448 | tf_op jit(solution)/shard_map/all_gather | solution.py:254
  16.7 9.6 %all-to-all-start.8 = ((f32[8,1,65]{2,1,0:T(1,128)}), f32[8,1,65]{2,1,0:T(1,128)S(1)}, u32[]{:S(2)}, u32[]{:S(2)}) async-start(f32[8,1,65]{2,1,0:T(1,128)} %broadcast_in_dim.72), calls=%async_computation.8 | async-start | bytes 8192 | tf_op jit(solution)/shard_map/all_to_all | solution.py:27
  28.7 11.1 %all-to-all-start.9 = ((f32[4,1,320]{2,1,0:T(1,128)}), f32[4,1,320]{2,1,0:T(1,128)S(1)}, u32[]{:S(2)}, u32[]{:S(2)}) async-start(f32[4,1,320]{2,1,0:T(1,128)} %reshape.699), calls=%async_computation.9 | async-start | bytes 12288 | tf_op jit(solution)/shard_map/all_to_all | solution.py:27
  41.6 49.3 %all-to-all-start.10 = ((bf16[8,4,2,128,128]{4,3,2,1,0:T(8,128)(2,1)}), bf16[8,4,2,128,128]{4,3,2,1,0:T(8,128)(2,1)}, u32[]{:S(2)}, u32[]{:S(2)}) async-start(bf16[8,4,2,128,128]{4,3,2,1,0:T(8,128)(2,1)} %broadcast_in_dim.85), calls=%async_computation.10 | async-start | bytes 4194304 | tf_op jit(solution)/shard_map/all_to_all | solution.py:27
  96.8 15.4 %all-to-all-start.2 = ((bf16[4,10,128,128]{3,2,1,0:T(8,128)(2,1)}), bf16[4,10,128,128]{3,2,1,0:T(8,128)(2,1)S(1)}, u32[]{:S(2)}, u32[]{:S(2)}) async-start(bf16[4,10,128,128]{3,2,1,0:T(8,128)(2,1)} %select.124), calls=%async_computation.2 | async-start | bytes 2621440 | tf_op jit(solution)/shard_map/cond/branch_2_fun/all_to_all | solution.py:27
Sparse Core Ops, SparseCore 0:
  10.1 83.9 all-gather.2
